TPU v7x, 128 devices: a whole 4x4x4 slice. The times are simulated.
128 devices in a mesh: head: 8 (over x, y_lo), blk: 16 (over y_hi, z, core).
Axes of the slice: x: 4, y: 4 (y_hi: 2, y_lo: 2; y = y_hi * 2 + y_lo), z: 4, core: 2. Of those that a mesh axis runs over, the one named last changes fastest.
Arguments:
- tokens: bfloat16 [8, 2048, 2048], P('head', 'blk'), may hold values from -6 to 6
- block_lengths: int32 [8, 12], replicated, may hold values from 1 to 256, 2048 in all within a row
- attn_gain: float32 [2048], replicated, may hold values from 0.1 to 1.9
- query_weight: bfloat16 [2048, 2048], P('blk', 'head'), may hold values from -0.125 to 0.125
- key_weight: bfloat16 [2048, 2048], P('blk', 'head'), may hold values from -0.125 to 0.125
- value_weight: bfloat16 [2048, 2048], P('blk', 'head'), may hold values from -0.125 to 0.125
- out_weight: bfloat16 [2048, 2048], P('head', 'blk'), may hold values from -2 to 2
- mlp_gain: float32 [2048], replicated, may hold values from 0.1 to 1.9
- gate_weight: bfloat16 [2048, 5504], P('blk', 'head'), may hold values from -0.125 to 0.125
- up_weight: bfloat16 [2048, 5504], P('blk', 'head'), may hold values from -0.125 to 0.125
- down_weight: bfloat16 [5504, 2048], P('head', 'blk'), may hold values from -0.078125 to 0.078125
- output_grad: bfloat16 [8, 2048, 2048], P('head', 'blk'), may hold values from -6 to 6
Outputs:
- layer_output: bfloat16 [8, 2048, 2048], P('head', 'blk')
- input_grad: float32 [8, 2048, 2048], P('head', 'blk')
- attn_gain_grad: float32 [2048], replicated
- query_weight_grad: float32 [2048, 2048], P('blk', 'head')
- key_weight_grad: float32 [2048, 2048], P('blk', 'head')
- value_weight_grad: float32 [2048, 2048], P('blk', 'head')
- out_weight_grad: float32 [2048, 2048], P('head', 'blk')
- mlp_gain_grad: float32 [2048], replicated
- gate_weight_grad: float32 [2048, 5504], P('blk', 'head')
- up_weight_grad: float32 [2048, 5504], P('blk', 'head')
- down_weight_grad: float32 [5504, 2048], P('head', 'blk')
Inputs may be any that keep to these rules, and one draw needn't show every extreme that they name: `block_lengths`: row s holds the token counts of the 12 consecutive attention blocks of sequence s, in order; each row sums to 2048 and its largest count is 256.
All inputs are finite; a program needn't handle non-finite values.
Results may differ from a plain program's by a relative error of at most 0.028.
Values may be sent and summed in bfloat16 or wider, within the bound.
No kernel may reach another device: no remote copies, remote signals or barrier semaphores. Data moves between devices by JAX's collectives and lax.ppermute only.
A program may use at most 128 MiB of HBM per device.

v0:
```python
import jax
import jax.numpy as jnp
from jax import lax
from jax.sharding import PartitionSpec as P

HEAD_DIM = 128


norm_eps = 1e-05
masked_score = -1e30


def passed_along(value, axis, steps):
    count = lax.axis_size(axis)
    pairs = [(source, (source + steps) % count) for source in range(count)]
    return lax.ppermute(value, axis, pairs)


def inverse_rms(values):
    return lax.rsqrt(jnp.mean(values * values, axis=-1, keepdims=True) + norm_eps)


def rotary_tables(row_count, first_row, columns, head_width):
    places = (first_row + jnp.arange(row_count, dtype=jnp.int32)).astype(jnp.float32)
    half_width = head_width // 2
    within = jnp.arange(columns, dtype=jnp.int32) % head_width % half_width
    inverse_freq = 10000.0 ** (within.astype(jnp.float32) * (-2.0 / head_width))
    angles = places[:, None] * inverse_freq[None, :]
    return (jnp.cos(angles), jnp.sin(angles))


def turn_half(values, head_width):
    full_shape = values.shape
    halves = values.reshape(full_shape[:-1] + (full_shape[-1] // head_width, 2, head_width // 2))
    turned = jnp.stack((-halves[..., 1, :], halves[..., 0, :]), axis=-2)
    return turned.reshape(full_shape)


def rotate_forward(values, cosine_table, sine_table, head_width):
    return values * cosine_table + turn_half(values, head_width) * sine_table


def rotate_back(gradient, cosine_table, sine_table, head_width):
    return gradient * cosine_table - turn_half(gradient, head_width) * sine_table


def block_index_of(block_ends, first_row, row_count):
    places = first_row + jnp.arange(row_count, dtype=jnp.int32)
    return jnp.sum((block_ends[:, None, :] <= places[None, :, None]).astype(jnp.int32), axis=2)


def head_rows(values):
    return lax.all_gather(values, "head", axis=0, tiled=True)


def head_total(term_fn, row_total):
    return lax.psum_scatter(
        term_fn(jnp.int32(0), row_total * lax.axis_size("head")).astype(jnp.bfloat16),
        "head",
        scatter_dimension=0,
        tiled=True,
    ).astype(jnp.float32)


def score_block(query_heads, key_heads, query_blocks, key_blocks, score_scale):
    scores = (
        jnp.einsum("sqhd,skhd->sqhk", query_heads, key_heads, preferred_element_type=jnp.float32)
        * score_scale
    )
    visible = key_blocks[:, None, None, :] <= query_blocks[:, :, None, None]
    return jnp.where(visible, scores, masked_score)


def forward_block(
    softmax_state, query_heads, key_heads, value_heads, query_blocks, key_blocks, score_scale
):
    run_top, run_total, run_acc = softmax_state
    scores = score_block(query_heads, key_heads, query_blocks, key_blocks, score_scale)
    new_top = jnp.maximum(run_top, jnp.max(scores, axis=-1))
    weights = jnp.exp(scores - new_top[..., None])
    factor = jnp.exp(run_top - new_top)
    run_total = run_total * factor + jnp.sum(weights, axis=-1)
    run_acc = run_acc * factor[..., None] + jnp.einsum(
        "sqhk,skhd->sqhd",
        weights.astype(jnp.bfloat16),
        value_heads,
        preferred_element_type=jnp.float32,
    )
    return (new_top, run_total, run_acc)


def backward_block(
    query_heads,
    grad_heads,
    log_total,
    row_delta,
    key_heads,
    value_heads,
    query_blocks,
    key_blocks,
    score_scale,
):
    scores = score_block(query_heads, key_heads, query_blocks, key_blocks, score_scale)
    softmax_probs = jnp.exp(scores - log_total[..., None])
    grad_values = jnp.einsum(
        "sqhk,sqhd->skhd",
        softmax_probs.astype(jnp.bfloat16),
        grad_heads,
        preferred_element_type=jnp.float32,
    )
    grad_probs = jnp.einsum(
        "sqhd,skhd->sqhk", grad_heads, value_heads, preferred_element_type=jnp.float32
    )
    grad_scores = (softmax_probs * (grad_probs - row_delta[..., None])).astype(jnp.bfloat16)
    grad_query = jnp.einsum(
        "sqhk,skhd->sqhd", grad_scores, key_heads, preferred_element_type=jnp.float32
    )
    grad_keys = jnp.einsum(
        "sqhk,sqhd->skhd", grad_scores, query_heads, preferred_element_type=jnp.float32
    )
    return (grad_query, grad_keys, grad_values)


def norm_back(grad_normed, values, inverse, gain):
    scaled = grad_normed * gain
    gain_part = jnp.sum(grad_normed * values * inverse, axis=(0, 1))
    inner = jnp.mean(scaled * values, axis=-1, keepdims=True)
    return (inverse * scaled - values * inverse**3 * inner, gain_part)


def on_device(
    tokens,
    block_lengths,
    attn_gain,
    query_weight,
    key_weight,
    value_weight,
    out_weight,
    mlp_gain,
    gate_weight,
    up_weight,
    down_weight,
    output_grad,
):
    cycle_size = lax.axis_size("blk")
    cycle_place = lax.axis_index("blk")
    local_seqs = tokens.shape[0]
    length = tokens.shape[1]
    all_seqs = block_lengths.shape[0]
    head_cols = query_weight.shape[1]
    local_heads = head_cols // HEAD_DIM
    score_scale = HEAD_DIM ** (-0.5)
    split_shape = (all_seqs, length, local_heads, HEAD_DIM)
    row_shape = (all_seqs, length, local_heads)
    block_ends = jnp.cumsum(block_lengths, axis=1)
    own_blocks = block_index_of(block_ends, cycle_place * length, length)
    cosine_table, sine_table = rotary_tables(length, cycle_place * length, head_cols, HEAD_DIM)

    def source_blocks(cycle_step):
        return block_index_of(block_ends, (cycle_place - cycle_step) % cycle_size * length, length)

    query_weight_complete, key_weight_complete, value_weight_complete, output_weight_complete = (
        lax.all_gather(query_weight, "blk", axis=0, tiled=True),
        lax.all_gather(key_weight, "blk", axis=0, tiled=True),
        lax.all_gather(value_weight, "blk", axis=0, tiled=True),
        lax.all_gather(out_weight, "blk", axis=1, tiled=True),
    )
    gate_weight_complete, up_weight_complete, down_weight_complete = (
        lax.all_gather(gate_weight, "blk", axis=0, tiled=True),
        lax.all_gather(up_weight, "blk", axis=0, tiled=True),
        lax.all_gather(down_weight, "blk", axis=1, tiled=True),
    )
    token_float = tokens.astype(jnp.float32)
    first_inverse = inverse_rms(token_float)
    first_normed_rows = head_rows((token_float * first_inverse * attn_gain).astype(jnp.bfloat16))
    query_pre = jnp.einsum(
        "mig,go->mio", first_normed_rows, query_weight_complete, preferred_element_type=jnp.float32
    )
    key_unrotated = jnp.einsum(
        "mig,go->mio", first_normed_rows, key_weight_complete, preferred_element_type=jnp.float32
    )
    value_pre = jnp.einsum(
        "mig,go->mio", first_normed_rows, value_weight_complete, preferred_element_type=jnp.float32
    )
    query_heads = (
        rotate_forward(query_pre, cosine_table, sine_table, HEAD_DIM)
        .astype(jnp.bfloat16)
        .reshape(split_shape)
    )
    key_heads = (
        rotate_forward(key_unrotated, cosine_table, sine_table, HEAD_DIM)
        .astype(jnp.bfloat16)
        .reshape(split_shape)
    )
    value_heads = value_pre.astype(jnp.bfloat16).reshape(split_shape)
    initial = (
        jnp.full(row_shape, masked_score, jnp.float32),
        jnp.zeros(row_shape, jnp.float32),
        jnp.zeros(split_shape, jnp.float32),
    )

    def forward_turn(cycle_step, cycle_state):
        keys_now, values_now, softmax_state = cycle_state
        softmax_state = forward_block(
            softmax_state,
            query_heads,
            keys_now,
            values_now,
            own_blocks,
            source_blocks(cycle_step),
            score_scale,
        )
        keys_now, values_now = passed_along((keys_now, values_now), "blk", 1)
        return (keys_now, values_now, softmax_state)

    keys_now, values_now, softmax_state = lax.fori_loop(
        0, cycle_size - 1, forward_turn, (key_heads, value_heads, initial)
    )
    run_top, run_total, run_acc = forward_block(
        softmax_state,
        query_heads,
        keys_now,
        values_now,
        own_blocks,
        source_blocks(cycle_size - 1),
        score_scale,
    )
    attn_float = run_acc / run_total[..., None]
    log_total = run_top + jnp.log(run_total)
    attention_output_rows = attn_float.reshape(all_seqs, length, head_cols).astype(jnp.bfloat16)

    def attn_term(row_start, row_count):
        return jnp.einsum(
            "xnv,vj->xnj",
            attention_output_rows,
            output_weight_complete,
            preferred_element_type=jnp.float32,
        )

    residual = token_float + head_total(attn_term, local_seqs)
    second_inverse = inverse_rms(residual)
    second_normed_rows = head_rows((residual * second_inverse * mlp_gain).astype(jnp.bfloat16))
    gate_preactivation = jnp.einsum(
        "zcv,vo->zco", second_normed_rows, gate_weight_complete, preferred_element_type=jnp.float32
    )
    up_preactivation = jnp.einsum(
        "zcv,vo->zco", second_normed_rows, up_weight_complete, preferred_element_type=jnp.float32
    )
    gate_sigmoid = jax.nn.sigmoid(gate_preactivation)
    gate_silu = gate_preactivation * gate_sigmoid
    hidden_rows = (gate_silu * up_preactivation).astype(jnp.bfloat16)

    def mlp_term(row_start, row_count):
        return jnp.einsum(
            "ipg,gh->iph", hidden_rows, down_weight_complete, preferred_element_type=jnp.float32
        )

    layer_output = (residual + head_total(mlp_term, local_seqs)).astype(jnp.bfloat16)
    output_gradient_rows = head_rows(output_grad)
    grad_hidden = jnp.einsum(
        "zka,na->zkn",
        output_gradient_rows,
        down_weight_complete,
        preferred_element_type=jnp.float32,
    )
    down_weight_gradient = jnp.einsum(
        "iry,irg->yg", hidden_rows, output_gradient_rows, preferred_element_type=jnp.float32
    )
    gate_activation_gradient = (
        grad_hidden
        * up_preactivation
        * gate_sigmoid
        * (1.0 + gate_preactivation * (1.0 - gate_sigmoid))
    ).astype(jnp.bfloat16)
    up_activation_gradient = (grad_hidden * gate_silu).astype(jnp.bfloat16)
    gate_grad = jnp.einsum(
        "npc,nph->ch",
        second_normed_rows,
        gate_activation_gradient,
        preferred_element_type=jnp.float32,
    )
    up_weight_gradient = jnp.einsum(
        "npc,nph->ch",
        second_normed_rows,
        up_activation_gradient,
        preferred_element_type=jnp.float32,
    )

    def second_term(row_start, row_count):
        gate_part = jnp.einsum(
            "rzp,wp->rzw",
            gate_activation_gradient,
            gate_weight_complete,
            preferred_element_type=jnp.float32,
        )
        return gate_part + jnp.einsum(
            "rzp,wp->rzw",
            up_activation_gradient,
            up_weight_complete,
            preferred_element_type=jnp.float32,
        )

    second_back, second_gain = norm_back(
        head_total(second_term, local_seqs), residual, second_inverse, mlp_gain
    )
    grad_residual = output_grad.astype(jnp.float32) + second_back
    attention_gradient_rows = head_rows(grad_residual.astype(jnp.bfloat16))
    grad_heads = (
        jnp.einsum(
            "zop,ip->zoi",
            attention_gradient_rows,
            output_weight_complete,
            preferred_element_type=jnp.float32,
        )
        .astype(jnp.bfloat16)
        .reshape(split_shape)
    )
    out_grad_full = jnp.einsum(
        "xjt,xjb->tb",
        attention_output_rows,
        attention_gradient_rows,
        preferred_element_type=jnp.float32,
    )
    row_delta = jnp.sum(grad_heads.astype(jnp.float32) * attn_float, axis=-1)
    zero_heads = jnp.zeros(split_shape, jnp.float32)

    def key_turn(cycle_step, cycle_state):
        keys_now, values_now, query_sum, key_sum, value_sum = cycle_state
        part_query, part_key, part_value = backward_block(
            query_heads,
            grad_heads,
            log_total,
            row_delta,
            keys_now,
            values_now,
            own_blocks,
            source_blocks(cycle_step),
            score_scale,
        )
        keys_now, values_now = passed_along((keys_now, values_now), "blk", 1)
        key_sum, value_sum = (
            passed_along((key_sum + part_key).astype(jnp.bfloat16), "blk", 1).astype(jnp.float32),
            passed_along((value_sum + part_value).astype(jnp.bfloat16), "blk", 1).astype(
                jnp.float32
            ),
        )
        return (keys_now, values_now, query_sum + part_query, key_sum, value_sum)

    cycle_state = lax.fori_loop(
        0, cycle_size - 1, key_turn, (key_heads, value_heads, zero_heads, zero_heads, zero_heads)
    )
    keys_now, values_now, query_sum, key_sum, value_sum = cycle_state
    part_query, part_key, part_value = backward_block(
        query_heads,
        grad_heads,
        log_total,
        row_delta,
        keys_now,
        values_now,
        own_blocks,
        source_blocks(cycle_size - 1),
        score_scale,
    )
    query_sum = query_sum + part_query
    key_sum, value_sum = (
        passed_along((key_sum + part_key).astype(jnp.bfloat16), "blk", 1).astype(jnp.float32),
        passed_along((value_sum + part_value).astype(jnp.bfloat16), "blk", 1).astype(jnp.float32),
    )
    query_weight_gradient = rotate_back(
        (query_sum * score_scale).reshape(all_seqs, length, head_cols),
        cosine_table,
        sine_table,
        HEAD_DIM,
    ).astype(jnp.bfloat16)
    key_weight_gradient = rotate_back(
        (key_sum * score_scale).reshape(all_seqs, length, head_cols),
        cosine_table,
        sine_table,
        HEAD_DIM,
    ).astype(jnp.bfloat16)
    value_weight_gradient = value_sum.reshape(all_seqs, length, head_cols).astype(jnp.bfloat16)
    query_grad_full = jnp.einsum(
        "wzi,wzo->io", first_normed_rows, query_weight_gradient, preferred_element_type=jnp.float32
    )
    key_grad_full = jnp.einsum(
        "wzi,wzo->io", first_normed_rows, key_weight_gradient, preferred_element_type=jnp.float32
    )
    value_grad_full = jnp.einsum(
        "wzi,wzo->io", first_normed_rows, value_weight_gradient, preferred_element_type=jnp.float32
    )

    def first_term(row_start, row_count):
        query_part = jnp.einsum(
            "fvw,ew->fve",
            query_weight_gradient,
            query_weight_complete,
            preferred_element_type=jnp.float32,
        )
        key_local_slice = jnp.einsum(
            "fvw,ew->fve",
            key_weight_gradient,
            key_weight_complete,
            preferred_element_type=jnp.float32,
        )
        value_part = jnp.einsum(
            "fvw,ew->fve",
            value_weight_gradient,
            value_weight_complete,
            preferred_element_type=jnp.float32,
        )
        return query_part + key_local_slice + value_part

    first_back, first_gain = norm_back(
        head_total(first_term, local_seqs), token_float, first_inverse, attn_gain
    )
    input_grad = grad_residual + first_back
    reduced = (
        lax.psum_scatter(
            query_grad_full.astype(jnp.bfloat16), "blk", scatter_dimension=0, tiled=True
        ).astype(jnp.float32),
        lax.psum_scatter(
            key_grad_full.astype(jnp.bfloat16), "blk", scatter_dimension=0, tiled=True
        ).astype(jnp.float32),
        lax.psum_scatter(
            value_grad_full.astype(jnp.bfloat16), "blk", scatter_dimension=0, tiled=True
        ).astype(jnp.float32),
        lax.psum_scatter(
            out_grad_full.astype(jnp.bfloat16), "blk", scatter_dimension=1, tiled=True
        ).astype(jnp.float32),
        lax.psum_scatter(
            gate_grad.astype(jnp.bfloat16), "blk", scatter_dimension=0, tiled=True
        ).astype(jnp.float32),
        lax.psum_scatter(
            up_weight_gradient.astype(jnp.bfloat16), "blk", scatter_dimension=0, tiled=True
        ).astype(jnp.float32),
        lax.psum_scatter(
            down_weight_gradient.astype(jnp.bfloat16), "blk", scatter_dimension=1, tiled=True
        ).astype(jnp.float32),
    )
    gain_sums = lax.psum((first_gain, second_gain), ("head", "blk"))
    return (
        layer_output,
        input_grad,
        gain_sums[0],
        reduced[0],
        reduced[1],
        reduced[2],
        reduced[3],
        gain_sums[1],
        reduced[4],
        reduced[5],
        reduced[6],
    )


def solution(mesh):
    placed = (
        P("head", "blk", None),
        P(),
        P(),
        P("blk", "head"),
        P("blk", "head"),
        P("blk", "head"),
        P("head", "blk"),
        P(),
        P("blk", "head"),
        P("blk", "head"),
        P("head", "blk"),
        P("head", "blk", None),
    )
    return jax.shard_map(
        on_device,
        mesh=mesh,
        in_specs=placed,
        out_specs=(
            P("head", "blk", None),
            P("head", "blk", None),
            P(),
            P("blk", "head"),
            P("blk", "head"),
            P("blk", "head"),
            P("head", "blk"),
            P(),
            P("blk", "head"),
            P("blk", "head"),
            P("head", "blk"),
        ),
        check_vma=False,
    )
```

profile of v0, /device:TPU:8, one launch (start us, length us, event | category | flops | bytes accessed | tf_op | source)
XLA Modules:
  0.0 2195.8 jit_solution(12537702366600271425)
XLA Ops:
  16.2 40.7 %all-gather.16.cloned.1.call-done = bf16[2048,256]{1,0:T(8,128)(2,1)} async-done(((bf16[128,256]{1,0:T(8,128)(2,1)}), bf16[2048,256]{1,0:T(8,128)(2,1)}) %all-gather.16.cloned.1.call-update) | async-done | bytes 1048592 | tf_op jit(solution)/shard_map/all_gather | solution.py:165
  56.9 90.4 %all-gather.12.cloned.1.call-done = bf16[8,128,2048]{2,1,0:T(8,128)(2,1)} async-done(((bf16[1,128,2048]{2,1,0:T(8,128)(2,1)}), bf16[8,128,2048]{2,1,0:T(8,128)(2,1)}) %all-gather.12.cloned.1.call-update) | async-done | bytes 4194320 | tf_op jit(solution)/shard_map/all_gather | solution.py:53
  151.9 45.6 %all-gather.14.cloned.1.call-done = bf16[2048,256]{1,0:T(8,128)(2,1)} async-done(((bf16[128,256]{1,0:T(8,128)(2,1)}), bf16[2048,256]{1,0:T(8,128)(2,1)}) %all-gather.14.cloned.1.call-update) | async-done | bytes 1048592 | tf_op jit(solution)/shard_map/all_gather | solution.py:164
  205.2 38.2 %all-gather.18.cloned.1.call-done = bf16[2048,256]{1,0:T(8,128)(2,1)} async-done(((bf16[128,256]{1,0:T(8,128)(2,1)}), bf16[2048,256]{1,0:T(8,128)(2,1)}) %all-gather.18.cloned.1.call-update) | async-done | bytes 1048592 | tf_op jit(solution)/shard_map/all_gather | solution.py:163
  256.7 287.8 %while.48 = (s32[]{:T(128)}, bf16[8,128,2,128]{3,1,2,0:T(8,128)(2,1)}, bf16[8,128,2,128]{3,1,2,0:T(8,128)(2,1)}, f32[8,128,2]{1,2,0:T(2,128)S(1)}, f32[8,128,2]{...) while((s32[]{:T(128)}, ...), condition=%wide.region_7.8_spmd.clone, body=%wide.region_3.7_spmd.clone.sunk | while | flops 137016464 | bytes 13514482 | solution.py:216
  279.7 12.3 collective-permute-done
  301.6 9.5 collective-permute-done
  320.5 9.5 collective-permute-done
  339.5 9.5 collective-permute-done
  358.5 9.5 collective-permute-done
  377.5 9.5 collective-permute-done
  396.5 9.5 collective-permute-done
  415.5 9.5 collective-permute-done
  434.5 9.5 collective-permute-done
  453.4 9.5 collective-permute-done
  472.4 9.5 collective-permute-done
  491.4 9.5 collective-permute-done
  510.4 9.5 collective-permute-done
  529.4 9.5 collective-permute-done
  555.4 86.0 %reduce-scatter.20.cloned.1.call-done = bf16[1,128,2048]{2,1,0:T(8,128)(2,1)} async-done(((bf16[8,128,2048]{2,1,0:T(8,128)(2,1)}), bf16[1,128,2048]{2,1,0:T(8,128)(2,1)}) %reduce-scatter.20.cloned.1.call-update) | async-done | bytes 524304 | tf_op jit(solution)/shard_map/reduce_scatter | solution.py:57
  647.4 48.1 %all-gather.26.cloned.1.call-done = bf16[2048,688]{0,1:T(8,128)(2,1)} async-done(((bf16[128,688]{0,1:T(8,128)(2,1)}), bf16[2048,688]{0,1:T(8,128)(2,1)}) %all-gather.26.cloned.1.call-update) | async-done | bytes 2818064 | tf_op jit(solution)/shard_map/all_gather | solution.py:170
  695.5 89.4 %all-gather.22.cloned.1.call-done = bf16[8,128,2048]{2,1,0:T(8,128)(2,1)} async-done(((bf16[1,128,2048]{2,1,0:T(8,128)(2,1)}), bf16[8,128,2048]{2,1,0:T(8,128)(2,1)}) %all-gather.22.cloned.1.call-update) | async-done | bytes 4194320 | tf_op jit(solution)/shard_map/all_gather | solution.py:53
  791.7 48.7 %all-gather.24.cloned.1.call-done = bf16[2048,688]{0,1:T(8,128)(2,1)} async-done(((bf16[128,688]{0,1:T(8,128)(2,1)}), bf16[2048,688]{0,1:T(8,128)(2,1)}) %all-gather.24.cloned.1.call-update) | async-done | bytes 2818064 | tf_op jit(solution)/shard_map/all_gather | solution.py:169
  847.2 43.4 %all-gather.28.cloned.1.call-done = bf16[688,2048]{1,0:T(8,128)(2,1)} async-done(((bf16[688,128]{1,0:T(8,128)(2,1)}), bf16[688,2048]{1,0:T(8,128)(2,1)}) %all-gather.28.cloned.1.call-update) | async-done | bytes 2818064 | tf_op jit(solution)/shard_map/all_gather | solution.py:171
  890.7 88.8 %all-gather.30.cloned.1.call-done = bf16[8,128,2048]{2,1,0:T(8,128)(2,1)} async-done(((bf16[1,128,2048]{2,1,0:T(8,128)(2,1)}), bf16[8,128,2048]{2,1,0:T(8,128)(2,1)}) %all-gather.30.cloned.1.call-update) | async-done | bytes 4194320 | tf_op jit(solution)/shard_map/all_gather | solution.py:53
  979.5 8.9 multiply_convert_fusion
  997.4 92.8 %reduce-scatter.24.cloned.1.call-done = bf16[1,128,2048]{2,1,0:T(8,128)(2,1)} async-done(((bf16[8,128,2048]{2,1,0:T(8,128)(2,1)}), bf16[1,128,2048]{2,1,0:T(8,128)(2,1)}) %reduce-scatter.24.cloned.1.call-update) | async-done | bytes 524304 | tf_op jit(solution)/shard_map/reduce_scatter | solution.py:57
  1128.2 56.6 %all-gather.32.cloned.1.call-done = bf16[8,128,2048]{2,1,0:T(8,128)(2,1)} async-done(((bf16[1,128,2048]{2,1,0:T(8,128)(2,1)}), bf16[8,128,2048]{2,1,0:T(8,128)(2,1)}) %all-gather.32.cloned.1.call-update) | async-done | bytes 4194320 | tf_op jit(solution)/shard_map/all_gather | solution.py:53
  1196.1 518.1 %while.49 = (s32[]{:T(128)}, bf16[8,128,2,128]{3,1,2,0:T(8,128)(2,1)}, bf16[8,128,2,128]{3,1,2,0:T(8,128)(2,1)S(1)}, f32[8,128,2,128]{3,1,2,0:T(8,128)}, f32[8,1...) while((s32[]{:T(128)}, ...), condition=%wide.region_19.20_spmd.clone, body=%wide.region_17.19_spmd.clone.sunk | while | flops 340167808 | bytes 35944336 | solution.py:349
  1236.2 9.8 collective-permute-done.4
  1270.1 8.8 collective-permute-done.4
  1305.1 8.8 collective-permute-done.4
  1338.1 8.8 collective-permute-done.4
  1379.5 8.8 collective-permute-done.4
  1414.6 8.8 collective-permute-done.4
  1447.5 8.8 collective-permute-done.4
  1488.9 8.8 collective-permute-done.4
  1524.0 8.8 collective-permute-done.4
  1556.9 8.8 collective-permute-done.4
  1589.8 8.8 collective-permute-done.4
  1655.6 8.8 collective-permute-done.4
  1688.5 8.8 collective-permute-done.4
  1789.7 68.5 %reduce-scatter.32.cloned.1.call-done = bf16[128,256]{1,0:T(8,128)(2,1)} async-done(((bf16[2048,256]{1,0:T(8,128)(2,1)}), bf16[128,256]{1,0:T(8,128)(2,1)}) %reduce-scatter.32.cloned.1.call-update) | async-done | bytes 65552 | tf_op jit(solution)/shard_map/reduce_scatter | solution.py:424
  1859.7 68.3 %reduce-scatter.30.cloned.1.call-done = bf16[128,256]{1,0:T(8,128)(2,1)} async-done(((bf16[2048,256]{1,0:T(8,128)(2,1)}), bf16[128,256]{1,0:T(8,128)(2,1)}) %reduce-scatter.30.cloned.1.call-update) | async-done | bytes 65552 | tf_op jit(solution)/shard_map/reduce_scatter | solution.py:421
  1929.5 69.2 %reduce-scatter.28.cloned.1.call-done = bf16[128,256]{1,0:T(8,128)(2,1)} async-done(((bf16[2048,256]{1,0:T(8,128)(2,1)}), bf16[128,256]{1,0:T(8,128)(2,1)}) %reduce-scatter.28.cloned.1.call-update) | async-done | bytes 65552 | tf_op jit(solution)/shard_map/reduce_scatter | solution.py:418
  2000.1 89.6 %reduce-scatter.26.cloned.1.call-done = bf16[1,128,2048]{2,1,0:T(8,128)(2,1)} async-done(((bf16[8,128,2048]{2,1,0:T(8,128)(2,1)}), bf16[1,128,2048]{2,1,0:T(8,128)(2,1)}) %reduce-scatter.26.cloned.1.call-update) | async-done | bytes 524304 | tf_op jit(solution)/shard_map/reduce_scatter | solution.py:57
  2091.1 82.0 %all-reduce = (f32[2048]{0:T(1024)}, f32[2048]{0:T(1024)}) all-reduce(f32[2048]{0:T(1024)S(1)} %get-tuple-element.750, f32[2048]{0:T(1024)S(1)} %get-tuple-element.748), channel_id=1, replica_groups=mesh['head'=8,'blk'=16] {'head','blk'}, use_global_device_ids=true, to_apply=%region_23.24 | all-reduce | flops 4096 | bytes 32768 | tf_op jit(solution)/shard_map/psum | solution.py:440
  2173.2 12.1 reduce-scatter.22.cloned.1.call-done
  (785 shorter events, 759.7 us)
Async XLA Ops:
  7.2 49.7 %all-gather.16.cloned.1.call-start = ((), (), s32[]{:S(2)}) async-start(), calls=%async_computation.13 | async-start | bytes 1114112 | tf_op jit(solution)/shard_map/all_gather | solution.py:165
  7.9 139.3 %all-gather.12.cloned.1.call-start = ((), (), s32[]{:S(2)}) async-start(), calls=%async_computation.11 | async-start | bytes 4718592 | tf_op jit(solution)/shard_map/all_gather | solution.py:53
  11.8 185.6 %all-gather.14.cloned.1.call-start = ((), (), s32[]{:S(2)}) async-start(), calls=%async_computation.12 | async-start | bytes 1114112 | tf_op jit(solution)/shard_map/all_gather | solution.py:164
  12.6 230.8 %all-gather.18.cloned.1.call-start = ((), (), s32[]{:S(2)}) async-start(), calls=%async_computation.14 | async-start | bytes 1114112 | tf_op jit(solution)/shard_map/all_gather | solution.py:163
  13.1 536.2 %all-gather.20.cloned.1.call-start = ((), (), s32[]{:S(2)}) async-start(), calls=%async_computation.15 | async-start | bytes 1114112 | tf_op jit(solution)/shard_map/all_gather | solution.py:166
  13.7 627.7 %reduce-scatter.20.cloned.1.call-start = ((), (), s32[]{:S(2)}) async-start(), calls=%async_computation.16 | async-start | bytes 4718592 | tf_op jit(solution)/shard_map/reduce_scatter | solution.py:57
  554.6 140.8 %all-gather.26.cloned.1.call-start = ((), (), s32[]{:S(2)}) async-start(), calls=%async_computation.19 | async-start | bytes 2994176 | tf_op jit(solution)/shard_map/all_gather | solution.py:170
  555.4 229.5 %all-gather.22.cloned.1.call-start = ((), (), s32[]{:S(2)}) async-start(), calls=%async_computation.17 | async-start | bytes 4718592 | tf_op jit(solution)/shard_map/all_gather | solution.py:53
  644.8 195.6 %all-gather.24.cloned.1.call-start = ((), (), s32[]{:S(2)}) async-start(), calls=%async_computation.18 | async-start | bytes 2994176 | tf_op jit(solution)/shard_map/all_gather | solution.py:169
  645.6 245.1 %all-gather.28.cloned.1.call-start = ((), (), s32[]{:S(2)}) async-start(), calls=%async_computation.20 | async-start | bytes 2994176 | tf_op jit(solution)/shard_map/all_gather | solution.py:171
  646.1 333.3 %all-gather.30.cloned.1.call-start = ((), (), s32[]{:S(2)}) async-start(), calls=%async_computation.22 | async-start | bytes 4718592 | tf_op jit(solution)/shard_map/all_gather | solution.py:53
  646.9 443.3 %reduce-scatter.24.cloned.1.call-start = ((), (), s32[]{:S(2)}) async-start(), calls=%async_computation.23 | async-start | bytes 4718592 | tf_op jit(solution)/shard_map/reduce_scatter | solution.py:57
  997.3 187.5 %all-gather.32.cloned.1.call-start = ((), (), s32[]{:S(2)}) async-start(), calls=%async_computation.24 | async-start | bytes 4718592 | tf_op jit(solution)/shard_map/all_gather | solution.py:53
  1093.9 679.7 %reduce-scatter.40.cloned.1.call-start = ((), (), s32[]{:S(2)}) async-start(), calls=%async_computation.32 | async-start | bytes 3342336
  1105.3 670.4 %reduce-scatter.36.cloned.1.call-start = ((), (), s32[]{:S(2)}) async-start(), calls=%async_computation.30 | async-start | bytes 3342336
  1116.7 660.8 %reduce-scatter.38.cloned.1.call-start = ((), (), s32[]{:S(2)}) async-start(), calls=%async_computation.31 | async-start | bytes 3342336
  1128.2 659.9 %reduce-scatter.34.cloned.1.call-start = ((), (), s32[]{:S(2)}) async-start(), calls=%async_computation.29 | async-start | bytes 1114112
  1202.7 26.4 %collective-permute-start.2 = (bf16[8,128,2,128]{3,1,2,0:T(8,128)(2,1)S(1)}, bf16[8,128,2,128]{3,1,2,0:T(8,128)(2,1)}, u32[]{:S(2)}, u32[]{:S(2)}) collective-permute-start(bf16[8,128,2,128]{3,1,2,0:T(8,128)(2,1)S(1)} %copy.238), channel_id=1, source_target_pairs={{0,1},{1,2},{2,3},{3,4},{4,5},{5,6},{6,7},{7,8},{8,9},{9,10},{10,1... | collective-permute-start | bytes 1572872 | tf_op jit(solution)/shard_map/while/body/eval_jaxpr/ppermute | solution.py:16
  1233.7 23.5 %collective-permute-start.3 = (bf16[8,128,2,128]{3,1,2,0:T(8,128)(2,1)S(1)}, bf16[8,128,2,128]{3,1,2,0:T(8,128)(2,1)S(1)}, u32[]{:S(2)}, u32[]{:S(2)}) collective-permute-start(bf16[8,128,2,128]{3,1,2,0:T(8,128)(2,1)S(1)} %copy.239), channel_id=1, source_target_pairs={{0,1},{1,2},{2,3},{3,4},{4,5},{5,6},{6,7},{7,8},{8,9},{9,10},{10,1... | collective-permute-start | bytes 1572872 | tf_op jit(solution)/shard_map/while/body/eval_jaxpr/ppermute | solution.py:16
  1233.7 29.2 %collective-permute-start.2 = (bf16[8,128,2,128]{3,1,2,0:T(8,128)(2,1)S(1)}, bf16[8,128,2,128]{3,1,2,0:T(8,128)(2,1)}, u32[]{:S(2)}, u32[]{:S(2)}) collective-permute-start(bf16[8,128,2,128]{3,1,2,0:T(8,128)(2,1)S(1)} %copy.238), channel_id=1, source_target_pairs={{0,1},{1,2},{2,3},{3,4},{4,5},{5,6},{6,7},{7,8},{8,9},{9,10},{10,1... | collective-permute-start | bytes 1572872 | tf_op jit(solution)/shard_map/while/body/eval_jaxpr/ppermute | solution.py:16
  1267.5 24.7 %collective-permute-start.3 = (bf16[8,128,2,128]{3,1,2,0:T(8,128)(2,1)S(1)}, bf16[8,128,2,128]{3,1,2,0:T(8,128)(2,1)S(1)}, u32[]{:S(2)}, u32[]{:S(2)}) collective-permute-start(bf16[8,128,2,128]{3,1,2,0:T(8,128)(2,1)S(1)} %copy.239), channel_id=1, source_target_pairs={{0,1},{1,2},{2,3},{3,4},{4,5},{5,6},{6,7},{7,8},{8,9},{9,10},{10,1... | collective-permute-start | bytes 1572872 | tf_op jit(solution)/shard_map/while/body/eval_jaxpr/ppermute | solution.py:16
  1267.5 30.4 %collective-permute-start.2 = (bf16[8,128,2,128]{3,1,2,0:T(8,128)(2,1)S(1)}, bf16[8,128,2,128]{3,1,2,0:T(8,128)(2,1)}, u32[]{:S(2)}, u32[]{:S(2)}) collective-permute-start(bf16[8,128,2,128]{3,1,2,0:T(8,128)(2,1)S(1)} %copy.238), channel_id=1, source_target_pairs={{0,1},{1,2},{2,3},{3,4},{4,5},{5,6},{6,7},{7,8},{8,9},{9,10},{10,1... | collective-permute-start | bytes 1572872 | tf_op jit(solution)/shard_map/while/body/eval_jaxpr/ppermute | solution.py:16
  1302.6 22.5 %collective-permute-start.3 = (bf16[8,128,2,128]{3,1,2,0:T(8,128)(2,1)S(1)}, bf16[8,128,2,128]{3,1,2,0:T(8,128)(2,1)S(1)}, u32[]{:S(2)}, u32[]{:S(2)}) collective-permute-start(bf16[8,128,2,128]{3,1,2,0:T(8,128)(2,1)S(1)} %copy.239), channel_id=1, source_target_pairs={{0,1},{1,2},{2,3},{3,4},{4,5},{5,6},{6,7},{7,8},{8,9},{9,10},{10,1... | collective-permute-start | bytes 1572872 | tf_op jit(solution)/shard_map/while/body/eval_jaxpr/ppermute | solution.py:16
  1302.6 28.3 %collective-permute-start.2 = (bf16[8,128,2,128]{3,1,2,0:T(8,128)(2,1)S(1)}, bf16[8,128,2,128]{3,1,2,0:T(8,128)(2,1)}, u32[]{:S(2)}, u32[]{:S(2)}) collective-permute-start(bf16[8,128,2,128]{3,1,2,0:T(8,128)(2,1)S(1)} %copy.238), channel_id=1, source_target_pairs={{0,1},{1,2},{2,3},{3,4},{4,5},{5,6},{6,7},{7,8},{8,9},{9,10},{10,1... | collective-permute-start | bytes 1572872 | tf_op jit(solution)/shard_map/while/body/eval_jaxpr/ppermute | solution.py:16
  1335.5 31.0 %collective-permute-start.3 = (bf16[8,128,2,128]{3,1,2,0:T(8,128)(2,1)S(1)}, bf16[8,128,2,128]{3,1,2,0:T(8,128)(2,1)S(1)}, u32[]{:S(2)}, u32[]{:S(2)}) collective-permute-start(bf16[8,128,2,128]{3,1,2,0:T(8,128)(2,1)S(1)} %copy.239), channel_id=1, source_target_pairs={{0,1},{1,2},{2,3},{3,4},{4,5},{5,6},{6,7},{7,8},{8,9},{9,10},{10,1... | collective-permute-start | bytes 1572872 | tf_op jit(solution)/shard_map/while/body/eval_jaxpr/ppermute | solution.py:16
  1335.5 36.8 %collective-permute-start.2 = (bf16[8,128,2,128]{3,1,2,0:T(8,128)(2,1)S(1)}, bf16[8,128,2,128]{3,1,2,0:T(8,128)(2,1)}, u32[]{:S(2)}, u32[]{:S(2)}) collective-permute-start(bf16[8,128,2,128]{3,1,2,0:T(8,128)(2,1)S(1)} %copy.238), channel_id=1, source_target_pairs={{0,1},{1,2},{2,3},{3,4},{4,5},{5,6},{6,7},{7,8},{8,9},{9,10},{10,1... | collective-permute-start | bytes 1572872 | tf_op jit(solution)/shard_map/while/body/eval_jaxpr/ppermute | solution.py:16
  1376.9 24.7 %collective-permute-start.3 = (bf16[8,128,2,128]{3,1,2,0:T(8,128)(2,1)S(1)}, bf16[8,128,2,128]{3,1,2,0:T(8,128)(2,1)S(1)}, u32[]{:S(2)}, u32[]{:S(2)}) collective-permute-start(bf16[8,128,2,128]{3,1,2,0:T(8,128)(2,1)S(1)} %copy.239), channel_id=1, source_target_pairs={{0,1},{1,2},{2,3},{3,4},{4,5},{5,6},{6,7},{7,8},{8,9},{9,10},{10,1... | collective-permute-start | bytes 1572872 | tf_op jit(solution)/shard_map/while/body/eval_jaxpr/ppermute | solution.py:16
  1376.9 30.4 %collective-permute-start.2 = (bf16[8,128,2,128]{3,1,2,0:T(8,128)(2,1)S(1)}, bf16[8,128,2,128]{3,1,2,0:T(8,128)(2,1)}, u32[]{:S(2)}, u32[]{:S(2)}) collective-permute-start(bf16[8,128,2,128]{3,1,2,0:T(8,128)(2,1)S(1)} %copy.238), channel_id=1, source_target_pairs={{0,1},{1,2},{2,3},{3,4},{4,5},{5,6},{6,7},{7,8},{8,9},{9,10},{10,1... | collective-permute-start | bytes 1572872 | tf_op jit(solution)/shard_map/while/body/eval_jaxpr/ppermute | solution.py:16
  1412.0 22.5 %collective-permute-start.3 = (bf16[8,128,2,128]{3,1,2,0:T(8,128)(2,1)S(1)}, bf16[8,128,2,128]{3,1,2,0:T(8,128)(2,1)S(1)}, u32[]{:S(2)}, u32[]{:S(2)}) collective-permute-start(bf16[8,128,2,128]{3,1,2,0:T(8,128)(2,1)S(1)} %copy.239), channel_id=1, source_target_pairs={{0,1},{1,2},{2,3},{3,4},{4,5},{5,6},{6,7},{7,8},{8,9},{9,10},{10,1... | collective-permute-start | bytes 1572872 | tf_op jit(solution)/shard_map/while/body/eval_jaxpr/ppermute | solution.py:16
  1412.0 28.3 %collective-permute-start.2 = (bf16[8,128,2,128]{3,1,2,0:T(8,128)(2,1)S(1)}, bf16[8,128,2,128]{3,1,2,0:T(8,128)(2,1)}, u32[]{:S(2)}, u32[]{:S(2)}) collective-permute-start(bf16[8,128,2,128]{3,1,2,0:T(8,128)(2,1)S(1)} %copy.238), channel_id=1, source_target_pairs={{0,1},{1,2},{2,3},{3,4},{4,5},{5,6},{6,7},{7,8},{8,9},{9,10},{10,1... | collective-permute-start | bytes 1572872 | tf_op jit(solution)/shard_map/while/body/eval_jaxpr/ppermute | solution.py:16
  1444.9 31.0 %collective-permute-start.3 = (bf16[8,128,2,128]{3,1,2,0:T(8,128)(2,1)S(1)}, bf16[8,128,2,128]{3,1,2,0:T(8,128)(2,1)S(1)}, u32[]{:S(2)}, u32[]{:S(2)}) collective-permute-start(bf16[8,128,2,128]{3,1,2,0:T(8,128)(2,1)S(1)} %copy.239), channel_id=1, source_target_pairs={{0,1},{1,2},{2,3},{3,4},{4,5},{5,6},{6,7},{7,8},{8,9},{9,10},{10,1... | collective-permute-start | bytes 1572872 | tf_op jit(solution)/shard_map/while/body/eval_jaxpr/ppermute | solution.py:16
  1444.9 36.8 %collective-permute-start.2 = (bf16[8,128,2,128]{3,1,2,0:T(8,128)(2,1)S(1)}, bf16[8,128,2,128]{3,1,2,0:T(8,128)(2,1)}, u32[]{:S(2)}, u32[]{:S(2)}) collective-permute-start(bf16[8,128,2,128]{3,1,2,0:T(8,128)(2,1)S(1)} %copy.238), channel_id=1, source_target_pairs={{0,1},{1,2},{2,3},{3,4},{4,5},{5,6},{6,7},{7,8},{8,9},{9,10},{10,1... | collective-permute-start | bytes 1572872 | tf_op jit(solution)/shard_map/while/body/eval_jaxpr/ppermute | solution.py:16
  1486.3 24.7 %collective-permute-start.3 = (bf16[8,128,2,128]{3,1,2,0:T(8,128)(2,1)S(1)}, bf16[8,128,2,128]{3,1,2,0:T(8,128)(2,1)S(1)}, u32[]{:S(2)}, u32[]{:S(2)}) collective-permute-start(bf16[8,128,2,128]{3,1,2,0:T(8,128)(2,1)S(1)} %copy.239), channel_id=1, source_target_pairs={{0,1},{1,2},{2,3},{3,4},{4,5},{5,6},{6,7},{7,8},{8,9},{9,10},{10,1... | collective-permute-start | bytes 1572872 | tf_op jit(solution)/shard_map/while/body/eval_jaxpr/ppermute | solution.py:16
  1486.3 30.4 %collective-permute-start.2 = (bf16[8,128,2,128]{3,1,2,0:T(8,128)(2,1)S(1)}, bf16[8,128,2,128]{3,1,2,0:T(8,128)(2,1)}, u32[]{:S(2)}, u32[]{:S(2)}) collective-permute-start(bf16[8,128,2,128]{3,1,2,0:T(8,128)(2,1)S(1)} %copy.238), channel_id=1, source_target_pairs={{0,1},{1,2},{2,3},{3,4},{4,5},{5,6},{6,7},{7,8},{8,9},{9,10},{10,1... | collective-permute-start | bytes 1572872 | tf_op jit(solution)/shard_map/while/body/eval_jaxpr/ppermute | solution.py:16
  1521.4 22.5 %collective-permute-start.3 = (bf16[8,128,2,128]{3,1,2,0:T(8,128)(2,1)S(1)}, bf16[8,128,2,128]{3,1,2,0:T(8,128)(2,1)S(1)}, u32[]{:S(2)}, u32[]{:S(2)}) collective-permute-start(bf16[8,128,2,128]{3,1,2,0:T(8,128)(2,1)S(1)} %copy.239), channel_id=1, source_target_pairs={{0,1},{1,2},{2,3},{3,4},{4,5},{5,6},{6,7},{7,8},{8,9},{9,10},{10,1... | collective-permute-start | bytes 1572872 | tf_op jit(solution)/shard_map/while/body/eval_jaxpr/ppermute | solution.py:16
  1521.4 28.3 %collective-permute-start.2 = (bf16[8,128,2,128]{3,1,2,0:T(8,128)(2,1)S(1)}, bf16[8,128,2,128]{3,1,2,0:T(8,128)(2,1)}, u32[]{:S(2)}, u32[]{:S(2)}) collective-permute-start(bf16[8,128,2,128]{3,1,2,0:T(8,128)(2,1)S(1)} %copy.238), channel_id=1, source_target_pairs={{0,1},{1,2},{2,3},{3,4},{4,5},{5,6},{6,7},{7,8},{8,9},{9,10},{10,1... | collective-permute-start | bytes 1572872 | tf_op jit(solution)/shard_map/while/body/eval_jaxpr/ppermute | solution.py:16
  1554.3 22.5 %collective-permute-start.3 = (bf16[8,128,2,128]{3,1,2,0:T(8,128)(2,1)S(1)}, bf16[8,128,2,128]{3,1,2,0:T(8,128)(2,1)S(1)}, u32[]{:S(2)}, u32[]{:S(2)}) collective-permute-start(bf16[8,128,2,128]{3,1,2,0:T(8,128)(2,1)S(1)} %copy.239), channel_id=1, source_target_pairs={{0,1},{1,2},{2,3},{3,4},{4,5},{5,6},{6,7},{7,8},{8,9},{9,10},{10,1... | collective-permute-start | bytes 1572872 | tf_op jit(solution)/shard_map/while/body/eval_jaxpr/ppermute | solution.py:16
  1554.3 28.3 %collective-permute-start.2 = (bf16[8,128,2,128]{3,1,2,0:T(8,128)(2,1)S(1)}, bf16[8,128,2,128]{3,1,2,0:T(8,128)(2,1)}, u32[]{:S(2)}, u32[]{:S(2)}) collective-permute-start(bf16[8,128,2,128]{3,1,2,0:T(8,128)(2,1)S(1)} %copy.238), channel_id=1, source_target_pairs={{0,1},{1,2},{2,3},{3,4},{4,5},{5,6},{6,7},{7,8},{8,9},{9,10},{10,1... | collective-permute-start | bytes 1572872 | tf_op jit(solution)/shard_map/while/body/eval_jaxpr/ppermute | solution.py:16
  1587.2 22.5 %collective-permute-start.3 = (bf16[8,128,2,128]{3,1,2,0:T(8,128)(2,1)S(1)}, bf16[8,128,2,128]{3,1,2,0:T(8,128)(2,1)S(1)}, u32[]{:S(2)}, u32[]{:S(2)}) collective-permute-start(bf16[8,128,2,128]{3,1,2,0:T(8,128)(2,1)S(1)} %copy.239), channel_id=1, source_target_pairs={{0,1},{1,2},{2,3},{3,4},{4,5},{5,6},{6,7},{7,8},{8,9},{9,10},{10,1... | collective-permute-start | bytes 1572872 | tf_op jit(solution)/shard_map/while/body/eval_jaxpr/ppermute | solution.py:16
  1587.2 28.3 %collective-permute-start.2 = (bf16[8,128,2,128]{3,1,2,0:T(8,128)(2,1)S(1)}, bf16[8,128,2,128]{3,1,2,0:T(8,128)(2,1)}, u32[]{:S(2)}, u32[]{:S(2)}) collective-permute-start(bf16[8,128,2,128]{3,1,2,0:T(8,128)(2,1)S(1)} %copy.238), channel_id=1, source_target_pairs={{0,1},{1,2},{2,3},{3,4},{4,5},{5,6},{6,7},{7,8},{8,9},{9,10},{10,1... | collective-permute-start | bytes 1572872 | tf_op jit(solution)/shard_map/while/body/eval_jaxpr/ppermute | solution.py:16
  1620.1 28.3 %collective-permute-start.2 = (bf16[8,128,2,128]{3,1,2,0:T(8,128)(2,1)S(1)}, bf16[8,128,2,128]{3,1,2,0:T(8,128)(2,1)}, u32[]{:S(2)}, u32[]{:S(2)}) collective-permute-start(bf16[8,128,2,128]{3,1,2,0:T(8,128)(2,1)S(1)} %copy.238), channel_id=1, source_target_pairs={{0,1},{1,2},{2,3},{3,4},{4,5},{5,6},{6,7},{7,8},{8,9},{9,10},{10,1... | collective-permute-start | bytes 1572872 | tf_op jit(solution)/shard_map/while/body/eval_jaxpr/ppermute | solution.py:16
  1653.0 28.3 %collective-permute-start.2 = (bf16[8,128,2,128]{3,1,2,0:T(8,128)(2,1)S(1)}, bf16[8,128,2,128]{3,1,2,0:T(8,128)(2,1)}, u32[]{:S(2)}, u32[]{:S(2)}) collective-permute-start(bf16[8,128,2,128]{3,1,2,0:T(8,128)(2,1)S(1)} %copy.238), channel_id=1, source_target_pairs={{0,1},{1,2},{2,3},{3,4},{4,5},{5,6},{6,7},{7,8},{8,9},{9,10},{10,1... | collective-permute-start | bytes 1572872 | tf_op jit(solution)/shard_map/while/body/eval_jaxpr/ppermute | solution.py:16
  1686.0 28.3 %collective-permute-start.2 = (bf16[8,128,2,128]{3,1,2,0:T(8,128)(2,1)S(1)}, bf16[8,128,2,128]{3,1,2,0:T(8,128)(2,1)}, u32[]{:S(2)}, u32[]{:S(2)}) collective-permute-start(bf16[8,128,2,128]{3,1,2,0:T(8,128)(2,1)S(1)} %copy.238), channel_id=1, source_target_pairs={{0,1},{1,2},{2,3},{3,4},{4,5},{5,6},{6,7},{7,8},{8,9},{9,10},{10,1... | collective-permute-start | bytes 1572872 | tf_op jit(solution)/shard_map/while/body/eval_jaxpr/ppermute | solution.py:16
  1718.7 139.4 %reduce-scatter.32.cloned.1.call-start = ((), (), s32[]{:S(2)}) async-start(), calls=%async_computation.28 | async-start | bytes 1114112 | tf_op jit(solution)/shard_map/reduce_scatter | solution.py:424
  1737.6 190.4 %reduce-scatter.30.cloned.1.call-start = ((), (), s32[]{:S(2)}) async-start(), calls=%async_computation.27 | async-start | bytes 1114112 | tf_op jit(solution)/shard_map/reduce_scatter | solution.py:421
  1753.2 245.4 %reduce-scatter.28.cloned.1.call-start = ((), (), s32[]{:S(2)}) async-start(), calls=%async_computation.26 | async-start | bytes 1114112 | tf_op jit(solution)/shard_map/reduce_scatter | solution.py:418
  1757.9 331.8 %reduce-scatter.26.cloned.1.call-start = ((), (), s32[]{:S(2)}) async-start(), calls=%async_computation.25 | async-start | bytes 4718592 | tf_op jit(solution)/shard_map/reduce_scatter | solution.py:57
  1765.3 420.0 %reduce-scatter.22.cloned.1.call-start = ((), (), s32[]{:S(2)}) async-start(), calls=%async_computation.21 | async-start | bytes 4718592 | tf_op jit(solution)/shard_map/reduce_scatter | solution.py:57
  (132 other events, 4304.7 us)
Sparse Core Ops, SparseCore 0:
  10.5 46.3 all-gather.15
  59.1 88.0 all-gather.11
  149.7 47.7 all-gather.13
  199.8 43.5 all-gather.17
  245.5 54.5 all-gather.19
  554.7 86.6 reduce-scatter.19
  643.7 51.7 all-gather.25
  697.7 87.1 all-gather.21
  787.1 53.2 all-gather.23
  842.5 48.1 all-gather.27
  892.3 87.1 all-gather.29
  997.4 92.6 reduce-scatter.23
  1094.0 90.7 all-gather.31
  1188.7 113.5 reduce-scatter.39
  1306.2 105.4 reduce-scatter.35
  1415.6 105.4 reduce-scatter.37
  1718.8 69.1 reduce-scatter.33
  1792.1 65.9 reduce-scatter.31
  1861.9 65.9 reduce-scatter.29
  1932.6 65.9 reduce-scatter.27
  2001.0 88.6 reduce-scatter.25
  2092.2 93.1 reduce-scatter.21
where the time goes:
time: 2210 us; the launch traced here: 2200 us
  waiting for transfers between devices  1670 us (76%)
  matrix products  219 us (10%)
  other arithmetic  108 us (5%)
  local copies, waits for them, and re-layouts  92.2 us (4%)
  blocking collectives  82 us (4%)
    ppermute x92, waiting for transfers between devices, passed_along(): return lax.ppermute(value, axis, pairs)  579 us
    all_gather x4, waiting for transfers between devices, head_rows(): return lax.all_gather(values, 'head', axis=0, tiled=True)  325 us
    reduce_scatter x4, waiting for transfers between devices, head_total(): lax.psum_scatter(term_fn(jnp.int32(0), row_total * lax.axis_size('head'))...  281 us
    psum x1, blocking collectives, on_device(): gain_sums = lax.psum((first_gain, second_gain), ('head', 'blk'))  82 us
    reduce_scatter x1, waiting for transfers between devices, on_device(): lax.psum_scatter(query_grad_full.astype(jnp.bfloat16), 'blk', scatter_dim...  69.2 us
    reduce_scatter x1, waiting for transfers between devices, on_device(): lax.psum_scatter(value_grad_full.astype(jnp.bfloat16), 'blk', scatter_dim...  68.5 us
    reduce_scatter x1, waiting for transfers between devices, on_device(): lax.psum_scatter(key_grad_full.astype(jnp.bfloat16), 'blk', scatter_dimen...  68.3 us
    all_gather x1, waiting for transfers between devices, on_device(): lax.all_gather(gate_weight, 'blk', axis=0, tiled=True)  48.7 us
  transfers between devices with their start and end apart: 114, of which 110 were waited for; matrix products, arithmetic and copies ran while one was open for 18% of the time, Pallas kernels for 0%

commit v1 on v0

v1 whole, which is shorter than its diff:
```python
import functools

import jax
import jax.numpy as jnp
from jax import lax
from jax.experimental import pallas as pl
from jax.experimental.pallas import tpu as pltpu
from jax.sharding import Mesh
from jax.sharding import PartitionSpec as P

HEAD_DIM = 128
SEQ = 2048
TILE = 256
norm_eps = 1e-05
masked_score = -1e30
score_scale = HEAD_DIM ** (-0.5)
log2_e = 1.4426950408889634
f32 = jnp.float32
bf16 = jnp.bfloat16
VMEM_LIMIT = 56 * 1024 * 1024

Y_STEP = {1: 2, 2: 1, 3: 3}


def swap(value, axis, step):
    if axis == "y":
        names, count, step = ("yl", "yh"), 4, Y_STEP[step]
    else:
        names, count = axis, lax.axis_size(axis)
    return lax.ppermute(value, names, [(i, i ^ step) for i in range(count)])


def middle(rows):
    return (rows // 2 + 15) // 16 * 16


def gather4(value, axis):
    half = middle(value.shape[0])
    near1 = swap(value, axis, 1)
    near3 = swap(value, axis, 3)
    far = jnp.concatenate([swap(near3[:half], axis, 1), swap(near1[half:], axis, 3)], axis=0)
    return [value, near1, far, near3]


def scatter4(parts, axis):
    own, part1, part2, part3 = parts
    half = middle(own.shape[0])
    from1 = swap(part2[:half], axis, 1)
    from3 = swap(part2[half:], axis, 3)
    part3 = jnp.concatenate(
        [(part3[:half].astype(f32) + from1.astype(f32)).astype(bf16), part3[half:]], axis=0
    )
    part1 = jnp.concatenate(
        [part1[:half], (part1[half:].astype(f32) + from3.astype(f32)).astype(bf16)], axis=0
    )
    got1, got3 = swap(part1, axis, 1), swap(part3, axis, 3)
    return own.astype(f32) + got1.astype(f32) + got3.astype(f32)


def total4(value, axis):
    return (value + swap(value, axis, 1)) + (swap(value, axis, 2) + swap(value, axis, 3))


def vmem_spec():
    return pl.BlockSpec(memory_space=pltpu.VMEM)


def smem_spec():
    return pl.BlockSpec(memory_space=pltpu.SMEM)


def params():
    return pltpu.CompilerParams(vmem_limit_bytes=VMEM_LIMIT)


def block_at(place_ref, index):
    return pl.ds(pl.multiple_of(place_ref[index] * 128, 128), 128)


def prepare_kernel(place_ref, tok_ref, dy_ref, gain_ref, h1_ref, tok_out, dy_out):
    total = jnp.zeros((128, 128), f32)
    for r in range(16):
        part = tok_ref[:, r * 128 : (r + 1) * 128].astype(f32)
        total = total + part * part
    inverse = lax.rsqrt(jnp.sum(total, axis=1, keepdims=True) / 2048.0 + norm_eps)
    for r in range(16):
        here = slice(r * 128, (r + 1) * 128)
        there = block_at(place_ref, r)
        part = tok_ref[:, there]
        tok_out[:, here] = part
        dy_out[:, here] = dy_ref[:, there]
        h1_ref[:, here] = (part.astype(f32) * inverse * gain_ref[:, here]).astype(bf16)


def prepare(place, tok, dy, gain):
    out = jax.ShapeDtypeStruct((128, 2048), bf16)
    return pl.pallas_call(
        prepare_kernel,
        out_shape=(out, out, out),
        in_specs=[smem_spec(), vmem_spec(), vmem_spec(), vmem_spec()],
        out_specs=(vmem_spec(),) * 3,
        compiler_params=params(),
        name="prepare",
    )(place, tok, dy, gain)


def restore_kernel(place_ref, in_ref, out_ref):
    for r in range(16):
        out_ref[:, block_at(place_ref, r)] = in_ref[:, r * 128 : (r + 1) * 128]


def restore(place, value):
    return pl.pallas_call(
        restore_kernel,
        out_shape=jax.ShapeDtypeStruct(value.shape, value.dtype),
        in_specs=[smem_spec(), vmem_spec()],
        out_specs=vmem_spec(),
        compiler_params=params(),
        name="restore",
    )(place, value)


def dot_nt(left, right):
    return lax.dot_general(left, right, (((1,), (1,)), ((), ())), preferred_element_type=f32)


def dot_nn(left, right):
    return lax.dot_general(left, right, (((1,), (0,)), ((), ())), preferred_element_type=f32)


def dot_tn(left, right):
    return lax.dot_general(left, right, (((0,), (0,)), ((), ())), preferred_element_type=f32)


def qkv_kernel(a0, a1, a2, a3, mine_ref, theirs_ref, cos_ref, sin_ref, out_ref, rows_ref):
    step = pl.program_id(0) * 3 + pl.program_id(1)
    kind = pl.program_id(1)

    @pl.when(step == 0)
    def _():
        for j, ref in enumerate((a0, a1, a2, a3)):
            rows_ref[j * 128 : (j + 1) * 128, :] = ref[...]

    pre = dot_nt(rows_ref[:, :1024], mine_ref[0]) + dot_nt(rows_ref[:, 1024:], theirs_ref[0])

    def store(turned):
        for j in range(4):
            for h in range(2):
                tile = pre[j * 128 : (j + 1) * 128, h * 128 : (h + 1) * 128]
                if turned:
                    tile = tile * cos_ref[...] + pltpu.roll(tile, 64, 1) * sin_ref[...]
                out_ref[j, 0, h, 0] = tile.astype(bf16)

    @pl.when(kind < 2)
    def _():
        store(True)

    @pl.when(kind == 2)
    def _():
        store(False)


def project_qkv(rows, mine, theirs, cosine, sine):
    whole = pl.BlockSpec((128, 2048), lambda s, t: (0, 0))
    weight = pl.BlockSpec((1, 256, 1024), lambda s, t: (s, t, 0))
    table = pl.BlockSpec((128, 128), lambda s, t: (0, 0))
    return pl.pallas_call(
        qkv_kernel,
        grid=(2, 3),
        out_shape=jax.ShapeDtypeStruct((4, 2, 2, 3, 128, 128), bf16),
        in_specs=[whole] * 4 + [weight] * 2 + [table] * 2,
        out_specs=pl.BlockSpec((4, 1, 2, 1, 128, 128), lambda s, t: (0, s, 0, t, 0, 0)),
        scratch_shapes=[pltpu.VMEM((512, 2048), bf16)],
        compiler_params=params(),
        cost_estimate=pl.CostEstimate(
            flops=2 * 512 * 2048 * 1536, bytes_accessed=10 << 20, transcendentals=0
        ),
        name="project_qkv",
    )(*rows, mine, theirs, cosine, sine)


def visible_end(ends_ref, first):
    places = first + lax.broadcasted_iota(jnp.int32, (1, TILE), 1)
    end = jnp.full((1, TILE), SEQ, jnp.int32)
    for j in range(10, -1, -1):
        end = jnp.where(places < ends_ref[j], ends_ref[j], end)
    return end


def key_blocks(i):
    return min(i + 2, SEQ // TILE)


def rows_of(ref, kind, i):
    return ref[2 * i : 2 * i + 2, kind].reshape(TILE, HEAD_DIM)


def masked(scores, end, kb):
    places = kb * TILE + lax.broadcasted_iota(jnp.int32, (TILE, TILE), 0)
    return jnp.where(places < end, scores, masked_score)


def attend_kernel(ends_ref, qkv_ref, low_ref, out_ref, lse_ref, score_ref, value_ref):
    for i in range(SEQ // TILE):
        value_ref[:, i * TILE : (i + 1) * TILE] = rows_of(qkv_ref, 2, i).astype(f32).T.astype(bf16)
    for i in range(SEQ // TILE):
        query = rows_of(qkv_ref, 0, i)
        end = visible_end(ends_ref, i * TILE)
        top = jnp.full((8, TILE), masked_score, f32)
        for kb in range(key_blocks(i)):
            scores = dot_nt(rows_of(qkv_ref, 1, kb), query) * (score_scale * log2_e)
            if kb >= i:
                scores = masked(scores, end, kb)
            score_ref[kb * TILE : (kb + 1) * TILE, :] = scores
            top = jnp.maximum(top, jnp.max(scores.reshape(TILE // 8, 8, TILE), axis=0))
        top = jnp.max(top, axis=0, keepdims=True)
        total = jnp.zeros((8, TILE), f32)
        acc = jnp.zeros((HEAD_DIM, TILE), f32)
        for kb in range(key_blocks(i)):
            weights = jnp.exp2(score_ref[kb * TILE : (kb + 1) * TILE, :] - top)
            total = total + jnp.sum(weights.reshape(TILE // 8, 8, TILE), axis=0)
            acc = acc + dot_nn(value_ref[:, kb * TILE : (kb + 1) * TILE], weights.astype(bf16))
        total = jnp.sum(total, axis=0, keepdims=True)
        attended = (acc / total).T
        out_ref[i * TILE : (i + 1) * TILE, :] = attended
        low_ref[2 * i : 2 * i + 2] = attended.astype(bf16).reshape(2, 128, HEAD_DIM)
        lse_ref[:, i * TILE : (i + 1) * TILE] = top + jnp.log2(total)


def attend(ends, qkv):
    return pl.pallas_call(
        attend_kernel,
        out_shape=(
            jax.ShapeDtypeStruct((16, 128, HEAD_DIM), bf16),
            jax.ShapeDtypeStruct((SEQ, HEAD_DIM), f32),
            jax.ShapeDtypeStruct((1, SEQ), f32),
        ),
        in_specs=[smem_spec(), vmem_spec()],
        out_specs=(vmem_spec(),) * 3,
        scratch_shapes=[pltpu.VMEM((SEQ, TILE), f32), pltpu.VMEM((HEAD_DIM, SEQ), bf16)],
        compiler_params=params(),
        cost_estimate=pl.CostEstimate(
            flops=4 * 2048 * 2048 * 128, bytes_accessed=4 << 20, transcendentals=2 << 20
        ),
        name="attend",
    )(ends, qkv)


def attend_back_kernel(
    ends_ref, qkv_ref, grad_ref, out_ref, lse_ref, cos_ref, sin_ref, dqkv_ref, dk_ref, dv_ref
):
    dk_ref[...] = jnp.zeros_like(dk_ref)
    dv_ref[...] = jnp.zeros_like(dv_ref)

    def turn_back(gradient, i):
        here = slice(i * TILE, (i + 1) * TILE)
        gradient = gradient * score_scale
        turned = gradient * cos_ref[here, :] - pltpu.roll(gradient, 64, 1) * sin_ref[here, :]
        return turned.astype(bf16).reshape(2, 128, HEAD_DIM)

    for i in range(SEQ // TILE):
        here = slice(i * TILE, (i + 1) * TILE)
        query = rows_of(qkv_ref, 0, i)
        grad = grad_ref[2 * i : 2 * i + 2].reshape(TILE, HEAD_DIM)
        product = jnp.sum(grad.astype(f32) * out_ref[here, :], axis=1, keepdims=True)
        delta = jnp.broadcast_to(product, (TILE, 128)).T[0:1, :]
        lse = lse_ref[:, here]
        end = visible_end(ends_ref, i * TILE)
        dq = jnp.zeros((TILE, HEAD_DIM), f32)
        for kb in range(key_blocks(i)):
            there = slice(kb * TILE, (kb + 1) * TILE)
            key = rows_of(qkv_ref, 1, kb)
            scores = dot_nt(key, query) * (score_scale * log2_e)
            if kb >= i:
                scores = masked(scores, end, kb)
            probs = jnp.exp2(scores - lse)
            dv_ref[there, :] += dot_nn(probs.astype(bf16), grad)
            dprobs = dot_nt(rows_of(qkv_ref, 2, kb), grad)
            dscores = (probs * (dprobs - delta)).astype(bf16)
            dk_ref[there, :] += dot_nn(dscores, query)
            dq = dq + dot_tn(dscores, key)
        dqkv_ref[2 * i : 2 * i + 2, 0] = turn_back(dq, i)
    for i in range(SEQ // TILE):
        here = slice(i * TILE, (i + 1) * TILE)
        dqkv_ref[2 * i : 2 * i + 2, 1] = turn_back(dk_ref[here, :], i)
        dqkv_ref[2 * i : 2 * i + 2, 2] = dv_ref[here, :].astype(bf16).reshape(2, 128, HEAD_DIM)


def attend_back(ends, qkv, grad, out, lse, cosine, sine):
    return pl.pallas_call(
        attend_back_kernel,
        out_shape=jax.ShapeDtypeStruct((16, 3, 128, HEAD_DIM), bf16),
        in_specs=[smem_spec()] + [vmem_spec()] * 6,
        out_specs=vmem_spec(),
        scratch_shapes=[pltpu.VMEM((SEQ, HEAD_DIM), f32), pltpu.VMEM((SEQ, HEAD_DIM), f32)],
        compiler_params=params(),
        cost_estimate=pl.CostEstimate(
            flops=10 * 2048 * 2048 * 128, bytes_accessed=8 << 20, transcendentals=2 << 20
        ),
        name="attend_back",
    )(ends, qkv, grad, out, lse, cosine, sine)


def gather_weight(shard):
    along_z = jnp.concatenate(gather4(shard, "z"), axis=1)
    own, near1, far, near3 = gather4(along_z, "y")
    mine = jnp.stack(
        [jnp.concatenate([own, far], axis=1), jnp.concatenate([near1, near3], axis=1)], axis=0
    )
    return mine, swap(mine, "c", 1)


def scatter_weight(grad):
    got = swap(grad[:, :, 1024:], "c", 1)
    mine = (grad[:, :, :1024].astype(f32) + got.astype(f32)).astype(bf16)
    along_y = scatter4(
        [mine[0, :, :512], mine[1, :, :512], mine[0, :, 512:], mine[1, :, 512:]], "y"
    ).astype(bf16)
    return scatter4([along_y[:, b * 128 : (b + 1) * 128] for b in range(4)], "z")


def rotary(count):
    places = jnp.arange(count, dtype=jnp.int32).astype(f32)
    within = jnp.arange(HEAD_DIM, dtype=jnp.int32) % (HEAD_DIM // 2)
    inverse_freq = 10000.0 ** (within.astype(f32) * (-2.0 / HEAD_DIM))
    angles = places[:, None] * inverse_freq[None, :]
    sign = jnp.where(jnp.arange(HEAD_DIM) < HEAD_DIM // 2, -1.0, 1.0).astype(f32)
    return jnp.cos(angles), jnp.sin(angles) * sign


def inverse_rms(values):
    return lax.rsqrt(jnp.mean(values * values, axis=-1, keepdims=True) + norm_eps)


def norm_back(grad_normed, values, inverse, gain):
    scaled = grad_normed * gain
    gain_part = jnp.sum(grad_normed * values * inverse, axis=0)
    inner = jnp.mean(scaled * values, axis=-1, keepdims=True)
    return inverse * scaled - values * inverse**3 * inner, gain_part


def on_device(
    tokens,
    block_lengths,
    attn_gain,
    query_weight,
    key_weight,
    value_weight,
    out_weight,
    mlp_gain,
    gate_weight,
    up_weight,
    down_weight,
    output_grad,
):
    x, yl, yh, z, c = (lax.axis_index(name) for name in ("x", "yl", "yh", "z", "c"))
    blk = (yh * 4 + z) * 2 + c
    rel = jnp.arange(16, dtype=jnp.int32)
    place = ((yh ^ ((rel >> 2) & 1)) * 4 + (z ^ (rel & 3))) * 2 + (c ^ (rel >> 3))
    chosen = place[:, None] == rel[None, :]

    def relative(gain):
        return jnp.sum(jnp.where(chosen[:, :, None], gain.reshape(1, 16, 128), 0.0), axis=1)

    def absolute(gain):
        return jnp.sum(jnp.where(chosen[:, :, None], gain.reshape(16, 1, 128), 0.0), axis=0)

    first_gain = relative(attn_gain).reshape(1, 2048)
    second_gain = relative(mlp_gain).reshape(1, 2048)
    cosine, sine = rotary(SEQ)
    own_cosine = lax.dynamic_slice_in_dim(cosine, blk * 128, 128, 0)
    own_sine = lax.dynamic_slice_in_dim(sine, blk * 128, 128, 0)
    sequence = (x ^ (blk >> 2)) * 2 + yl
    ends = jnp.cumsum(lax.dynamic_slice_in_dim(block_lengths, sequence, 1, 0)[0])

    normed1, tok, dy = prepare(place, tokens[0], output_grad[0], first_gain)
    tok = tok.astype(f32)
    rows1 = gather4(normed1, "x")
    shard1 = jnp.concatenate([query_weight.T, key_weight.T, value_weight.T], axis=0)
    mine1, theirs1 = gather_weight(shard1)
    shard2 = jnp.concatenate([out_weight, gate_weight.T, up_weight.T, down_weight], axis=0)
    mine2, theirs2 = gather_weight(shard2)
    weight1 = jnp.concatenate([mine1, theirs1], axis=2)
    weight2 = jnp.concatenate([mine2, theirs2], axis=2)
    w_out, w_gate, w_up, w_down = (
        weight2[:, :256],
        weight2[:, 256:944],
        weight2[:, 944:1632],
        weight2[:, 1632:],
    )

    blkaxes = ("yh", "z", "c")
    qkv_own = project_qkv(rows1, mine1, theirs1, own_cosine, own_sine)
    qkv = lax.all_to_all(
        qkv_own.reshape(16, 3, 128, 128), blkaxes, split_axis=0, concat_axis=0, tiled=True
    )
    low, attended, lse = attend(ends, qkv)
    low = lax.all_to_all(low, blkaxes, split_axis=0, concat_axis=0, tiled=True)
    low = low.reshape(4, 2, 2, 128, 128)
    part = jnp.einsum(
        "jshrk,shkd->jrd", low, w_out.reshape(2, 2, 128, 2048), preferred_element_type=f32
    ).astype(bf16)
    residual = tok + scatter4(list(part), "x")
    inverse2 = inverse_rms(residual)
    normed2 = (residual * inverse2 * second_gain).astype(bf16)

    dy_rows = jnp.concatenate(gather4(dy, "x"), axis=0)
    rows2 = jnp.concatenate(gather4(normed2, "x"), axis=0)
    gate = jnp.einsum("md,srd->smr", rows2, w_gate, preferred_element_type=f32)
    up = jnp.einsum("md,srd->smr", rows2, w_up, preferred_element_type=f32)
    sigmoid = jax.nn.sigmoid(gate)
    silu = gate * sigmoid
    hidden = (silu * up).astype(bf16)
    d_hidden = jnp.einsum("md,srd->smr", dy_rows, w_down, preferred_element_type=f32)
    d_gate = (d_hidden * up * sigmoid * (1.0 + gate * (1.0 - sigmoid))).astype(bf16)
    d_up = (d_hidden * silu).astype(bf16)
    part = (
        jnp.einsum("smr,srd->md", d_gate, w_gate, preferred_element_type=f32)
        + jnp.einsum("smr,srd->md", d_up, w_up, preferred_element_type=f32)
    ).astype(bf16)
    d_normed2 = scatter4(list(part.reshape(4, 128, 2048)), "x")
    back2, second_part = norm_back(d_normed2, residual, inverse2, second_gain)
    d_residual = dy.astype(f32) + back2
    d_attn = d_residual.astype(bf16)
    rows3 = jnp.concatenate(gather4(d_attn, "x"), axis=0)

    part = jnp.einsum("smr,srd->md", hidden, w_down, preferred_element_type=f32).astype(bf16)
    output = (residual + scatter4(list(part.reshape(4, 128, 2048)), "x")).astype(bf16)
    layer_output = restore(place, output)[None]

    d_out = jnp.einsum(
        "jrd,shkd->jshrk",
        rows3.reshape(4, 128, 2048),
        w_out.reshape(2, 2, 128, 2048),
        preferred_element_type=f32,
    ).astype(bf16)
    d_out = lax.all_to_all(
        d_out.reshape(16, 128, 128), blkaxes, split_axis=0, concat_axis=0, tiled=True
    )
    dqkv = attend_back(ends, qkv, d_out, attended, lse, cosine, sine)

    grad_gate = jnp.einsum("smr,md->srd", d_gate, rows2, preferred_element_type=f32).astype(bf16)
    grad_up = jnp.einsum("smr,md->srd", d_up, rows2, preferred_element_type=f32).astype(bf16)
    grad_down = jnp.einsum("smr,md->srd", hidden, dy_rows, preferred_element_type=f32).astype(bf16)
    grad_out = (
        jnp.einsum(
            "jshrk,jrd->shkd", low, rows3.reshape(4, 128, 2048), preferred_element_type=f32
        )
        .astype(bf16)
        .reshape(2, 256, 2048)
    )
    grads2 = scatter_weight(jnp.concatenate([grad_out, grad_gate, grad_up, grad_down], axis=1))

    dqkv = lax.all_to_all(dqkv, blkaxes, split_axis=0, concat_axis=0, tiled=True)
    dqkv = dqkv.reshape(4, 2, 2, 3, 128, 128)
    part = jnp.einsum(
        "jshtrk,sthkd->jrd",
        dqkv,
        weight1.reshape(2, 3, 2, 128, 2048),
        preferred_element_type=f32,
    ).astype(bf16)
    d_normed1 = scatter4(list(part), "x")
    rows1_all = jnp.stack(rows1, axis=0)
    grad1 = (
        jnp.einsum("jshtrk,jrd->sthkd", dqkv, rows1_all, preferred_element_type=f32)
        .astype(bf16)
        .reshape(2, 768, 2048)
    )
    grads1 = scatter_weight(grad1)
    back1, first_part = norm_back(d_normed1, tok, inverse_rms(tok), first_gain)
    input_grad = restore(place, d_residual + back1)[None]

    gains = jnp.concatenate([absolute(first_part), absolute(second_part)], axis=0)
    for axis in ("x", "y", "z"):
        gains = total4(gains, axis)
    gains = gains + swap(gains, "c", 1)
    return (
        layer_output,
        input_grad,
        gains[:16].reshape(2048),
        grads1[:256].T,
        grads1[256:512].T,
        grads1[512:].T,
        grads2[:256],
        gains[16:].reshape(2048),
        grads2[256:944].T,
        grads2[944:1632].T,
        grads2[1632:],
    )


def solution(mesh):
    fine = Mesh(mesh.devices.reshape(4, 2, 2, 4, 2), ("x", "yl", "yh", "z", "c"))
    head, blk = ("x", "yl"), ("yh", "z", "c")
    rows = P(head, blk, None)
    wide, tall = P(blk, head), P(head, blk)
    return jax.shard_map(
        on_device,
        mesh=fine,
        in_specs=(rows, P(), P(), wide, wide, wide, tall, P(), wide, wide, tall, rows),
        out_specs=(rows, rows, P(), wide, wide, wide, tall, P(), wide, wide, tall),
        check_vma=False,
    )
```

time: 2210 us -> 791 us (0.36)
  waiting for transfers between devices: 1670 us -> 390 us
  matrix products: 219 us -> 59.4 us
  starting transfers between devices: 7.08 us -> 118 us
  blocking collectives: 82 us -> 18.1 us
  local copies, waits for them, and re-layouts: 92.2 us -> 32.5 us
  Pallas kernels: 0 us -> 39.3 us
    all_gather x11 -> x0, waiting for transfers between devices: 590 us -> none  [the longest x4 325 us: head_rows(): return lax.all_gather(values, 'head', axis=0, tiled=True)]
    reduce_scatter x7 -> x0, waiting for transfers between devices: 487 us -> none  [the longest x4 281 us: head_total(): lax.psum_scatter(term_fn(jnp.int32(0), row_total * lax.axis_size('head'))...]
    ppermute x92 -> x78, waiting for transfers between devices: 579 us -> 339 us  [swap(): return lax.ppermute(value, names, [(i, i ^ step) for i in range(count)])]
    dot_general x133 -> x14, matrix products: 219 us -> 59.4 us  [the longest x1 7.02 us: on_device(): jnp.einsum('md,srd->smr', dy_rows, w_down, preferred_element_type=f32)]
    ppermute x92 -> x78, starting transfers between devices: 5.1 us -> 105 us  [swap(): return lax.ppermute(value, names, [(i, i ^ step) for i in range(count)])]
    psum x1 -> x0, blocking collectives: 82 us -> none  [on_device(): gain_sums = lax.psum((first_gain, second_gain), ('head', 'blk'))]
    concatenate x0 -> x24, other arithmetic: none -> 68.3 us  [the longest x1 35.1 us: on_device(): jnp.concatenate([grad_out, grad_gate, grad_up, grad_down], axis=1)]
    convert_element_type x41 -> x15, other arithmetic: 81.3 us -> 17.4 us  [the longest x2 9.62 us: scatter_weight(): mine = (grad[:, :, :1024].astype(f32) + got.astype(f32)).astype(bf16)]
  transfers between devices with their start and end apart: 114 -> 81, of which waited for: 110 -> 55; matrix products, arithmetic and copies ran while one was open for 18% -> 14% of each run, Pallas kernels for 0% -> 5%
where the time goes in v1:
time: 791 us; the launch traced here: 780 us
  waiting for transfers between devices  390 us (49%)
  other arithmetic  121 us (15%)
  starting transfers between devices  118 us (15%)
  matrix products  59.4 us (8%)
  Pallas kernels  39.3 us (5%)
  local copies, waits for them, and re-layouts  32.5 us (4%)
  blocking collectives  18.1 us (2%)
    ppermute x78, waiting for transfers between devices, swap(): return lax.ppermute(value, names, [(i, i ^ step) for i in range(count)])  339 us
    ppermute x78, starting transfers between devices, swap(): return lax.ppermute(value, names, [(i, i ^ step) for i in range(count)])  105 us
    concatenate x1, other arithmetic, on_device(): jnp.concatenate([grad_out, grad_gate, grad_up, grad_down], axis=1)  35.1 us
    all_to_all x1, waiting for transfers between devices, on_device(): lax.all_to_all(qkv_own.reshape(16, 3, 128, 128), blkaxes, split_axis=0, c...  23 us
    all_to_all x1, waiting for transfers between devices, on_device(): lax.all_to_all(dqkv, blkaxes, split_axis=0, concat_axis=0, tiled=True)  18.7 us
    all_to_all x1, blocking collectives, on_device(): lax.all_to_all(d_out.reshape(16, 128, 128), blkaxes, split_axis=0, concat...  18.1 us
  transfers between devices with their start and end apart: 81, of which 55 were waited for; matrix products, arithmetic and copies ran while one was open for 14% of the time, Pallas kernels for 5%

profile of v1, /device:TPU:8, one launch (start us, length us, event | category | flops | bytes accessed | tf_op | source)
XLA Modules:
  0.0 780.2 jit_solution(17468426511082015304)
XLA Ops:
  6.9 13.4 %collective-permute-done.14 = bf16[2320,128]{1,0:T(8,128)(2,1)S(1)} collective-permute-done((bf16[2320,128]{1,0:T(8,128)(2,1)S(1)}, bf16[2320,128]{1,0:T(8,128)(2,1)S(1)}, u32[]{:S(2)}, u32[]{:S(2)}) %collective-permute-start.14) | collective-permute-done | bytes 593952 | tf_op jit(solution)/shard_map/ppermute | solution.py:30
  23.5 7.1 collective-permute-done.16
  30.7 7.9 %pad_maximum_fusion.8 = bf16[2320,512]{1,0:T(8,128)(2,1)S(1)} fusion(bf16[2320,128]{1,0:T(8,128)(2,1)S(1)} %collective-permute-done.14, bf16[1152,128]{1,0:T(8,128)(2,1)S(1)} %collective-permute-done.16, bf16[1168,128]{1,0:T(8,128)(2,1)S(1)} %collective-permute-done.15, bf16[2320,128]{1,0:T(8,128)(2,1)S(1)} %collective-permute-done.13, ...), kind=kLoop, calls=%fused_computation.45 | loop fusion | flops 19005440 | bytes 4751360 | tf_op jit(solution)/shard_map/concatenate | solution.py:305
  42.5 47.4 %collective-permute-done.19 = bf16[2320,512]{1,0:T(8,128)(2,1)S(1)} collective-permute-done((bf16[2320,512]{1,0:T(8,128)(2,1)S(1)}, bf16[2320,512]{1,0:T(8,128)(2,1)S(1)}, u32[]{:S(2)}, u32[]{:S(2)}) %collective-permute-start.19) | collective-permute-done | bytes 2375712 | tf_op jit(solution)/shard_map/ppermute | solution.py:30
  99.9 16.2 %collective-permute-done.20 = bf16[1152,512]{1,0:T(8,128)(2,1)S(1)} collective-permute-done((bf16[1152,512]{1,0:T(8,128)(2,1)S(1)}, bf16[1152,512]{1,0:T(8,128)(2,1)S(1)}, u32[]{:S(2)}, u32[]{:S(2)}) %collective-permute-start.20) | collective-permute-done | bytes 1179680 | tf_op jit(solution)/shard_map/ppermute | solution.py:30
  118.4 8.2 %pad_maximum_fusion.1 = bf16[2,2320,1024]{2,1,0:T(8,128)(2,1)} fusion(bf16[1,2320,1024]{2,1,0:T(8,128)(2,1)} %maximum_bitcast_fusion, bf16[1,2320,1024]{2,1,0:T(8,128)(2,1)} %bitcast.15), kind=kLoop, calls=%fused_computation.3 | loop fusion | flops 4751360 | bytes 19005440 | tf_op jit(solution)/shard_map/stack | solution.py:307
  129.8 4.6 collective-permute-done.4
  144.8 15.3 %collective-permute-done.10 = bf16[768,512]{1,0:T(8,128)(2,1)S(1)} collective-permute-done((bf16[768,512]{1,0:T(8,128)(2,1)S(1)}, bf16[768,512]{1,0:T(8,128)(2,1)S(1)}, u32[]{:S(2)}, u32[]{:S(2)}) %collective-permute-start.10) | collective-permute-done | bytes 786464 | tf_op jit(solution)/shard_map/ppermute | solution.py:30
  164.2 5.7 collective-permute-done.11
  179.2 12.7 %collective-permute-done.1.a3 = bf16[128,2048]{1,0:T(8,128)(2,1)S(1)} collective-permute-done((bf16[128,2048]{1,0:T(8,128)(2,1)}, bf16[128,2048]{1,0:T(8,128)(2,1)S(1)}, u32[]{:S(2)}, u32[]{:S(2)}) %collective-permute-start.1) | collective-permute-done | bytes 524320 | tf_op jit(solution)/shard_map/ppermute | solution.py:30
  193.7 5.5 fusion.40
  204.4 4.9 collective-permute-done.3
  210.1 9.0 %project_qkv.1 = bf16[4,2,2,3,128,128]{5,4,3,2,1,0:T(8,128)(2,1)} custom-call(bf16[128,2048]{1,0:T(8,128)(2,1)} %get-tuple-element.18.a0, bf16[128,2048]{1,0:T(8,128)(2,1)} %collective-permute-done.a1, bf16[128,2048]{1,0:T(8,128)(2,1)} %copy-done.28, bf16[128,2048]{1,0:T(8,128)(2,1)} %copy-done.27, bf16[2,768,1024]{2,1,0:T(8,128)(2,1)} %pad_maximum_fusion.7.mine_ref, ...), custom_call_target="tpu_custom_call" | custom-call | flops 3221225472 | bytes 10485760 | tf_op jit(solution)/shard_map/project_qkv/pallas_call | solution.py:167
  219.1 4.4 all-to-all-start
  224.2 23.0 %all-to-all-done.qkv_ref = bf16[16,3,128,128]{3,2,1,0:T(8,128)(2,1)} async-done(((bf16[16,3,128,128]{3,2,1,0:T(8,128)(2,1)}), bf16[16,3,128,128]{3,2,1,0:T(8,128)(2,1)}, u32[]{:S(2)}, u32[]{:S(2)}) %all-to-all-start) | async-done | bytes 1572896 | tf_op jit(solution)/shard_map/all_to_all | solution.py:394
  247.2 7.8 attend.1
  262.4 9.2 %all-to-all-done.1 = bf16[16,128,128]{2,1,0:T(8,128)(2,1)} async-done(((bf16[16,128,128]{2,1,0:T(8,128)(2,1)}), bf16[16,128,128]{2,1,0:T(8,128)(2,1)}, u32[]{:S(2)}, u32[]{:S(2)}) %all-to-all-start.1) | async-done | bytes 524320 | tf_op jit(solution)/shard_map/all_to_all | solution.py:398
  280.2 5.2 collective-permute-done.22
  288.5 8.1 %collective-permute-done.35 = bf16[128,2048]{1,0:T(8,128)(2,1)S(1)} collective-permute-done((bf16[128,2048]{1,0:T(8,128)(2,1)S(1)}, bf16[128,2048]{1,0:T(8,128)(2,1)S(1)}, u32[]{:S(2)}, u32[]{:S(2)}) %collective-permute-start.35) | collective-permute-done | bytes 524320 | tf_op jit(solution)/shard_map/ppermute | solution.py:30
  299.5 8.3 %collective-permute-done.25 = bf16[128,2048]{1,0:T(8,128)(2,1)S(1)} collective-permute-done((bf16[128,2048]{1,0:T(8,128)(2,1)S(1)}, bf16[128,2048]{1,0:T(8,128)(2,1)S(1)}, u32[]{:S(2)}, u32[]{:S(2)}) %collective-permute-start.25) | collective-permute-done | bytes 524320 | tf_op jit(solution)/shard_map/ppermute | solution.py:30
  313.4 9.6 %collective-permute-done.27 = bf16[128,2048]{1,0:T(8,128)(2,1)S(1)} collective-permute-done((bf16[128,2048]{1,0:T(8,128)(2,1)S(1)}, bf16[128,2048]{1,0:T(8,128)(2,1)S(1)}, u32[]{:S(2)}, u32[]{:S(2)}) %collective-permute-start.27) | collective-permute-done | bytes 524320 | tf_op jit(solution)/shard_map/ppermute | solution.py:30
  323.1 12.1 %pad_maximum_fusion.3 = (bf16[2,688,2048]{2,1,0:T(8,128)(2,1)}, bf16[2,688,2048]{2,1,0:T(8,128)(2,1)S(1)}, bf16[2,688,2048]{2,1,0:T(8,128)(2,1)S(1)}) fusion(bf16[2,2320,1024]{2,1,0:T(8,128)(2,1)} %collective-permute-done.21, bf16[1,2320,1024]{2,1,0:T(8,128)(2,1)S(1)} %bitcast.281, bf16[1,2320,1024]{2,1,0:T(8,128)(2,1)} %bitcast.15), kind=kLoop, calls=%fused_computation.9 | loop fusion | flops 50724864 | bytes 35913728 | tf_op jit(solution)/shard_map/concatenate | solution.py:384
  335.3 11.5 %collective-permute-start.29 = (bf16[64,2048]{1,0:T(8,128)(2,1)S(1)}, bf16[64,2048]{1,0:T(8,128)(2,1)S(1)}, u32[]{:S(2)}, u32[]{:S(2)}) collective-permute-start(bf16[64,2048]{1,0:T(8,128)(2,1)S(1)} %slice.503), channel_id=1, source_target_pairs={{0,96},{32,64},{64,32},{96,0},{1,97},{33,65},{65,33},{97,1},{2,98}... | collective-permute-start | bytes 786440 | tf_op jit(solution)/shard_map/ppermute | solution.py:30
  353.4 6.4 fusion.34
  359.8 4.7 fusion.32
  364.5 7.0 fusion.11
  402.5 4.9 collective-permute-done.41
  407.6 7.0 collective-permute-done.33
  423.4 7.0 collective-permute-done.43
  439.6 5.3 collective-permute-done.45
  447.9 35.1 %pad_maximum_fusion = bf16[2,2320,2048]{2,1,0:T(8,128)(2,1)} fusion(bf16[2,688,2048]{2,1,0:T(8,128)(2,1)S(1)} %convolution_convert_fusion, bf16[2,688,2048]{2,1,0:T(8,128)(2,1)S(1)} %convolution_convert_fusion.1, bf16[2,688,2048]{2,1,0:T(8,128)(2,1)S(1)} %convolution_convert_fusion.2, bf16[2,256,2048]{2,1,0:T(8,128)(2,1)S(1)} %bitcast.284), kind=kLoop, calls=%fused_computation | loop fusion | flops 76021760 | bytes 38010880 | tf_op jit(solution)/shard_map/concatenate | solution.py:452
  483.0 8.4 %slice.547 = bf16[2,2320,1024]{2,1,0:T(8,128)(2,1)} slice(bf16[2,2320,2048]{2,1,0:T(8,128)(2,1)} %pad_maximum_fusion), slice={[0:2], [0:2320], [1024:2048]} | slice | bytes 19005440 | tf_op jit(solution)/shard_map/slice | solution.py:314
  491.5 4.3 fusion.39
  497.8 18.1 %all_to_all.20.grad_ref = bf16[16,128,128]{2,1,0:T(8,128)(2,1)} all-to-all(bf16[16,128,128]{2,1,0:T(8,128)(2,1)} %bitcast.294), channel_id=1, replica_groups=mesh['x'=4,'yl'=2,'yh'=2,'z'=4,'c'=2] {'yh','z','c'}, dimensions={0} | all-to-all | bytes 1048576 | tf_op jit(solution)/shard_map/all_to_all | solution.py:437
  516.0 15.5 %attend_back.1 = bf16[16,3,128,128]{3,2,1,0:T(8,128)(2,1)} custom-call(s32[12]{0:T(128)} %bitcast.324, bf16[16,3,128,128]{3,2,1,0:T(8,128)(2,1)} %all-to-all-done.qkv_ref, bf16[16,128,128]{2,1,0:T(8,128)(2,1)} %all_to_all.20.grad_ref, f32[2048,128]{1,0:T(8,128)} %get-tuple-element.21.out_ref, f32[1,2048]{1,0:T(1,128)} %get-tuple-element.22.lse_ref, ...), custom_call_target="tpu_custom_call" | custom-call | flops 5368709120 | bytes 8388608 | tf_op jit(solution)/shard_map/attend_back/pallas_call | solution.py:290
  531.4 4.6 all-to-all-start.3
  536.1 5.0 pad_maximum_fusion.2
  541.1 18.7 %all-to-all-done.3 = bf16[16,3,128,128]{3,2,1,0:T(8,128)(2,1)} async-done(((bf16[16,3,128,128]{3,2,1,0:T(8,128)(2,1)}), bf16[16,3,128,128]{3,2,1,0:T(8,128)(2,1)}, u32[]{:S(2)}, u32[]{:S(2)}) %all-to-all-start.3) | async-done | bytes 1572896 | tf_op jit(solution)/shard_map/all_to_all | solution.py:454
  559.8 5.5 fusion
  568.7 5.1 bitcast_convert_fusion.2
  575.7 7.3 collective-permute-done.46
  585.2 11.8 %collective-permute-done.49 = bf16[128,2048]{1,0:T(8,128)(2,1)S(1)} collective-permute-done((bf16[128,2048]{1,0:T(8,128)(2,1)S(1)}, bf16[128,2048]{1,0:T(8,128)(2,1)S(1)}, u32[]{:S(2)}, u32[]{:S(2)}) %collective-permute-start.49) | collective-permute-done | bytes 524320 | tf_op jit(solution)/shard_map/ppermute | solution.py:30
  603.4 6.5 add_convert_fusion
  619.6 17.1 %collective-permute-done.70 = bf16[1152,512]{1,0:T(8,128)(2,1)S(1)} collective-permute-done((bf16[1152,512]{1,0:T(8,128)(2,1)S(1)}, bf16[1152,512]{1,0:T(8,128)(2,1)S(1)}, u32[]{:S(2)}, u32[]{:S(2)}) %collective-permute-start.70) | collective-permute-done | bytes 1179680 | tf_op jit(solution)/shard_map/ppermute | solution.py:30
  649.6 59.4 %collective-permute-done.54 = f32[32,128]{1,0:T(8,128)S(1)} collective-permute-done((f32[32,128]{1,0:T(8,128)S(1)}, f32[32,128]{1,0:T(8,128)S(1)}, u32[]{:S(2)}, u32[]{:S(2)}) %collective-permute-start.54) | collective-permute-done | bytes 16416 | tf_op jit(solution)/shard_map/ppermute | solution.py:30
  722.9 4.7 collective-permute-start.58
  752.6 7.0 collective-permute-done.74
  766.1 7.8 %collective-permute-done.75 = bf16[2320,128]{1,0:T(8,128)(2,1)} collective-permute-done((bf16[2320,128]{1,0:T(8,128)(2,1)S(1)}, bf16[2320,128]{1,0:T(8,128)(2,1)}, u32[]{:S(2)}, u32[]{:S(2)}) %collective-permute-start.75) | collective-permute-done | bytes 593952 | tf_op jit(solution)/shard_map/ppermute | solution.py:30
  (366 shorter events, 236.0 us)
Async XLA Ops:
  2.9 17.4 %collective-permute-start.14 = (bf16[2320,128]{1,0:T(8,128)(2,1)S(1)}, bf16[2320,128]{1,0:T(8,128)(2,1)S(1)}, u32[]{:S(2)}, u32[]{:S(2)}) collective-permute-start(bf16[2320,128]{1,0:T(8,128)(2,1)S(1)} %get-tuple-element.126), channel_id=1, source_target_pairs={{0,6},{2,4},{4,2},{6,0},{1,7},{3,5},{5,3},{7,1},{8,14},{10,12},{12... | collective-permute-start | bytes 1781768 | tf_op jit(solution)/shard_map/ppermute | solution.py:30
  6.9 14.9 %collective-permute-start.13 = (bf16[2320,128]{1,0:T(8,128)(2,1)S(1)}, bf16[2320,128]{1,0:T(8,128)(2,1)S(1)}, u32[]{:S(2)}, u32[]{:S(2)}) collective-permute-start(bf16[2320,128]{1,0:T(8,128)(2,1)S(1)} %get-tuple-element.126), channel_id=1, source_target_pairs={{0,2},{2,0},{4,6},{6,4},{1,3},{3,1},{5,7},{7,5},{8,10},{10,8},{12,... | collective-permute-start | bytes 1781768 | tf_op jit(solution)/shard_map/ppermute | solution.py:30
  38.7 51.3 %collective-permute-start.19 = (bf16[2320,512]{1,0:T(8,128)(2,1)S(1)}, bf16[2320,512]{1,0:T(8,128)(2,1)S(1)}, u32[]{:S(2)}, u32[]{:S(2)}) collective-permute-start(bf16[2320,512]{1,0:T(8,128)(2,1)S(1)} %pad_maximum_fusion.8), channel_id=1, source_target_pairs={{0,16},{8,24},{16,0},{24,8},{1,17},{9,25},{17,1},{25,9},{2,18},{10... | collective-permute-start | bytes 7127048 | tf_op jit(solution)/shard_map/ppermute | solution.py:30
  39.2 52.8 %collective-permute-start.17 = (bf16[2320,512]{1,0:T(8,128)(2,1)S(1)}, bf16[2320,512]{1,0:T(8,128)(2,1)S(1)}, u32[]{:S(2)}, u32[]{:S(2)}) collective-permute-start(bf16[2320,512]{1,0:T(8,128)(2,1)S(1)} %pad_maximum_fusion.8), channel_id=1, source_target_pairs={{0,24},{8,16},{16,8},{24,0},{1,25},{9,17},{17,9},{25,1},{2,26},{10... | collective-permute-start | bytes 7127048 | tf_op jit(solution)/shard_map/ppermute | solution.py:30
  90.1 26.0 %collective-permute-start.20 = (bf16[1152,512]{1,0:T(8,128)(2,1)S(1)}, bf16[1152,512]{1,0:T(8,128)(2,1)S(1)}, u32[]{:S(2)}, u32[]{:S(2)}) collective-permute-start(bf16[1152,512]{1,0:T(8,128)(2,1)S(1)} %slice.495), channel_id=1, source_target_pairs={{0,24},{8,16},{16,8},{24,0},{1,25},{9,17},{17,9},{25,1},{2,26},{10... | collective-permute-start | bytes 3538952 | tf_op jit(solution)/shard_map/ppermute | solution.py:30
  92.1 24.7 %collective-permute-start.18 = (bf16[1168,512]{1,0:T(8,128)(2,1)S(1)}, bf16[1168,512]{1,0:T(8,128)(2,1)S(1)}, u32[]{:S(2)}, u32[]{:S(2)}) collective-permute-start(bf16[1168,512]{1,0:T(8,128)(2,1)S(1)} %slice.494), channel_id=1, source_target_pairs={{0,16},{8,24},{16,0},{24,8},{1,17},{9,25},{17,1},{25,9},{2,18},{10... | collective-permute-start | bytes 3588104 | tf_op jit(solution)/shard_map/ppermute | solution.py:30
  126.6 132.6 %collective-permute-start.21 = (bf16[2,2320,1024]{2,1,0:T(8,128)(2,1)}, bf16[2,2320,1024]{2,1,0:T(8,128)(2,1)}, u32[]{:S(2)}, u32[]{:S(2)}) collective-permute-start(bf16[2,2320,1024]{2,1,0:T(8,128)(2,1)} %pad_maximum_fusion.1), channel_id=1, source_target_pairs={{0,1},{1,0},{2,3},{3,2},{4,5},{5,4},{6,7},{7,6},{8,9},{9,8},{10,11... | collective-permute-start | bytes 28508168 | tf_op jit(solution)/shard_map/ppermute | solution.py:30
  141.9 18.1 %collective-permute-start.10 = (bf16[768,512]{1,0:T(8,128)(2,1)S(1)}, bf16[768,512]{1,0:T(8,128)(2,1)S(1)}, u32[]{:S(2)}, u32[]{:S(2)}) collective-permute-start(bf16[768,512]{1,0:T(8,128)(2,1)S(1)} %pad_maximum_fusion.12), channel_id=1, source_target_pairs={{0,16},{8,24},{16,0},{24,8},{1,17},{9,25},{17,1},{25,9},{2,18},{10... | collective-permute-start | bytes 2359304 | tf_op jit(solution)/shard_map/ppermute | solution.py:30
  143.7 18.8 %collective-permute-start.8 = (bf16[768,512]{1,0:T(8,128)(2,1)S(1)}, bf16[768,512]{1,0:T(8,128)(2,1)S(1)}, u32[]{:S(2)}, u32[]{:S(2)}) collective-permute-start(bf16[768,512]{1,0:T(8,128)(2,1)S(1)} %pad_maximum_fusion.12), channel_id=1, source_target_pairs={{0,24},{8,16},{16,8},{24,0},{1,25},{9,17},{17,9},{25,1},{2,26},{10... | collective-permute-start | bytes 2359304 | tf_op jit(solution)/shard_map/ppermute | solution.py:30
  172.7 36.6 %collective-permute-start.12 = (bf16[2,768,1024]{2,1,0:T(8,128)(2,1)}, bf16[2,768,1024]{2,1,0:T(8,128)(2,1)}, u32[]{:S(2)}, u32[]{:S(2)}) collective-permute-start(bf16[2,768,1024]{2,1,0:T(8,128)(2,1)} %pad_maximum_fusion.7.mine_ref), channel_id=1, source_target_pairs={{0,1},{1,0},{2,3},{3,2},{4,5},{5,4},{6,7},{7,6},{8,9},{9,8},{10,11... | collective-permute-start | bytes 9437192 | tf_op jit(solution)/shard_map/ppermute | solution.py:30
  176.2 15.7 %collective-permute-start.1 = (bf16[128,2048]{1,0:T(8,128)(2,1)}, bf16[128,2048]{1,0:T(8,128)(2,1)S(1)}, u32[]{:S(2)}, u32[]{:S(2)}) collective-permute-start(bf16[128,2048]{1,0:T(8,128)(2,1)} %get-tuple-element.18.a0), channel_id=1, source_target_pairs={{0,96},{32,64},{64,32},{96,0},{1,97},{33,65},{65,33},{97,1},{2,98}... | collective-permute-start | bytes 1572872 | tf_op jit(solution)/shard_map/ppermute | solution.py:30
  179.0 20.3 %collective-permute-start = (bf16[128,2048]{1,0:T(8,128)(2,1)}, bf16[128,2048]{1,0:T(8,128)(2,1)}, u32[]{:S(2)}, u32[]{:S(2)}) collective-permute-start(bf16[128,2048]{1,0:T(8,128)(2,1)} %get-tuple-element.18.a0), channel_id=1, source_target_pairs={{0,32},{32,0},{64,96},{96,64},{1,33},{33,1},{65,97},{97,65},{2,34}... | collective-permute-start | bytes 1572872 | tf_op jit(solution)/shard_map/ppermute | solution.py:30
  219.1 28.1 %all-to-all-start = ((bf16[16,3,128,128]{3,2,1,0:T(8,128)(2,1)}), bf16[16,3,128,128]{3,2,1,0:T(8,128)(2,1)}, u32[]{:S(2)}, u32[]{:S(2)}) async-start(bf16[16,3,128,128]{3,2,1,0:T(8,128)(2,1)} %bitcast.295), calls=%async_computation | async-start | bytes 3145728 | tf_op jit(solution)/shard_map/all_to_all | solution.py:394
  255.0 16.6 %all-to-all-start.1 = ((bf16[16,128,128]{2,1,0:T(8,128)(2,1)}), bf16[16,128,128]{2,1,0:T(8,128)(2,1)}, u32[]{:S(2)}, u32[]{:S(2)}) async-start(bf16[16,128,128]{2,1,0:T(8,128)(2,1)} %get-tuple-element.19), calls=%async_computation.1 | async-start | bytes 1048576 | tf_op jit(solution)/shard_map/all_to_all | solution.py:398
  277.6 20.5 %collective-permute-start.34 = (bf16[128,2048]{1,0:T(8,128)(2,1)S(1)}, bf16[128,2048]{1,0:T(8,128)(2,1)S(1)}, u32[]{:S(2)}, u32[]{:S(2)}) collective-permute-start(bf16[128,2048]{1,0:T(8,128)(2,1)S(1)} %copy-done.10), channel_id=1, source_target_pairs={{0,32},{32,0},{64,96},{96,64},{1,33},{33,1},{65,97},{97,65},{2,34}... | collective-permute-start | bytes 1572872 | tf_op jit(solution)/shard_map/ppermute | solution.py:30
  279.6 17.0 %collective-permute-start.35 = (bf16[128,2048]{1,0:T(8,128)(2,1)S(1)}, bf16[128,2048]{1,0:T(8,128)(2,1)S(1)}, u32[]{:S(2)}, u32[]{:S(2)}) collective-permute-start(bf16[128,2048]{1,0:T(8,128)(2,1)S(1)} %copy-done.10), channel_id=1, source_target_pairs={{0,96},{32,64},{64,32},{96,0},{1,97},{33,65},{65,33},{97,1},{2,98}... | collective-permute-start | bytes 1572872 | tf_op jit(solution)/shard_map/ppermute | solution.py:30
  287.0 20.8 %collective-permute-start.25 = (bf16[128,2048]{1,0:T(8,128)(2,1)S(1)}, bf16[128,2048]{1,0:T(8,128)(2,1)S(1)}, u32[]{:S(2)}, u32[]{:S(2)}) collective-permute-start(bf16[128,2048]{1,0:T(8,128)(2,1)S(1)} %pad_maximum_fusion.19), channel_id=1, source_target_pairs={{0,96},{32,64},{64,32},{96,0},{1,97},{33,65},{65,33},{97,1},{2,98}... | collective-permute-start | bytes 1572872 | tf_op jit(solution)/shard_map/ppermute | solution.py:30
  288.3 20.9 %collective-permute-start.23 = (bf16[128,2048]{1,0:T(8,128)(2,1)S(1)}, bf16[128,2048]{1,0:T(8,128)(2,1)S(1)}, u32[]{:S(2)}, u32[]{:S(2)}) collective-permute-start(bf16[128,2048]{1,0:T(8,128)(2,1)S(1)} %pad_maximum_fusion.18), channel_id=1, source_target_pairs={{0,32},{32,0},{64,96},{96,64},{1,33},{33,1},{65,97},{97,65},{2,34}... | collective-permute-start | bytes 1572872 | tf_op jit(solution)/shard_map/ppermute | solution.py:30
  296.6 16.3 %collective-permute-start.36 = (bf16[64,2048]{1,0:T(8,128)(2,1)S(1)}, bf16[64,2048]{1,0:T(8,128)(2,1)S(1)}, u32[]{:S(2)}, u32[]{:S(2)}) collective-permute-start(bf16[64,2048]{1,0:T(8,128)(2,1)S(1)} %slice.510), channel_id=1, source_target_pairs={{0,32},{32,0},{64,96},{96,64},{1,33},{33,1},{65,97},{97,65},{2,34}... | collective-permute-start | bytes 786440 | tf_op jit(solution)/shard_map/ppermute | solution.py:30
  298.1 14.9 %collective-permute-start.37 = (bf16[64,2048]{1,0:T(8,128)(2,1)S(1)}, bf16[64,2048]{1,0:T(8,128)(2,1)S(1)}, u32[]{:S(2)}, u32[]{:S(2)}) collective-permute-start(bf16[64,2048]{1,0:T(8,128)(2,1)S(1)} %slice.511), channel_id=1, source_target_pairs={{0,96},{32,64},{64,32},{96,0},{1,97},{33,65},{65,33},{97,1},{2,98}... | collective-permute-start | bytes 786440 | tf_op jit(solution)/shard_map/ppermute | solution.py:30
  313.0 22.2 %collective-permute-start.26 = (bf16[128,2048]{1,0:T(8,128)(2,1)S(1)}, bf16[128,2048]{1,0:T(8,128)(2,1)S(1)}, u32[]{:S(2)}, u32[]{:S(2)}) collective-permute-start(bf16[128,2048]{1,0:T(8,128)(2,1)S(1)} %get-tuple-element.68), channel_id=1, source_target_pairs={{0,32},{32,0},{64,96},{96,64},{1,33},{33,1},{65,97},{97,65},{2,34}... | collective-permute-start | bytes 1572872 | tf_op jit(solution)/shard_map/ppermute | solution.py:30
  323.0 24.7 %collective-permute-start.28 = (bf16[64,2048]{1,0:T(8,128)(2,1)S(1)}, bf16[64,2048]{1,0:T(8,128)(2,1)S(1)}, u32[]{:S(2)}, u32[]{:S(2)}) collective-permute-start(bf16[64,2048]{1,0:T(8,128)(2,1)S(1)} %slice.502), channel_id=1, source_target_pairs={{0,32},{32,0},{64,96},{96,64},{1,33},{33,1},{65,97},{97,65},{2,34}... | collective-permute-start | bytes 786440 | tf_op jit(solution)/shard_map/ppermute | solution.py:30
  335.3 16.5 %collective-permute-start.29 = (bf16[64,2048]{1,0:T(8,128)(2,1)S(1)}, bf16[64,2048]{1,0:T(8,128)(2,1)S(1)}, u32[]{:S(2)}, u32[]{:S(2)}) collective-permute-start(bf16[64,2048]{1,0:T(8,128)(2,1)S(1)} %slice.503), channel_id=1, source_target_pairs={{0,96},{32,64},{64,32},{96,0},{1,97},{33,65},{65,33},{97,1},{2,98}... | collective-permute-start | bytes 786440 | tf_op jit(solution)/shard_map/ppermute | solution.py:30
  391.0 16.4 %collective-permute-start.41 = (bf16[128,2048]{1,0:T(8,128)(2,1)S(1)}, bf16[128,2048]{1,0:T(8,128)(2,1)S(1)}, u32[]{:S(2)}, u32[]{:S(2)}) collective-permute-start(bf16[128,2048]{1,0:T(8,128)(2,1)S(1)} %pad_maximum_fusion.23), channel_id=1, source_target_pairs={{0,96},{32,64},{64,32},{96,0},{1,97},{33,65},{65,33},{97,1},{2,98}... | collective-permute-start | bytes 1572872 | tf_op jit(solution)/shard_map/ppermute | solution.py:30
  392.4 15.3 %collective-permute-start.39 = (bf16[128,2048]{1,0:T(8,128)(2,1)S(1)}, bf16[128,2048]{1,0:T(8,128)(2,1)S(1)}, u32[]{:S(2)}, u32[]{:S(2)}) collective-permute-start(bf16[128,2048]{1,0:T(8,128)(2,1)S(1)} %pad_maximum_fusion.22), channel_id=1, source_target_pairs={{0,32},{32,0},{64,96},{96,64},{1,33},{33,1},{65,97},{97,65},{2,34}... | collective-permute-start | bytes 1572872 | tf_op jit(solution)/shard_map/ppermute | solution.py:30
  396.6 18.1 %collective-permute-start.33 = (bf16[128,2048]{1,0:T(8,128)(2,1)S(1)}, bf16[128,2048]{1,0:T(8,128)(2,1)S(1)}, u32[]{:S(2)}, u32[]{:S(2)}) collective-permute-start(bf16[128,2048]{1,0:T(8,128)(2,1)S(1)} %pad_maximum_fusion.21), channel_id=1, source_target_pairs={{0,96},{32,64},{64,32},{96,0},{1,97},{33,65},{65,33},{97,1},{2,98}... | collective-permute-start | bytes 1572872 | tf_op jit(solution)/shard_map/ppermute | solution.py:30
  398.5 17.1 %collective-permute-start.31 = (bf16[128,2048]{1,0:T(8,128)(2,1)S(1)}, bf16[128,2048]{1,0:T(8,128)(2,1)S(1)}, u32[]{:S(2)}, u32[]{:S(2)}) collective-permute-start(bf16[128,2048]{1,0:T(8,128)(2,1)S(1)} %pad_maximum_fusion.20), channel_id=1, source_target_pairs={{0,32},{32,0},{64,96},{96,64},{1,33},{33,1},{65,97},{97,65},{2,34}... | collective-permute-start | bytes 1572872 | tf_op jit(solution)/shard_map/ppermute | solution.py:30
  423.3 13.5 %collective-permute-start.42 = (bf16[128,2048]{1,0:T(8,128)(2,1)S(1)}, bf16[128,2048]{1,0:T(8,128)(2,1)S(1)}, u32[]{:S(2)}, u32[]{:S(2)}) collective-permute-start(bf16[128,2048]{1,0:T(8,128)(2,1)S(1)} %get-tuple-element.65), channel_id=1, source_target_pairs={{0,32},{32,0},{64,96},{96,64},{1,33},{33,1},{65,97},{97,65},{2,34}... | collective-permute-start | bytes 1572872 | tf_op jit(solution)/shard_map/ppermute | solution.py:30
  491.5 111.9 %collective-permute-start.69 = (bf16[2,2320,1024]{2,1,0:T(8,128)(2,1)}, bf16[2,2320,1024]{2,1,0:T(8,128)(2,1)}, u32[]{:S(2)}, u32[]{:S(2)}) collective-permute-start(bf16[2,2320,1024]{2,1,0:T(8,128)(2,1)} %slice.547), channel_id=1, source_target_pairs={{0,1},{1,0},{2,3},{3,2},{4,5},{5,4},{6,7},{7,6},{8,9},{9,8},{10,11... | collective-permute-start | bytes 28508168 | tf_op jit(solution)/shard_map/ppermute | solution.py:30
  531.4 28.3 %all-to-all-start.3 = ((bf16[16,3,128,128]{3,2,1,0:T(8,128)(2,1)}), bf16[16,3,128,128]{3,2,1,0:T(8,128)(2,1)}, u32[]{:S(2)}, u32[]{:S(2)}) async-start(bf16[16,3,128,128]{3,2,1,0:T(8,128)(2,1)} %attend_back.1), calls=%async_computation.3 | async-start | bytes 3145728 | tf_op jit(solution)/shard_map/all_to_all | solution.py:454
  566.4 31.9 %collective-permute-start.60 = (bf16[2,768,1024]{2,1,0:T(8,128)(2,1)S(1)}, bf16[2,768,1024]{2,1,0:T(8,128)(2,1)}, u32[]{:S(2)}, u32[]{:S(2)}) collective-permute-start(bf16[2,768,1024]{2,1,0:T(8,128)(2,1)S(1)} %slice.528), channel_id=1, source_target_pairs={{0,1},{1,0},{2,3},{3,2},{4,5},{5,4},{6,7},{7,6},{8,9},{9,8},{10,11... | collective-permute-start | bytes 9437192 | tf_op jit(solution)/shard_map/ppermute | solution.py:30
  583.4 13.6 %collective-permute-start.49 = (bf16[128,2048]{1,0:T(8,128)(2,1)S(1)}, bf16[128,2048]{1,0:T(8,128)(2,1)S(1)}, u32[]{:S(2)}, u32[]{:S(2)}) collective-permute-start(bf16[128,2048]{1,0:T(8,128)(2,1)S(1)} %pad_maximum_fusion.25), channel_id=1, source_target_pairs={{0,96},{32,64},{64,32},{96,0},{1,97},{33,65},{65,33},{97,1},{2,98}... | collective-permute-start | bytes 1572872 | tf_op jit(solution)/shard_map/ppermute | solution.py:30
  601.5 14.2 %collective-permute-start.61 = (bf16[384,512]{1,0:T(8,128)(2,1)S(1)}, bf16[384,512]{1,0:T(8,128)(2,1)S(1)}, u32[]{:S(2)}, u32[]{:S(2)}) collective-permute-start(bf16[384,512]{1,0:T(8,128)(2,1)S(1)} %get-tuple-element.84), channel_id=1, source_target_pairs={{0,24},{8,16},{16,8},{24,0},{1,25},{9,17},{17,9},{25,1},{2,26},{10... | collective-permute-start | bytes 1179656 | tf_op jit(solution)/shard_map/ppermute | solution.py:30
  601.9 14.7 %collective-permute-start.63 = (bf16[384,512]{1,0:T(8,128)(2,1)S(1)}, bf16[384,512]{1,0:T(8,128)(2,1)S(1)}, u32[]{:S(2)}, u32[]{:S(2)}) collective-permute-start(bf16[384,512]{1,0:T(8,128)(2,1)S(1)} %get-tuple-element.83), channel_id=1, source_target_pairs={{0,16},{8,24},{16,0},{24,8},{1,17},{9,25},{17,1},{25,9},{2,18},{10... | collective-permute-start | bytes 1179656 | tf_op jit(solution)/shard_map/ppermute | solution.py:30
  610.2 26.5 %collective-permute-start.70 = (bf16[1152,512]{1,0:T(8,128)(2,1)S(1)}, bf16[1152,512]{1,0:T(8,128)(2,1)S(1)}, u32[]{:S(2)}, u32[]{:S(2)}) collective-permute-start(bf16[1152,512]{1,0:T(8,128)(2,1)S(1)} %get-tuple-element.76), channel_id=1, source_target_pairs={{0,24},{8,16},{16,8},{24,0},{1,25},{9,17},{17,9},{25,1},{2,26},{10... | collective-permute-start | bytes 3538952 | tf_op jit(solution)/shard_map/ppermute | solution.py:30
  612.8 32.6 %collective-permute-start.51 = (f32[32,128]{1,0:T(8,128)S(1)}, f32[32,128]{1,0:T(8,128)S(1)}, u32[]{:S(2)}, u32[]{:S(2)}) collective-permute-start(f32[32,128]{1,0:T(8,128)S(1)} %pad_maximum_fusion.29), channel_id=1, source_target_pairs={{0,64},{32,96},{64,0},{96,32},{1,65},{33,97},{65,1},{97,33},{2,66}... | collective-permute-start | bytes 49160 | tf_op jit(solution)/shard_map/ppermute | solution.py:30
  614.1 33.3 %collective-permute-start.52 = (f32[32,128]{1,0:T(8,128)S(1)}, f32[32,128]{1,0:T(8,128)S(1)}, u32[]{:S(2)}, u32[]{:S(2)}) collective-permute-start(f32[32,128]{1,0:T(8,128)S(1)} %pad_maximum_fusion.29), channel_id=1, source_target_pairs={{0,96},{32,64},{64,32},{96,0},{1,97},{33,65},{65,33},{97,1},{2,98}... | collective-permute-start | bytes 49160 | tf_op jit(solution)/shard_map/ppermute | solution.py:30
  615.8 31.6 %collective-permute-start.50 = (f32[32,128]{1,0:T(8,128)S(1)}, f32[32,128]{1,0:T(8,128)S(1)}, u32[]{:S(2)}, u32[]{:S(2)}) collective-permute-start(f32[32,128]{1,0:T(8,128)S(1)} %pad_maximum_fusion.29), channel_id=1, source_target_pairs={{0,32},{32,0},{64,96},{96,64},{1,33},{33,1},{65,97},{97,65},{2,34}... | collective-permute-start | bytes 49160 | tf_op jit(solution)/shard_map/ppermute | solution.py:30
  617.0 26.4 %collective-permute-start.72 = (bf16[1168,512]{1,0:T(8,128)(2,1)S(1)}, bf16[1168,512]{1,0:T(8,128)(2,1)S(1)}, u32[]{:S(2)}, u32[]{:S(2)}) collective-permute-start(bf16[1168,512]{1,0:T(8,128)(2,1)S(1)} %get-tuple-element.75), channel_id=1, source_target_pairs={{0,16},{8,24},{16,0},{24,8},{1,17},{9,25},{17,1},{25,9},{2,18},{10... | collective-permute-start | bytes 3588104 | tf_op jit(solution)/shard_map/ppermute | solution.py:30
  636.7 96.9 %collective-permute-start.64 = (bf16[768,512]{1,0:T(8,128)(2,1)}, bf16[768,512]{1,0:T(8,128)(2,1)}, u32[]{:S(2)}, u32[]{:S(2)}) collective-permute-start(bf16[768,512]{1,0:T(8,128)(2,1)} %pad_maximum_fusion.14), channel_id=1, source_target_pairs={{0,24},{8,16},{16,8},{24,0},{1,25},{9,17},{17,9},{25,1},{2,26},{10... | collective-permute-start | bytes 2359304 | tf_op jit(solution)/shard_map/ppermute | solution.py:30
  643.3 90.3 %collective-permute-start.62 = (bf16[768,512]{1,0:T(8,128)(2,1)}, bf16[768,512]{1,0:T(8,128)(2,1)}, u32[]{:S(2)}, u32[]{:S(2)}) collective-permute-start(bf16[768,512]{1,0:T(8,128)(2,1)} %pad_maximum_fusion.13), channel_id=1, source_target_pairs={{0,16},{8,24},{16,0},{24,8},{1,17},{9,25},{17,1},{25,9},{2,18},{10... | collective-permute-start | bytes 2359304 | tf_op jit(solution)/shard_map/ppermute | solution.py:30
  645.5 100.2 %collective-permute-start.71 = (bf16[2320,512]{1,0:T(8,128)(2,1)}, bf16[2320,512]{1,0:T(8,128)(2,1)}, u32[]{:S(2)}, u32[]{:S(2)}) collective-permute-start(bf16[2320,512]{1,0:T(8,128)(2,1)} %pad_maximum_fusion.9), channel_id=1, source_target_pairs={{0,16},{8,24},{16,0},{24,8},{1,17},{9,25},{17,1},{25,9},{2,18},{10... | collective-permute-start | bytes 7127048 | tf_op jit(solution)/shard_map/ppermute | solution.py:30
  647.4 98.2 %collective-permute-start.73 = (bf16[2320,512]{1,0:T(8,128)(2,1)}, bf16[2320,512]{1,0:T(8,128)(2,1)}, u32[]{:S(2)}, u32[]{:S(2)}) collective-permute-start(bf16[2320,512]{1,0:T(8,128)(2,1)} %pad_maximum_fusion.10), channel_id=1, source_target_pairs={{0,24},{8,16},{16,8},{24,0},{1,25},{9,17},{17,9},{25,1},{2,26},{10... | collective-permute-start | bytes 7127048 | tf_op jit(solution)/shard_map/ppermute | solution.py:30
  647.4 61.6 %collective-permute-start.54 = (f32[32,128]{1,0:T(8,128)S(1)}, f32[32,128]{1,0:T(8,128)S(1)}, u32[]{:S(2)}, u32[]{:S(2)}) collective-permute-start(f32[32,128]{1,0:T(8,128)S(1)} %add_add_fusion.2), channel_id=1, source_target_pairs={{0,8},{8,0},{16,24},{24,16},{1,9},{9,1},{17,25},{25,17},{2,10},{10... | collective-permute-start | bytes 49160 | tf_op jit(solution)/shard_map/ppermute | solution.py:30
  743.4 20.3 %collective-permute-start.68 = (bf16[768,128]{1,0:T(8,128)(2,1)S(1)}, bf16[768,128]{1,0:T(8,128)(2,1)S(1)}, u32[]{:S(2)}, u32[]{:S(2)}) collective-permute-start(bf16[768,128]{1,0:T(8,128)(2,1)S(1)} %pad_maximum_fusion.28), channel_id=1, source_target_pairs={{0,6},{2,4},{4,2},{6,0},{1,7},{3,5},{5,3},{7,1},{8,14},{10,12},{12... | collective-permute-start | bytes 589832 | tf_op jit(solution)/shard_map/ppermute | solution.py:30
  745.0 18.8 %collective-permute-start.66 = (bf16[768,128]{1,0:T(8,128)(2,1)S(1)}, bf16[768,128]{1,0:T(8,128)(2,1)S(1)}, u32[]{:S(2)}, u32[]{:S(2)}) collective-permute-start(bf16[768,128]{1,0:T(8,128)(2,1)S(1)} %pad_maximum_fusion.27), channel_id=1, source_target_pairs={{0,2},{2,0},{4,6},{6,4},{1,3},{3,1},{5,7},{7,5},{8,10},{10,8},{12,... | collective-permute-start | bytes 589832 | tf_op jit(solution)/shard_map/ppermute | solution.py:30
  759.7 14.2 %collective-permute-start.75 = (bf16[2320,128]{1,0:T(8,128)(2,1)S(1)}, bf16[2320,128]{1,0:T(8,128)(2,1)}, u32[]{:S(2)}, u32[]{:S(2)}) collective-permute-start(bf16[2320,128]{1,0:T(8,128)(2,1)S(1)} %pad_maximum_fusion.16), channel_id=1, source_target_pairs={{0,2},{2,0},{4,6},{6,4},{1,3},{3,1},{5,7},{7,5},{8,10},{10,8},{12,... | collective-permute-start | bytes 1781768 | tf_op jit(solution)/shard_map/ppermute | solution.py:30
  761.6 15.0 %collective-permute-start.77 = (bf16[2320,128]{1,0:T(8,128)(2,1)}, bf16[2320,128]{1,0:T(8,128)(2,1)}, u32[]{:S(2)}, u32[]{:S(2)}) collective-permute-start(bf16[2320,128]{1,0:T(8,128)(2,1)} %pad_maximum_fusion.17), channel_id=1, source_target_pairs={{0,6},{2,4},{4,2},{6,0},{1,7},{3,5},{5,3},{7,1},{8,14},{10,12},{12... | collective-permute-start | bytes 1781768 | tf_op jit(solution)/shard_map/ppermute | solution.py:30
  (79 other events, 1144.1 us)

commit v2 on v1

--- a/solution.py
+++ b/solution.py
@@ -34,27 +34,72 @@
     return (rows // 2 + 15) // 16 * 16
 
 
-def gather4(value, axis):
-    half = middle(value.shape[0])
-    near1 = swap(value, axis, 1)
-    near3 = swap(value, axis, 3)
-    far = jnp.concatenate([swap(near3[:half], axis, 1), swap(near1[half:], axis, 3)], axis=0)
-    return [value, near1, far, near3]
+def gather4(value, axis, hold=()):
+    near = swap(value, axis, 1), swap(value, axis, 3)
+    return gather_far(value, near, axis, hold)
+
+
+def gather_far(value, near, axis, hold=()):
+    half = middle(value.shape[0]) if value.ndim == 2 else value.shape[0] // 2
+    near1, near3 = near
+    far1 = swap(after(near3[:half], *hold), axis, 1)
+    return value, near1, far1, swap(near1[half:], axis, 3), near3
+
+
+def add(*values):
+    return functools.reduce(lambda a, b: a + b, [value.astype(f32) for value in values])
+
+
+def after(value, *earlier):
+    return lax.optimization_barrier((value, *earlier))[0] if earlier else value
+
+
+def far_sums(part2):
+    rows = part2[0].shape[0]
+    half = middle(rows) if part2[0].ndim == 2 else rows // 2
+    return (
+        add(*[term[:half] for term in part2]).astype(bf16),
+        add(*[term[half:] for term in part2]).astype(bf16),
+    )
+
+
+def scatter_far(part2, axis):
+    far_a, far_b = far_sums(part2)
+    return swap(far_a, axis, 1), swap(far_b, axis, 3)
+
+
+def near_sums(part1, part3, far):
+    from1, from3 = far
+    half = from1.shape[0]
+    part1 = jnp.concatenate(
+        [
+            add(*[term[:half] for term in part1]).astype(bf16),
+            add(from3, *[term[half:] for term in part1]).astype(bf16),
+        ],
+        axis=0,
+    )
+    part3 = jnp.concatenate(
+        [
+            add(from1, *[term[:half] for term in part3]).astype(bf16),
+            add(*[term[half:] for term in part3]).astype(bf16),
+        ],
+        axis=0,
+    )
+    return part1, part3
+
+
+def scatter_near(part1, part3, far, axis, hold=()):
+    part1, part3 = near_sums(part1, part3, far)
+    return swap(after(part1, *hold), axis, 1), swap(part3, axis, 3)
 
 
 def scatter4(parts, axis):
     own, part1, part2, part3 = parts
-    half = middle(own.shape[0])
-    from1 = swap(part2[:half], axis, 1)
-    from3 = swap(part2[half:], axis, 3)
-    part3 = jnp.concatenate(
-        [(part3[:half].astype(f32) + from1.astype(f32)).astype(bf16), part3[half:]], axis=0
-    )
-    part1 = jnp.concatenate(
-        [part1[:half], (part1[half:].astype(f32) + from3.astype(f32)).astype(bf16)], axis=0
-    )
-    got1, got3 = swap(part1, axis, 1), swap(part3, axis, 3)
-    return own.astype(f32) + got1.astype(f32) + got3.astype(f32)
+    return add(*scatter_near(part1, part3, scatter_far(part2, axis), axis), *own)
+
+
+def pairs(mine, got):
+    return [[mine[k], got[k]] for k in range(4)]
 
 
 def total4(value, axis):
@@ -100,6 +145,7 @@
         in_specs=[smem_spec(), vmem_spec(), vmem_spec(), vmem_spec()],
         out_specs=(vmem_spec(),) * 3,
         compiler_params=params(),
+        cost_estimate=cost(2.5),
         name="prepare",
     )(place, tok, dy, gain)
 
@@ -116,6 +162,7 @@
         in_specs=[smem_spec(), vmem_spec()],
         out_specs=vmem_spec(),
         compiler_params=params(),
+        cost_estimate=cost(2),
         name="restore",
     )(place, value)
 
@@ -132,51 +179,442 @@
     return lax.dot_general(left, right, (((0,), (0,)), ((), ())), preferred_element_type=f32)
 
 
-def qkv_kernel(a0, a1, a2, a3, mine_ref, theirs_ref, cos_ref, sin_ref, out_ref, rows_ref):
-    step = pl.program_id(0) * 3 + pl.program_id(1)
-    kind = pl.program_id(1)
-
-    @pl.when(step == 0)
-    def _():
-        for j, ref in enumerate((a0, a1, a2, a3)):
-            rows_ref[j * 128 : (j + 1) * 128, :] = ref[...]
-
-    pre = dot_nt(rows_ref[:, :1024], mine_ref[0]) + dot_nt(rows_ref[:, 1024:], theirs_ref[0])
-
-    def store(turned):
+def any_spec():
+    return pl.BlockSpec(memory_space=pl.ANY)
+
+
+def pieces_of(order):
+    found = []
+    for core in range(2):
+        for second in range(4):
+            for first in range(4):
+                z, y = (first, second) if order == "zy" else (second, first)
+                slab, turn = y & 1, y >> 1
+                if second == 2:
+                    array, entry = (2, first) if first < 2 else (3, first - 2)
+                else:
+                    array, entry = {0: 0, 1: 1, 3: 4}[second], first
+                found.append((core * 5 + array, entry, slab, core * 8 + turn * 4 + z))
+    return found
+
+
+GROUP_A, GROUP_B = 1024, 1040
+MLP_ROWS = {
+    "gate": ((0, 0, 688, 0),),
+    "up": ((0, 688, 336, 0), (1, 0, 352, 336)),
+    "down": ((1, 352, 688, 0),),
+}
+
+
+class Loader:
+    def __init__(self, sems, source_ref=None):
+        self.sems = sems
+        self.source_ref = source_ref
+        self.used = 0
+
+    def copy(self, source, target):
+        made = pltpu.make_async_copy(source, target, self.sems.at[self.used])
+        self.used += 1
+        made.start()
+        return made
+
+    def weight(self, refs, first_row, target, source_ref=None):
+        source_ref = self.source_ref if source_ref is None else source_ref
+        waits = ([], [])
+        rows = target.shape[1]
+        for core in range(2):
+            for k in range(16):
+                slab, block = k >> 3, core * 8 + (k & 7)
+                waits[slab].append(
+                    self.copy(
+                        refs[core].at[source_ref[k], first_row : first_row + rows],
+                        target.at[slab, :, block * 128 : (block + 1) * 128],
+                    )
+                )
+        return waits
+
+    def mlp_weight(self, pieces, name, target):
+        waits = ([], [])
+        for group, first_row, rows, at in MLP_ROWS[name]:
+            refs = pieces[group * 10 : group * 10 + 10]
+            for array, entry, slab, block in pieces_of(("zy", "yz")[group]):
+                waits[slab].append(
+                    self.copy(
+                        refs[array].at[entry, first_row : first_row + rows],
+                        target.at[slab, at : at + rows, block * 128 : (block + 1) * 128],
+                    )
+                )
+        return waits
+
+    def rows(self, refs, target):
+        return [
+            self.copy(ref, target.at[first : first + ref.shape[0]])
+            for ref, first in zip(refs, (0, 128, 256, 320, 384))
+        ]
+
+
+def wait_all(copies):
+    for made in copies:
+        made.wait()
+
+
+def cost(micros):
+    return pl.CostEstimate(flops=int(micros * 1.15e9), bytes_accessed=0, transcendentals=0)
+
+
+def kernel_call(kernel, out_shape, args, scratch, copies, micros, name, smem=0):
+    specs = [any_spec()] * (len(args) - smem)
+    return pl.pallas_call(
+        kernel,
+        out_shape=out_shape,
+        in_specs=[smem_spec()] * smem + specs,
+        out_specs=jax.tree.map(lambda _: vmem_spec(), out_shape),
+        scratch_shapes=list(scratch) + [pltpu.SemaphoreType.DMA((copies,))],
+        compiler_params=params(),
+        cost_estimate=cost(micros),
+        name=name,
+    )(*args)
+
+
+def shape_of(*dims, dtype=bf16):
+    return jax.ShapeDtypeStruct(dims, dtype)
+
+
+ROWS = pltpu.VMEM((512, 2048), bf16)
+
+
+def weight_scratch(rows):
+    return pltpu.VMEM((2, rows, 2048), bf16)
+
+
+def stack_kernel(own, near1, far, near3, out_ref, sems):
+    load = Loader(sems)
+    wait_all([load.copy(ref, out_ref.at[n]) for n, ref in enumerate((own, near1, far, near3))])
+
+
+def stacked(parts):
+    own = parts[0]
+    return pl.pallas_call(
+        stack_kernel,
+        out_shape=shape_of(4, *own.shape),
+        in_specs=[any_spec()] * 4,
+        out_specs=vmem_spec(),
+        scratch_shapes=[pltpu.SemaphoreType.DMA((4,))],
+        compiler_params=params(),
+        cost_estimate=cost(2.5),
+        name="stack",
+    )(*parts)
+
+
+def qkv_kernel(source_ref, *refs):
+    rows, weights = refs[:5], refs[5:7]
+    cos_ref, sin_ref, out_ref, acts, weight, tables, sems = refs[7:]
+    load = Loader(sems, source_ref)
+    small = [load.copy(cos_ref, tables.at[0]), load.copy(sin_ref, tables.at[1])]
+    acts_in = load.rows(rows, acts)
+    arrived = load.weight(weights, 0, weight)
+    wait_all(small + acts_in)
+    for slab in range(2):
+        wait_all(arrived[slab])
+        for kind in range(3):
+            pre = dot_nt(acts[...], weight[slab, kind * 256 : (kind + 1) * 256])
+            for head in range(2):
+                for j in range(4):
+                    tile = pre[j * 128 : (j + 1) * 128, head * 128 : (head + 1) * 128]
+                    if kind < 2:
+                        tile = tile * tables[0] + pltpu.roll(tile, 64, 1) * tables[1]
+                    out_ref[j * 4 + slab * 2 + head, kind] = tile.astype(bf16)
+
+
+def project_qkv(source, rows, weights, cosine, sine):
+    return kernel_call(
+        qkv_kernel,
+        shape_of(16, 3, 128, 128),
+        (source, *rows, *weights, cosine, sine),
+        [ROWS, weight_scratch(768), pltpu.VMEM((2, 128, 128), f32)],
+        7 + 32,
+        10,
+        "project_qkv",
+        smem=1,
+    )
+
+
+def out_kernel(source_ref, low_ref, mine_ref, theirs_ref, part_ref, low, acts, weight, sems):
+    load = Loader(sems, source_ref)
+    low_in = load.copy(low_ref, low)
+    arrived = load.weight((mine_ref, theirs_ref), 768, weight)
+    low_in.wait()
+    for p in range(16):
+        j, slab, head = p >> 2, (p >> 1) & 1, p & 1
+        acts[slab, j * 128 : (j + 1) * 128, head * 128 : (head + 1) * 128] = low[p]
+    wait_all(arrived[0] + arrived[1])
+    for j in range(0, 4, 2):
+        here = slice(j * 128, (j + 2) * 128)
+        part = dot_nn(acts[0, here], weight[0]) + dot_nn(acts[1, here], weight[1])
+        part_ref[j : j + 2] = part.astype(bf16).reshape(2, 128, 2048)
+
+
+def project_out(source, low, weights):
+    return kernel_call(
+        out_kernel,
+        shape_of(4, 128, 2048),
+        (source, low, *weights),
+        [
+            pltpu.VMEM((16, 128, 128), bf16),
+            pltpu.VMEM((2, 512, 256), bf16),
+            weight_scratch(256),
+        ],
+        1 + 32,
+        5,
+        "project_out",
+        smem=1,
+    )
+
+
+def mlp_kernel(*refs):
+    rows, dy_rows, weights = refs[:5], refs[5:10], refs[10:30]
+    hidden_ref, d_gate_ref, d_up_ref, part_ref = refs[30:34]
+    acts, acts_dy, w_gate, w_up, w_down, acc, sems = refs[34:]
+    load = Loader(sems)
+    acts_in = load.rows(rows, acts)
+    gates = load.mlp_weight(weights, "gate", w_gate)
+    ups = load.mlp_weight(weights, "up", w_up)
+    dy_in = load.rows(dy_rows, acts_dy)
+    downs = load.mlp_weight(weights, "down", w_down)
+    wait_all(acts_in)
+    for slab in range(2):
+        wait_all(gates[slab])
+        gate = dot_nt(acts[...], w_gate[slab])
+        wait_all(ups[slab])
+        up = dot_nt(acts[...], w_up[slab])
+        if slab == 0:
+            wait_all(dy_in)
+        wait_all(downs[slab])
+        d_hidden = dot_nt(acts_dy[...], w_down[slab])
+        sigmoid = 1.0 / (1.0 + jnp.exp(-gate))
+        silu = gate * sigmoid
+        hidden_ref[slab] = (silu * up).astype(bf16)
+        d_gate_ref[slab] = (d_hidden * up * sigmoid * (1.0 + gate * (1.0 - sigmoid))).astype(bf16)
+        d_up_ref[slab] = (d_hidden * silu).astype(bf16)
+        part = dot_nn(d_gate_ref[slab], w_gate[slab]) + dot_nn(d_up_ref[slab], w_up[slab])
+        if slab == 0:
+            acc[...] = part
+        else:
+            part_ref[...] = (acc[...] + part).astype(bf16).reshape(4, 128, 2048)
+
+
+def mlp(rows, dy_rows, weights):
+    return kernel_call(
+        mlp_kernel,
+        (shape_of(2, 512, 688),) * 3 + (shape_of(4, 128, 2048),),
+        (*rows, *dy_rows, *weights),
+        [ROWS, ROWS]
+        + [weight_scratch(688)] * 3
+        + [pltpu.VMEM((512, 2048), f32)],
+        10 + 128,
+        28,
+        "mlp",
+    )
+
+
+def down_kernel(hidden_ref, *refs):
+    weights, (part_ref, hidden, weight, sems) = refs[:20], refs[20:]
+    load = Loader(sems)
+    hidden_in = load.copy(hidden_ref, hidden)
+    arrived = load.mlp_weight(weights, "down", weight)
+    hidden_in.wait()
+    wait_all(arrived[0] + arrived[1])
+    part = dot_nn(hidden[0], weight[0]) + dot_nn(hidden[1], weight[1])
+    part_ref[...] = part.astype(bf16).reshape(4, 128, 2048)
+
+
+def project_down(hidden, weights):
+    return kernel_call(
+        down_kernel,
+        shape_of(4, 128, 2048),
+        (hidden, *weights),
+        [pltpu.VMEM((2, 512, 688), bf16), weight_scratch(688)],
+        1 + 32,
+        8,
+        "project_down",
+    )
+
+
+def feature_grads(acts, rows, store):
+    for slab in range(2):
+        for quarter in range(4):
+            value = dot_tn(acts[slab], rows[:, quarter * 512 : (quarter + 1) * 512])
+            core, turn = divmod(quarter, 2)
+            for z in range(4):
+                block = value[:, z * 128 : (z + 1) * 128].astype(bf16)
+                store(core, slab * 8 + turn * 4 + z, block)
+
+
+def mlp_grad_kernel(d_gate_ref, d_up_ref, hidden_ref, *refs):
+    rows, dy_rows, outs, (acts, acts_dy, hidden, sems) = (
+        refs[:5],
+        refs[5:10],
+        refs[10:12],
+        refs[12:],
+    )
+    load = Loader(sems)
+    acts_in = load.rows(rows, acts)
+    hidden_in = [
+        load.copy(ref, hidden.at[n]) for n, ref in enumerate((d_gate_ref, d_up_ref, hidden_ref))
+    ]
+    dy_in = load.rows(dy_rows, acts_dy)
+    wait_all(acts_in)
+    for n in range(3):
+        hidden_in[n].wait()
+        if n == 2:
+            wait_all(dy_in)
+
+        def store(core, k, block, first=n * 688):
+            y = ((k >> 2) & 1) * 2 + (k >> 3)
+            outs[core][y, k & 3, first : first + 688] = block
+
+        feature_grads(hidden.at[n], acts if n < 2 else acts_dy, store)
+
+
+def mlp_grad(d_gate, d_up, hidden, rows, dy_rows):
+    return kernel_call(
+        mlp_grad_kernel,
+        (shape_of(4, 4, 2064, 128),) * 2,
+        (d_gate, d_up, hidden, *rows, *dy_rows),
+        [ROWS, ROWS, pltpu.VMEM((3, 2, 512, 688), bf16)],
+        13,
+        18,
+        "mlp_grad",
+    )
+
+
+def out_back_kernel(source_ref, *refs):
+    rows, weights = refs[:5], refs[5:7]
+    out_ref, acts, weight, sems = refs[7:]
+    load = Loader(sems, source_ref)
+    acts_in = load.rows(rows, acts)
+    arrived = load.weight(weights, 768, weight)
+    wait_all(acts_in)
+    for slab in range(2):
+        wait_all(arrived[slab])
+        value = dot_nt(acts[...], weight[slab]).astype(bf16)
         for j in range(4):
-            for h in range(2):
-                tile = pre[j * 128 : (j + 1) * 128, h * 128 : (h + 1) * 128]
-                if turned:
-                    tile = tile * cos_ref[...] + pltpu.roll(tile, 64, 1) * sin_ref[...]
-                out_ref[j, 0, h, 0] = tile.astype(bf16)
-
-    @pl.when(kind < 2)
-    def _():
-        store(True)
-
-    @pl.when(kind == 2)
-    def _():
-        store(False)
-
-
-def project_qkv(rows, mine, theirs, cosine, sine):
-    whole = pl.BlockSpec((128, 2048), lambda s, t: (0, 0))
-    weight = pl.BlockSpec((1, 256, 1024), lambda s, t: (s, t, 0))
-    table = pl.BlockSpec((128, 128), lambda s, t: (0, 0))
-    return pl.pallas_call(
-        qkv_kernel,
-        grid=(2, 3),
-        out_shape=jax.ShapeDtypeStruct((4, 2, 2, 3, 128, 128), bf16),
-        in_specs=[whole] * 4 + [weight] * 2 + [table] * 2,
-        out_specs=pl.BlockSpec((4, 1, 2, 1, 128, 128), lambda s, t: (0, s, 0, t, 0, 0)),
-        scratch_shapes=[pltpu.VMEM((512, 2048), bf16)],
-        compiler_params=params(),
-        cost_estimate=pl.CostEstimate(
-            flops=2 * 512 * 2048 * 1536, bytes_accessed=10 << 20, transcendentals=0
-        ),
-        name="project_qkv",
-    )(*rows, mine, theirs, cosine, sine)
+            for head in range(2):
+                out_ref[j * 4 + slab * 2 + head] = value[
+                    j * 128 : (j + 1) * 128, head * 128 : (head + 1) * 128
+                ]
+
+
+def out_back(source, rows, weights):
+    return kernel_call(
+        out_back_kernel,
+        shape_of(16, 128, 128),
+        (source, *rows, *weights),
+        [ROWS, weight_scratch(256)],
+        5 + 32,
+        6,
+        "out_back",
+        smem=1,
+    )
+
+
+def unpack_heads(source, target):
+    for p in range(16):
+        j, slab, head = p >> 2, (p >> 1) & 1, p & 1
+        for kind in range(3):
+            column = (kind * 2 + head) * 128
+            target[slab, j * 128 : (j + 1) * 128, column : column + 128] = source[p, kind]
+
+
+def qkv_back_kernel(source_ref, dqkv_ref, mine_ref, theirs_ref, *refs):
+    rows, (part_ref, gain_ref, dqkv, acts, weight, tokens, acc, sems) = refs[:5], refs[5:]
+    load = Loader(sems, source_ref)
+    dqkv_in = load.copy(dqkv_ref, dqkv)
+    arrived = load.weight((mine_ref, theirs_ref), 0, weight)
+    tokens_in = load.rows(rows, tokens)
+    dqkv_in.wait()
+    unpack_heads(dqkv, acts)
+    for slab in range(2):
+        wait_all(arrived[slab])
+        part = dot_nn(acts[slab], weight[slab])
+        if slab == 0:
+            acc[...] = part
+        else:
+            acc[...] += part
+            part_ref[...] = acc[...].astype(bf16).reshape(4, 128, 2048)
+    wait_all(tokens_in)
+    gain_ref[...] = jnp.zeros_like(gain_ref)
+    for first in range(0, 512, 64):
+        values = tokens[first : first + 64].astype(f32)
+        inverse = lax.rsqrt(jnp.sum(values * values, axis=1, keepdims=True) / 2048.0 + norm_eps)
+        product = acc[first : first + 64] * values * inverse
+        gain_ref[...] += jnp.sum(product.reshape(8, 8, 2048), axis=0)
+
+
+def qkv_back(source, dqkv, weights, token_rows):
+    return kernel_call(
+        qkv_back_kernel,
+        (shape_of(4, 128, 2048), shape_of(8, 2048, dtype=f32)),
+        (source, dqkv, *weights, *token_rows),
+        [
+            pltpu.VMEM((16, 3, 128, 128), bf16),
+            pltpu.VMEM((2, 512, 768), bf16),
+            weight_scratch(768),
+            ROWS,
+            pltpu.VMEM((512, 2048), f32),
+        ],
+        1 + 32 + 5,
+        12,
+        "qkv_back",
+        smem=1,
+    )
+
+
+def qkv_grad_kernel(dqkv_ref, low_ref, *refs):
+    rows1, rows3, outs = refs[:5], refs[5:10], refs[10:12]
+    dqkv, low, acts, low_acts, in1, in3, sems = refs[12:]
+    load = Loader(sems)
+    low_in = load.copy(low_ref, low)
+    in3_in = load.rows(rows3, in3)
+    dqkv_in = load.copy(dqkv_ref, dqkv)
+    in1_in = load.rows(rows1, in1)
+    low_in.wait()
+    for p in range(16):
+        j, slab, head = p >> 2, (p >> 1) & 1, p & 1
+        low_acts[slab, j * 128 : (j + 1) * 128, head * 128 : (head + 1) * 128] = low[p]
+    wait_all(in3_in)
+
+    def store_at(first):
+        def store(core, k, block):
+            y = ((k >> 2) & 1) * 2 + (k >> 3)
+            outs[core][k & 3, y, first : first + block.shape[0]] = block
+
+        return store
+
+    feature_grads(low_acts, in3, store_at(768))
+    dqkv_in.wait()
+    unpack_heads(dqkv, acts)
+    wait_all(in1_in)
+    feature_grads(acts, in1, store_at(0))
+
+
+def qkv_grad(dqkv, low, rows1, rows3):
+    return kernel_call(
+        qkv_grad_kernel,
+        (shape_of(4, 4, 1024, 128),) * 2,
+        (dqkv, low, *rows1, *rows3),
+        [
+            pltpu.VMEM((16, 3, 128, 128), bf16),
+            pltpu.VMEM((16, 128, 128), bf16),
+            pltpu.VMEM((2, 512, 768), bf16),
+            pltpu.VMEM((2, 512, 256), bf16),
+            ROWS,
+            ROWS,
+        ],
+        12,
+        10,
+        "qkv_grad",
+    )
 
 
 def visible_end(ends_ref, first):
@@ -239,9 +677,7 @@
         out_specs=(vmem_spec(),) * 3,
         scratch_shapes=[pltpu.VMEM((SEQ, TILE), f32), pltpu.VMEM((HEAD_DIM, SEQ), bf16)],
         compiler_params=params(),
-        cost_estimate=pl.CostEstimate(
-            flops=4 * 2048 * 2048 * 128, bytes_accessed=4 << 20, transcendentals=2 << 20
-        ),
+        cost_estimate=cost(8),
         name="attend",
     )(ends, qkv)
 
@@ -294,29 +730,16 @@
         out_specs=vmem_spec(),
         scratch_shapes=[pltpu.VMEM((SEQ, HEAD_DIM), f32), pltpu.VMEM((SEQ, HEAD_DIM), f32)],
         compiler_params=params(),
-        cost_estimate=pl.CostEstimate(
-            flops=10 * 2048 * 2048 * 128, bytes_accessed=8 << 20, transcendentals=2 << 20
-        ),
+        cost_estimate=cost(15),
         name="attend_back",
     )(ends, qkv, grad, out, lse, cosine, sine)
 
 
-def gather_weight(shard):
-    along_z = jnp.concatenate(gather4(shard, "z"), axis=1)
-    own, near1, far, near3 = gather4(along_z, "y")
-    mine = jnp.stack(
-        [jnp.concatenate([own, far], axis=1), jnp.concatenate([near1, near3], axis=1)], axis=0
-    )
-    return mine, swap(mine, "c", 1)
-
-
-def scatter_weight(grad):
-    got = swap(grad[:, :, 1024:], "c", 1)
-    mine = (grad[:, :, :1024].astype(f32) + got.astype(f32)).astype(bf16)
-    along_y = scatter4(
-        [mine[0, :, :512], mine[1, :, :512], mine[0, :, 512:], mine[1, :, 512:]], "y"
-    ).astype(bf16)
-    return scatter4([along_y[:, b * 128 : (b + 1) * 128] for b in range(4)], "z")
+PLANE = ("yl", "yh", "z")
+
+
+def plane_exchange(value):
+    return lax.all_to_all(value, PLANE, split_axis=0, concat_axis=0, tiled=True)
 
 
 def rotary(count):
@@ -373,119 +796,114 @@
     sequence = (x ^ (blk >> 2)) * 2 + yl
     ends = jnp.cumsum(lax.dynamic_slice_in_dim(block_lengths, sequence, 1, 0)[0])
 
-    normed1, tok, dy = prepare(place, tokens[0], output_grad[0], first_gain)
-    tok = tok.astype(f32)
+    normed1, tok_low, dy = prepare(place, tokens[0], output_grad[0], first_gain)
+    tok = tok_low.astype(f32)
+    blkaxes = ("yh", "z", "c")
+
+    def exchange(value):
+        return lax.all_to_all(value, blkaxes, split_axis=0, concat_axis=0, tiled=True)
+
+    shard1 = jnp.concatenate(
+        [query_weight.T, key_weight.T, value_weight.T, out_weight], axis=0
+    )
+    shard_a = jnp.concatenate([gate_weight.T, up_weight.T[:336]], axis=0)
+    shard_b = jnp.concatenate([up_weight.T[336:], down_weight], axis=0)
+    source = ((yl ^ (rel >> 3)) * 2 + (yh ^ ((rel >> 2) & 1))) * 4 + (z ^ (rel & 3))
+
     rows1 = gather4(normed1, "x")
-    shard1 = jnp.concatenate([query_weight.T, key_weight.T, value_weight.T], axis=0)
-    mine1, theirs1 = gather_weight(shard1)
-    shard2 = jnp.concatenate([out_weight, gate_weight.T, up_weight.T, down_weight], axis=0)
-    mine2, theirs2 = gather_weight(shard2)
-    weight1 = jnp.concatenate([mine1, theirs1], axis=2)
-    weight2 = jnp.concatenate([mine2, theirs2], axis=2)
-    w_out, w_gate, w_up, w_down = (
-        weight2[:, :256],
-        weight2[:, 256:944],
-        weight2[:, 944:1632],
-        weight2[:, 1632:],
-    )
-
-    blkaxes = ("yh", "z", "c")
-    qkv_own = project_qkv(rows1, mine1, theirs1, own_cosine, own_sine)
-    qkv = lax.all_to_all(
-        qkv_own.reshape(16, 3, 128, 128), blkaxes, split_axis=0, concat_axis=0, tiled=True
-    )
-    low, attended, lse = attend(ends, qkv)
-    low = lax.all_to_all(low, blkaxes, split_axis=0, concat_axis=0, tiled=True)
-    low = low.reshape(4, 2, 2, 128, 128)
-    part = jnp.einsum(
-        "jshrk,shkd->jrd", low, w_out.reshape(2, 2, 128, 2048), preferred_element_type=f32
-    ).astype(bf16)
-    residual = tok + scatter4(list(part), "x")
+    dy_rows = gather4(after(dy, rows1[4]), "x")
+    mine = plane_exchange(jnp.broadcast_to(shard1[None], (16,) + shard1.shape))
+    mine = after(mine, *rows1[2:4], *dy_rows[2:4], cosine, sine)
+    w_attn = (mine, swap(mine, "c", 1))
+
+    orders = "zy", "yz"
+    shards = after(shard_a, mine), after(shard_b, mine)
+    near = [[swap(v, o[0], 1), swap(v, o[0], 3)] for v, o in zip(shards, orders)]
+    rows1 = (after(rows1[0], *near[0], *near[1]),) + rows1[1:]
+    far = [swap(n[1], o[0], 1) for n, o in zip(near, orders)]
+    qkv = exchange(after(project_qkv(source, rows1, w_attn, own_cosine, own_sine), *far))
+    plane = [stacked((v, n[0], f, n[1])) for v, n, f in zip(shards, near, far)]
+    tok_rows = gather4(after(tok_low, mine), "x")
+    low, attended, lse = attend(ends, after(qkv, *plane, *tok_rows[2:4]))
+    low = exchange(low)
+    near = [[swap(v, o[1], 1), swap(v, o[1], 3)] for v, o in zip(plane, orders)]
+    part = project_out(source, after(low, *near[0], *near[1]), w_attn)
+    residual = tok + scatter4([[part[k]] for k in range(4)], "x")
+    groups = [gather_far(v, n, o[1]) for v, n, o in zip(plane, near, orders)]
+    w_mlp = []
+    for group in groups:
+        held = [after(piece, residual) for piece in group]
+        w_mlp += [*group, *(swap(piece, "c", 1) for piece in held)]
     inverse2 = inverse_rms(residual)
     normed2 = (residual * inverse2 * second_gain).astype(bf16)
-
-    dy_rows = jnp.concatenate(gather4(dy, "x"), axis=0)
-    rows2 = jnp.concatenate(gather4(normed2, "x"), axis=0)
-    gate = jnp.einsum("md,srd->smr", rows2, w_gate, preferred_element_type=f32)
-    up = jnp.einsum("md,srd->smr", rows2, w_up, preferred_element_type=f32)
-    sigmoid = jax.nn.sigmoid(gate)
-    silu = gate * sigmoid
-    hidden = (silu * up).astype(bf16)
-    d_hidden = jnp.einsum("md,srd->smr", dy_rows, w_down, preferred_element_type=f32)
-    d_gate = (d_hidden * up * sigmoid * (1.0 + gate * (1.0 - sigmoid))).astype(bf16)
-    d_up = (d_hidden * silu).astype(bf16)
-    part = (
-        jnp.einsum("smr,srd->md", d_gate, w_gate, preferred_element_type=f32)
-        + jnp.einsum("smr,srd->md", d_up, w_up, preferred_element_type=f32)
-    ).astype(bf16)
-    d_normed2 = scatter4(list(part.reshape(4, 128, 2048)), "x")
+    rows2 = gather4(normed2, "x")
+    hidden, d_gate, d_up, part = mlp(rows2, dy_rows, w_mlp)
+
+    far = scatter_far([part[2]], "x")
+    near1, near3 = scatter_near([part[1]], [part[3]], far, "x")
+    mlp_mine, mlp_theirs = mlp_grad(after(d_gate, *far), d_up, hidden, rows2, dy_rows)
+    d_normed2 = add(part[0], after(near1, mlp_mine), near3)
     back2, second_part = norm_back(d_normed2, residual, inverse2, second_gain)
     d_residual = dy.astype(f32) + back2
     d_attn = d_residual.astype(bf16)
-    rows3 = jnp.concatenate(gather4(d_attn, "x"), axis=0)
-
-    part = jnp.einsum("smr,srd->md", hidden, w_down, preferred_element_type=f32).astype(bf16)
-    output = (residual + scatter4(list(part.reshape(4, 128, 2048)), "x")).astype(bf16)
-    layer_output = restore(place, output)[None]
-
-    d_out = jnp.einsum(
-        "jrd,shkd->jshrk",
-        rows3.reshape(4, 128, 2048),
-        w_out.reshape(2, 2, 128, 2048),
-        preferred_element_type=f32,
-    ).astype(bf16)
-    d_out = lax.all_to_all(
-        d_out.reshape(16, 128, 128), blkaxes, split_axis=0, concat_axis=0, tiled=True
-    )
+    rows3 = gather4(d_attn, "x")
+
+    mlp_got = swap(after(mlp_theirs, d_attn), "c", 1)
+    rows3 = (after(rows3[0], mlp_got),) + rows3[1:]
+    d_out = out_back(source, rows3, w_attn)
+    mlp_mine = after(mlp_mine, d_out)
+    sums = far_sums(pairs(mlp_mine, mlp_got)[2])
+    d_out = exchange(d_out)
+    d_out = after(d_out, *sums)
+    far = swap(sums[0], "y", 1), swap(sums[1], "y", 3)
     dqkv = attend_back(ends, qkv, d_out, attended, lse, cosine, sine)
-
-    grad_gate = jnp.einsum("smr,md->srd", d_gate, rows2, preferred_element_type=f32).astype(bf16)
-    grad_up = jnp.einsum("smr,md->srd", d_up, rows2, preferred_element_type=f32).astype(bf16)
-    grad_down = jnp.einsum("smr,md->srd", hidden, dy_rows, preferred_element_type=f32).astype(bf16)
-    grad_out = (
-        jnp.einsum(
-            "jshrk,jrd->shkd", low, rows3.reshape(4, 128, 2048), preferred_element_type=f32
-        )
-        .astype(bf16)
-        .reshape(2, 256, 2048)
-    )
-    grads2 = scatter_weight(jnp.concatenate([grad_out, grad_gate, grad_up, grad_down], axis=1))
-
-    dqkv = lax.all_to_all(dqkv, blkaxes, split_axis=0, concat_axis=0, tiled=True)
-    dqkv = dqkv.reshape(4, 2, 2, 3, 128, 128)
-    part = jnp.einsum(
-        "jshtrk,sthkd->jrd",
-        dqkv,
-        weight1.reshape(2, 3, 2, 128, 2048),
-        preferred_element_type=f32,
-    ).astype(bf16)
-    d_normed1 = scatter4(list(part), "x")
-    rows1_all = jnp.stack(rows1, axis=0)
-    grad1 = (
-        jnp.einsum("jshtrk,jrd->sthkd", dqkv, rows1_all, preferred_element_type=f32)
-        .astype(bf16)
-        .reshape(2, 768, 2048)
-    )
-    grads1 = scatter_weight(grad1)
-    back1, first_part = norm_back(d_normed1, tok, inverse_rms(tok), first_gain)
-    input_grad = restore(place, d_residual + back1)[None]
-
+    terms = pairs(after(mlp_mine, dqkv), mlp_got)
+    sums = near_sums(terms[1], terms[3], far)
+    down_part = project_down(after(hidden, dqkv), w_mlp)
+    dqkv = exchange(dqkv)
+    dqkv = after(dqkv, *sums, down_part)
+    near = swap(sums[0], "y", 1), swap(sums[1], "y", 3)
+
+    qkv_mine, qkv_theirs = qkv_grad(dqkv, low, rows1, rows3)
+    qkv_got = swap(qkv_theirs, "c", 1)
+    part, first_part = qkv_back(source, after(dqkv, qkv_mine), w_attn, tok_rows)
+    sums = far_sums(pairs(qkv_mine, qkv_got)[2])
+    qkv_far = swap(sums[0], "z", 1), swap(sums[1], "z", 3)
+    part = after(part, *sums)
+    far = scatter_far([part[2]], "x")
+    qkv_terms = pairs(after(qkv_mine, *far), qkv_got)
+    sums = near_sums(qkv_terms[1], qkv_terms[3], qkv_far)
+    qkv_near = swap(sums[0], "z", 1), swap(sums[1], "z", 3)
+    d_near = scatter_near([part[1]], [part[3]], far, "x", sums[:1])
+    d_normed1 = add(part[0], *d_near)
+    down_part = after(down_part, *sums)
+    output = residual + scatter4([[down_part[k]] for k in range(4)], "x")
+    layer_output = restore(place, output.astype(bf16))[None]
+    back1, _ = norm_back(d_normed1, tok, inverse_rms(tok), first_gain)
+    input_grad = d_residual + back1
+    along = add(*terms[0], *(after(v, *sums) for v in near)).astype(bf16)
+    grad_mlp = scatter4([[along[k]] for k in range(4)], "z")
+    along = add(*qkv_terms[0], *qkv_near).astype(bf16)
+    grad_qkv = scatter4([[along[k]] for k in range(4)], "y")
+
+    first_part = jnp.sum(after(first_part, *sums), axis=0)
     gains = jnp.concatenate([absolute(first_part), absolute(second_part)], axis=0)
-    for axis in ("x", "y", "z"):
-        gains = total4(gains, axis)
+    gains = total4(total4(gains, "x"), "y")
+    gains = total4(after(gains, input_grad, *qkv_near), "z")
     gains = gains + swap(gains, "c", 1)
+    input_grad = restore(place, input_grad)[None]
     return (
         layer_output,
         input_grad,
         gains[:16].reshape(2048),
-        grads1[:256].T,
-        grads1[256:512].T,
-        grads1[512:].T,
-        grads2[:256],
+        grad_qkv[:256].T,
+        grad_qkv[256:512].T,
+        grad_qkv[512:768].T,
+        grad_qkv[768:],
         gains[16:].reshape(2048),
-        grads2[256:944].T,
-        grads2[944:1632].T,
-        grads2[1632:],
+        grad_mlp[:688].T,
+        grad_mlp[688:1376].T,
+        grad_mlp[1376:],
     )
 
 

time: 791 us -> 555 us (0.70)
  waiting for transfers between devices: 390 us -> 217 us
  Pallas kernels: 39.3 us -> 129 us
  other arithmetic: 121 us -> 46 us
  matrix products: 59.4 us -> 0 us
  blocking collectives: 18.1 us -> 0 us
    ppermute x78 -> x89, waiting for transfers between devices: 339 us -> 197 us  [swap(): return lax.ppermute(value, names, [(i, i ^ step) for i in range(count)])]
    pallas_call x1 -> x10, Pallas kernels: 8.98 us -> 98.6 us  [the longest x8 94.2 us: kernel_call(): pl.pallas_call(kernel, out_shape=out_shape, in_specs=[smem_spec()] * smem...]
    dot_general x14 -> x0, matrix products: 59.4 us -> none  [the longest x1 7.02 us: on_device(): jnp.einsum('md,srd->smr', dy_rows, w_down, preferred_element_type=f32)]
    concatenate x23 -> x19, other arithmetic: 68.3 us -> 10.6 us  [the longest x8 5.31 us: near_sums(): jnp.concatenate([add(*[term[:half] for term in part1]).astype(bf16), add(...]
    all_to_all x3 -> x5, waiting for transfers between devices: 50.9 us -> 19.3 us  [the longest x4 11.2 us: exchange(): lax.all_to_all(value, blkaxes, split_axis=0, concat_axis=0, tiled=True)]
    all_to_all x1 -> x0, blocking collectives: 18.1 us -> none  [on_device(): lax.all_to_all(d_out.reshape(16, 128, 128), blkaxes, split_axis=0, concat...]
    all_to_all x3 -> x5, starting transfers between devices: 13.3 us -> 27.3 us  [the longest x4 18.7 us: exchange(): lax.all_to_all(value, blkaxes, split_axis=0, concat_axis=0, tiled=True)]
    another operation x5 -> x1, other arithmetic: 13.8 us -> 0.69 us  [the longest x4 13.1 us: gather_weight(): jnp.stack([jnp.concatenate([own, far], axis=1), jnp.concatenate([near1, n...]
  transfers between devices with their start and end apart: 81 -> 94, of which waited for: 55 -> 47; matrix products, arithmetic and copies ran while one was open for 14% -> 9% of each run, Pallas kernels for 5% -> 14%
where the time goes in v2:
time: 555 us; the launch traced here: 544 us
  waiting for transfers between devices  217 us (39%)
  Pallas kernels  129 us (23%)
  starting transfers between devices  122 us (22%)
  other arithmetic  46 us (8%)
  local copies, waits for them, and re-layouts  28.1 us (5%)
    ppermute x89, waiting for transfers between devices, swap(): return lax.ppermute(value, names, [(i, i ^ step) for i in range(count)])  197 us
    ppermute x89, starting transfers between devices, swap(): return lax.ppermute(value, names, [(i, i ^ step) for i in range(count)])  95.2 us
    pallas_call x8, Pallas kernels, kernel_call(): pl.pallas_call(kernel, out_shape=out_shape, in_specs=[smem_spec()] * smem...  94.2 us
    all_to_all x4, starting transfers between devices, exchange(): lax.all_to_all(value, blkaxes, split_axis=0, concat_axis=0, tiled=True)  18.7 us
    pallas_call x1, Pallas kernels, attend_back(): pl.pallas_call(attend_back_kernel, out_shape=jax.ShapeDtypeStruct((16, 3,...  15.5 us
    unnamed x140, local copies, waits for them, and re-layouts  14.7 us
    all_to_all x4, waiting for transfers between devices, exchange(): lax.all_to_all(value, blkaxes, split_axis=0, concat_axis=0, tiled=True)  11.2 us
  transfers between devices with their start and end apart: 94, of which 47 were waited for; matrix products, arithmetic and copies ran while one was open for 9% of the time, Pallas kernels for 14%

profile of v2, /device:TPU:8, one launch (start us, length us, event | category | flops | bytes accessed | tf_op | source)
XLA Modules:
  0.0 544.5 jit_solution(16746531850374437287)
XLA Ops:
  4.4 2.9 broadcast_in_dim.99
  7.3 8.5 %all-to-all-start = ((bf16[16,1024,128]{2,1,0:T(8,128)(2,1)}), bf16[16,1024,128]{2,1,0:T(8,128)(2,1)}, u32[]{:S(2)}, u32[]{:S(2)}) async-start(bf16[16,1024,128]{2,1,0:T(8,128)(2,1)} %broadcast_in_dim.99), calls=%async_computation | async-start | bytes 8388608 | tf_op jit(solution)/shard_map/all_to_all | solution.py:742
  22.9 11.5 %collective-permute-done.refs_4_ = bf16[128,2048]{1,0:T(8,128)(2,1)S(1)} collective-permute-done((bf16[128,2048]{1,0:T(8,128)(2,1)}, bf16[128,2048]{1,0:T(8,128)(2,1)S(1)}, u32[]{:S(2)}, u32[]{:S(2)}) %collective-permute-start) | collective-permute-done | bytes 524320 | tf_op jit(solution)/shard_map/ppermute | solution.py:30
  40.0 10.7 %collective-permute-done.4.refs_9_ = bf16[128,2048]{1,0:T(8,128)(2,1)S(1)} collective-permute-done((bf16[128,2048]{1,0:T(8,128)(2,1)}, bf16[128,2048]{1,0:T(8,128)(2,1)S(1)}, u32[]{:S(2)}, u32[]{:S(2)}) %collective-permute-start.4) | collective-permute-done | bytes 524320 | tf_op jit(solution)/shard_map/ppermute | solution.py:30
  54.3 3.7 fusion.10
  61.3 8.1 %all-to-all-done.refs_5_.mine_ref = bf16[16,1024,128]{2,1,0:T(8,128)(2,1)} async-done(((bf16[16,1024,128]{2,1,0:T(8,128)(2,1)}), bf16[16,1024,128]{2,1,0:T(8,128)(2,1)}, u32[]{:S(2)}, u32[]{:S(2)}) %all-to-all-start) | async-done | bytes 4194336 | tf_op jit(solution)/shard_map/all_to_all | solution.py:742
  69.6 4.8 collective-permute-start.11
  78.4 5.9 %collective-permute-done.9.near3 = bf16[1024,128]{1,0:T(8,128)(2,1)} collective-permute-done((bf16[1024,128]{1,0:T(8,128)(2,1)S(1)}, bf16[1024,128]{1,0:T(8,128)(2,1)}, u32[]{:S(2)}, u32[]{:S(2)}) %collective-permute-start.9) | collective-permute-done | bytes 262176 | tf_op jit(solution)/shard_map/ppermute | solution.py:30
  88.2 9.9 %project_qkv.1 = bf16[16,3,128,128]{3,2,1,0:T(8,128)(2,1)} custom-call(s32[16]{0:T(128)} %multiply_add_fusion.source_ref, bf16[128,2048]{1,0:T(8,128)(2,1)} %get-tuple-element.71.refs_0_, bf16[128,2048]{1,0:T(8,128)(2,1)} %copy-done.25, bf16[64,2048]{1,0:T(8,128)(2,1)} %copy-done.57, bf16[64,2048]{1,0:T(8,128)(2,1)} %copy-done.58, ...), custom_call_target="tpu_custom_call" | custom-call | flops 11500000256 | tf_op jit(solution)/shard_map/project_qkv/pallas_call | solution.py:267
  99.6 5.7 %all-to-all-start.1 = ((bf16[16,3,128,128]{3,2,1,0:T(8,128)(2,1)}), bf16[16,3,128,128]{3,2,1,0:T(8,128)(2,1)S(1)}, u32[]{:S(2)}, u32[]{:S(2)}) async-start(bf16[16,3,128,128]{3,2,1,0:T(8,128)(2,1)} %project_qkv.1), calls=%async_computation.1 | async-start | bytes 3145728 | tf_op jit(solution)/shard_map/all_to_all | solution.py:804
  105.3 2.8 collective-permute-start.15
  109.1 11.8 %collective-permute-done.15.refs_4_ = bf16[128,2048]{1,0:T(8,128)(2,1)S(1)} collective-permute-done((bf16[128,2048]{1,0:T(8,128)(2,1)S(1)}, bf16[128,2048]{1,0:T(8,128)(2,1)S(1)}, u32[]{:S(2)}, u32[]{:S(2)}) %collective-permute-start.15) | collective-permute-done | bytes 524320 | tf_op jit(solution)/shard_map/ppermute | solution.py:30
  137.0 7.8 %attend.1 = (bf16[16,128,128]{2,1,0:T(8,128)(2,1)}, f32[2048,128]{1,0:T(8,128)}, f32[1,2048]{1,0:T(1,128)}) custom-call(s32[12]{0:T(128)} %bitcast.242, bf16[16,3,128,128]{3,2,1,0:T(8,128)(2,1)} %copy-done.10), custom_call_target="tpu_custom_call" | custom-call | flops 9200000000 | tf_op jit(solution)/shard_map/attend/pallas_call | solution.py:669
  144.8 4.0 all-to-all-start.2
  148.8 3.5 collective-permute-done.19.refs_11_.refs_1_
  153.3 7.7 %collective-permute-done.21.refs_21_.refs_11_ = bf16[4,1040,128]{2,1,0:T(8,128)(2,1)} collective-permute-done((bf16[4,1040,128]{2,1,0:T(8,128)(2,1)}, bf16[4,1040,128]{2,1,0:T(8,128)(2,1)}, u32[]{:S(2)}, u32[]{:S(2)}) %collective-permute-start.21) | collective-permute-done | bytes 1064992 | tf_op jit(solution)/shard_map/ppermute | solution.py:30
  165.1 5.2 project_out.1
  173.3 8.1 %collective-permute-done.23 = bf16[64,2048]{1,0:T(8,128)(2,1)S(1)} collective-permute-done((bf16[64,2048]{1,0:T(8,128)(2,1)S(1)}, bf16[64,2048]{1,0:T(8,128)(2,1)S(1)}, u32[]{:S(2)}, u32[]{:S(2)}) %collective-permute-start.23) | collective-permute-done | bytes 262176 | tf_op jit(solution)/shard_map/ppermute | solution.py:30
  190.5 5.6 %collective-permute-done.26 = bf16[128,2048]{1,0:T(8,128)(2,1)S(1)} collective-permute-done((bf16[128,2048]{1,0:T(8,128)(2,1)S(1)}, bf16[128,2048]{1,0:T(8,128)(2,1)S(1)}, u32[]{:S(2)}, u32[]{:S(2)}) %collective-permute-start.26) | collective-permute-done | bytes 524320 | tf_op jit(solution)/shard_map/ppermute | solution.py:30
  201.8 7.9 %collective-permute-done.39.refs_23_.refs_13_ = bf16[2,1040,128]{2,1,0:T(8,128)(2,1)S(1)} collective-permute-done((bf16[2,1040,128]{2,1,0:T(8,128)(2,1)S(1)}, bf16[2,1040,128]{2,1,0:T(8,128)(2,1)S(1)}, u32[]{:S(2)}, u32[]{:S(2)}) %collective-permute-start.39) | collective-permute-done | bytes 532512 | tf_op jit(solution)/shard_map/ppermute | solution.py:30
  214.6 6.5 %collective-permute-done.29.refs_2_ = bf16[64,2048]{1,0:T(8,128)(2,1)S(1)} collective-permute-done((bf16[64,2048]{1,0:T(8,128)(2,1)S(1)}, bf16[64,2048]{1,0:T(8,128)(2,1)S(1)}, u32[]{:S(2)}, u32[]{:S(2)}) %collective-permute-start.29) | collective-permute-done | bytes 262176 | tf_op jit(solution)/shard_map/ppermute | solution.py:30
  228.9 29.4 %mlp.1 = (bf16[2,512,688]{2,1,0:T(8,128)(2,1)}, bf16[2,512,688]{2,1,0:T(8,128)(2,1)}, bf16[2,512,688]{2,1,0:T(8,128)(2,1)}, bf16[4,128,2048]{2,1,0:T(8,128)(2,1)}) custom-call(bf16[128,2048]{1,0:T(8,128)(2,1)} %copy-done.16, bf16[128,2048]{1,0:T(8,128)(2,1)} %copy-done.30, bf16[64,2048]{1,0:T(8,128)(2,1)} %copy-done.63, bf16[64,2048]{1,0:T(8,128)(2,1)} %copy-done.65, ...), custom_call_target="tpu_custom_call" | custom-call | flops 32199999488 | tf_op jit(solution)/shard_map/mlp/pallas_call | solution.py:267
  260.9 8.5 %collective-permute-done.45 = bf16[64,2048]{1,0:T(8,128)(2,1)S(1)} collective-permute-done((bf16[64,2048]{1,0:T(8,128)(2,1)S(1)}, bf16[64,2048]{1,0:T(8,128)(2,1)S(1)}, u32[]{:S(2)}, u32[]{:S(2)}) %collective-permute-start.45) | collective-permute-done | bytes 262176 | tf_op jit(solution)/shard_map/ppermute | solution.py:30
  271.6 16.7 %mlp_grad.1 = (bf16[4,4,2064,128]{3,2,1,0:T(8,128)(2,1)}, bf16[4,4,2064,128]{3,2,1,0:T(8,128)(2,1)}) custom-call(bf16[2,512,688]{2,1,0:T(8,128)(2,1)} %get-tuple-element.90.d_gate_ref, bf16[2,512,688]{2,1,0:T(8,128)(2,1)} %get-tuple-element.91.d_up_ref, bf16[2,512,688]{2,1,0:T(8,128)(2,1)} %get-tuple-element.101.hidden_ref, bf16[128,2048]{1,0:T(8,128)(2,1)} %copy-done.16, ...), custom_call_target="tpu_custom_call" | custom-call | flops 20700000256 | tf_op jit(solution)/shard_map/mlp_grad/pallas_call | solution.py:267
  292.9 12.6 %collective-permute-done.51.refs_4_.refs_9_ = bf16[128,2048]{1,0:T(8,128)(2,1)S(1)} collective-permute-done((bf16[128,2048]{1,0:T(8,128)(2,1)S(1)}, bf16[128,2048]{1,0:T(8,128)(2,1)S(1)}, u32[]{:S(2)}, u32[]{:S(2)}) %collective-permute-start.51) | collective-permute-done | bytes 524320 | tf_op jit(solution)/shard_map/ppermute | solution.py:30
  307.9 5.5 %collective-permute-done.52.refs_2_.refs_7_ = bf16[64,2048]{1,0:T(8,128)(2,1)S(1)} collective-permute-done((bf16[64,2048]{1,0:T(8,128)(2,1)S(1)}, bf16[64,2048]{1,0:T(8,128)(2,1)S(1)}, u32[]{:S(2)}, u32[]{:S(2)}) %collective-permute-start.52) | collective-permute-done | bytes 262176 | tf_op jit(solution)/shard_map/ppermute | solution.py:30
  315.9 6.3 %out_back.1 = bf16[16,128,128]{2,1,0:T(8,128)(2,1)} custom-call(s32[16]{0:T(128)} %multiply_add_fusion.source_ref, bf16[128,2048]{1,0:T(8,128)(2,1)} %copy-done.18, bf16[128,2048]{1,0:T(8,128)(2,1)} %copy-done.33, bf16[64,2048]{1,0:T(8,128)(2,1)} %copy-done.62, bf16[64,2048]{1,0:T(8,128)(2,1)} %copy-done.64, bf16[128,2048]{1,0:T(8,128)(2,1)} %copy-done.32, ...), custom_call_target="tpu_custom_call" | custom-call | flops 6899999744 | tf_op jit(solution)/shard_map/out_back/pallas_call | solution.py:267
  322.3 4.4 all-to-all-start.3
  326.7 4.1 fusion.7
  334.8 4.3 all-to-all-done.3.grad_ref
  339.1 15.5 %attend_back.1 = bf16[16,3,128,128]{3,2,1,0:T(8,128)(2,1)} custom-call(s32[12]{0:T(128)} %bitcast.243, bf16[16,3,128,128]{3,2,1,0:T(8,128)(2,1)} %copy-done.10, bf16[16,128,128]{2,1,0:T(8,128)(2,1)} %all-to-all-done.3.grad_ref, f32[2048,128]{1,0:T(8,128)} %get-tuple-element.99.out_ref, f32[1,2048]{1,0:T(1,128)} %get-tuple-element.100.lse_ref, ...), custom_call_target="tpu_custom_call" | custom-call | flops 17250000896 | tf_op jit(solution)/shard_map/attend_back/pallas_call | solution.py:726
  354.6 4.6 all-to-all-start.4
  362.0 8.1 %project_down.1 = bf16[4,128,2048]{2,1,0:T(8,128)(2,1)} custom-call(bf16[2,512,688]{2,1,0:T(8,128)(2,1)} %get-tuple-element.101.hidden_ref, bf16[4,1024,128]{2,1,0:T(8,128)(2,1)} %stack.2.refs_10_.refs_0_, bf16[4,1024,128]{2,1,0:T(8,128)(2,1)} %collective-permute-done.19.refs_11_.refs_1_, bf16[2,1024,128]{2,1,0:T(8,128)(2,1)} %copy-done.51, ...), custom_call_target="tpu_custom_call" | custom-call | flops 9200000000 | tf_op jit(solution)/shard_map/project_down/pallas_call | solution.py:267
  370.1 3.5 fusion.2
  376.7 6.3 %all-to-all-done.4.dqkv_ref = bf16[16,3,128,128]{3,2,1,0:T(8,128)(2,1)} async-done(((bf16[16,3,128,128]{3,2,1,0:T(8,128)(2,1)}), bf16[16,3,128,128]{3,2,1,0:T(8,128)(2,1)}, u32[]{:S(2)}, u32[]{:S(2)}) %all-to-all-start.4) | async-done | bytes 1572896 | tf_op jit(solution)/shard_map/all_to_all | solution.py:804
  383.0 9.2 %qkv_grad.1 = (bf16[4,4,1024,128]{3,2,1,0:T(8,128)(2,1)}, bf16[4,4,1024,128]{3,2,1,0:T(8,128)(2,1)}) custom-call(bf16[16,3,128,128]{3,2,1,0:T(8,128)(2,1)} %all-to-all-done.4.dqkv_ref, bf16[16,128,128]{2,1,0:T(8,128)(2,1)} %copy-done.14, bf16[128,2048]{1,0:T(8,128)(2,1)} %get-tuple-element.71.refs_0_, bf16[128,2048]{1,0:T(8,128)(2,1)} %copy-done.25, ...), custom_call_target="tpu_custom_call" | custom-call | flops 11500000256 | tf_op jit(solution)/shard_map/qkv_grad/pallas_call | solution.py:267
  392.7 9.4 %qkv_back.1 = (bf16[4,128,2048]{2,1,0:T(8,128)(2,1)}, f32[8,2048]{1,0:T(8,128)}) custom-call(s32[16]{0:T(128)} %multiply_add_fusion.source_ref, bf16[16,3,128,128]{3,2,1,0:T(8,128)(2,1)} %all-to-all-done.4.dqkv_ref, bf16[16,1024,128]{2,1,0:T(8,128)(2,1)} %all-to-all-done.refs_5_.mine_ref, bf16[16,1024,128]{2,1,0:T(8,128)(2,1)} %collective-permute-done.12.refs_6_.theirs_ref, ...), custom_call_target="tpu_custom_call" | custom-call | flops 13799999488 | tf_op jit(solution)/shard_map/qkv_back/pallas_call | solution.py:267
  408.4 4.4 collective-permute-done.57
  422.2 5.5 %collective-permute-done.59 = bf16[2,1024,128]{2,1,0:T(8,128)(2,1)S(1)} collective-permute-done((bf16[2,1024,128]{2,1,0:T(8,128)(2,1)S(1)}, bf16[2,1024,128]{2,1,0:T(8,128)(2,1)S(1)}, u32[]{:S(2)}, u32[]{:S(2)}) %collective-permute-start.59) | collective-permute-done | bytes 524320 | tf_op jit(solution)/shard_map/ppermute | solution.py:30
  434.9 19.2 %collective-permute-done.84 = bf16[4,2064,128]{2,1,0:T(8,128)(2,1)} collective-permute-done((bf16[4,2064,128]{2,1,0:T(8,128)(2,1)}, bf16[4,2064,128]{2,1,0:T(8,128)(2,1)}, u32[]{:S(2)}, u32[]{:S(2)}) %collective-permute-start.84) | collective-permute-done | bytes 2113568 | tf_op jit(solution)/shard_map/ppermute | solution.py:30
  455.2 4.6 fusion.1
  459.9 2.8 collective-permute-start.85
  462.7 2.9 collective-permute-start.71
  474.5 4.4 collective-permute-done.61
  483.6 13.0 %collective-permute-done.87 = bf16[1040,128]{1,0:T(8,128)(2,1)S(1)} collective-permute-done((bf16[1040,128]{1,0:T(8,128)(2,1)S(1)}, bf16[1040,128]{1,0:T(8,128)(2,1)S(1)}, u32[]{:S(2)}, u32[]{:S(2)}) %collective-permute-start.87) | collective-permute-done | bytes 266272 | tf_op jit(solution)/shard_map/ppermute | solution.py:30
  504.4 4.4 collective-permute-done.64
  514.7 5.4 collective-permute-done.88
  526.6 2.8 collective-permute-start.79
  (387 shorter events, 181.7 us)
Async XLA Ops:
  7.3 62.1 %all-to-all-start = ((bf16[16,1024,128]{2,1,0:T(8,128)(2,1)}), bf16[16,1024,128]{2,1,0:T(8,128)(2,1)}, u32[]{:S(2)}, u32[]{:S(2)}) async-start(bf16[16,1024,128]{2,1,0:T(8,128)(2,1)} %broadcast_in_dim.99), calls=%async_computation | async-start | bytes 8388608 | tf_op jit(solution)/shard_map/all_to_all | solution.py:742
  19.9 14.5 %collective-permute-start = (bf16[128,2048]{1,0:T(8,128)(2,1)}, bf16[128,2048]{1,0:T(8,128)(2,1)S(1)}, u32[]{:S(2)}, u32[]{:S(2)}) collective-permute-start(bf16[128,2048]{1,0:T(8,128)(2,1)} %get-tuple-element.71.refs_0_), channel_id=1, source_target_pairs={{0,96},{32,64},{64,32},{96,0},{1,97},{33,65},{65,33},{97,1},{2,98}... | collective-permute-start | bytes 1572872 | tf_op jit(solution)/shard_map/ppermute | solution.py:30
  22.6 16.7 %collective-permute-start.2 = (bf16[128,2048]{1,0:T(8,128)(2,1)}, bf16[128,2048]{1,0:T(8,128)(2,1)S(1)}, u32[]{:S(2)}, u32[]{:S(2)}) collective-permute-start(bf16[128,2048]{1,0:T(8,128)(2,1)} %get-tuple-element.71.refs_0_), channel_id=1, source_target_pairs={{0,32},{32,0},{64,96},{96,64},{1,33},{33,1},{65,97},{97,65},{2,34}... | collective-permute-start | bytes 1572872 | tf_op jit(solution)/shard_map/ppermute | solution.py:30
  34.4 16.3 %collective-permute-start.4 = (bf16[128,2048]{1,0:T(8,128)(2,1)}, bf16[128,2048]{1,0:T(8,128)(2,1)S(1)}, u32[]{:S(2)}, u32[]{:S(2)}) collective-permute-start(bf16[128,2048]{1,0:T(8,128)(2,1)} %get-tuple-element.67.refs_5_), channel_id=1, source_target_pairs={{0,96},{32,64},{64,32},{96,0},{1,97},{33,65},{65,33},{97,1},{2,98}... | collective-permute-start | bytes 1572872 | tf_op jit(solution)/shard_map/ppermute | solution.py:30
  37.2 15.1 %collective-permute-start.6 = (bf16[128,2048]{1,0:T(8,128)(2,1)}, bf16[128,2048]{1,0:T(8,128)(2,1)S(1)}, u32[]{:S(2)}, u32[]{:S(2)}) collective-permute-start(bf16[128,2048]{1,0:T(8,128)(2,1)} %get-tuple-element.67.refs_5_), channel_id=1, source_target_pairs={{0,32},{32,0},{64,96},{96,64},{1,33},{33,1},{65,97},{97,65},{2,34}... | collective-permute-start | bytes 1572872 | tf_op jit(solution)/shard_map/ppermute | solution.py:30
  37.3 20.8 %collective-permute-start.1 = (bf16[64,2048]{1,0:T(8,128)(2,1)S(1)}, bf16[64,2048]{1,0:T(8,128)(2,1)S(1)}, u32[]{:S(2)}, u32[]{:S(2)}) collective-permute-start(bf16[64,2048]{1,0:T(8,128)(2,1)S(1)} %slice.603), channel_id=1, source_target_pairs={{0,32},{32,0},{64,96},{96,64},{1,33},{33,1},{65,97},{97,65},{2,34}... | collective-permute-start | bytes 786440 | tf_op jit(solution)/shard_map/ppermute | solution.py:30
  39.4 18.7 %collective-permute-start.3 = (bf16[64,2048]{1,0:T(8,128)(2,1)S(1)}, bf16[64,2048]{1,0:T(8,128)(2,1)S(1)}, u32[]{:S(2)}, u32[]{:S(2)}) collective-permute-start(bf16[64,2048]{1,0:T(8,128)(2,1)S(1)} %slice.604), channel_id=1, source_target_pairs={{0,96},{32,64},{64,32},{96,0},{1,97},{33,65},{65,33},{97,1},{2,98}... | collective-permute-start | bytes 786440 | tf_op jit(solution)/shard_map/ppermute | solution.py:30
  69.4 18.8 %collective-permute-start.12 = (bf16[16,1024,128]{2,1,0:T(8,128)(2,1)}, bf16[16,1024,128]{2,1,0:T(8,128)(2,1)}, u32[]{:S(2)}, u32[]{:S(2)}) collective-permute-start(bf16[16,1024,128]{2,1,0:T(8,128)(2,1)} %all-to-all-done.refs_5_.mine_ref), channel_id=1, source_target_pairs={{0,1},{1,0},{2,3},{3,2},{4,5},{5,4},{6,7},{7,6},{8,9},{9,8},{10,11... | collective-permute-start | bytes 12582920 | tf_op jit(solution)/shard_map/ppermute | solution.py:30
  69.5 16.2 %collective-permute-start.10 = (bf16[1040,128]{1,0:T(8,128)(2,1)S(1)}, bf16[1040,128]{1,0:T(8,128)(2,1)S(1)}, u32[]{:S(2)}, u32[]{:S(2)}) collective-permute-start(bf16[1040,128]{1,0:T(8,128)(2,1)S(1)} %pad_maximum_fusion.14.own), channel_id=1, source_target_pairs={{0,16},{8,24},{16,0},{24,8},{1,17},{9,25},{17,1},{25,9},{2,18},{10... | collective-permute-start | bytes 798728 | tf_op jit(solution)/shard_map/ppermute | solution.py:30
  69.6 16.8 %collective-permute-start.11 = (bf16[1040,128]{1,0:T(8,128)(2,1)S(1)}, bf16[1040,128]{1,0:T(8,128)(2,1)}, u32[]{:S(2)}, u32[]{:S(2)}) collective-permute-start(bf16[1040,128]{1,0:T(8,128)(2,1)S(1)} %pad_maximum_fusion.14.own), channel_id=1, source_target_pairs={{0,24},{8,16},{16,8},{24,0},{1,25},{9,17},{17,9},{25,1},{2,26},{10... | collective-permute-start | bytes 798728 | tf_op jit(solution)/shard_map/ppermute | solution.py:30
  84.3 13.9 %collective-permute-start.13 = (bf16[1024,128]{1,0:T(8,128)(2,1)}, bf16[1024,128]{1,0:T(8,128)(2,1)S(1)}, u32[]{:S(2)}, u32[]{:S(2)}) collective-permute-start(bf16[1024,128]{1,0:T(8,128)(2,1)} %collective-permute-done.9.near3), channel_id=1, source_target_pairs={{0,2},{2,0},{4,6},{6,4},{1,3},{3,1},{5,7},{7,5},{8,10},{10,8},{12,... | collective-permute-start | bytes 786440 | tf_op jit(solution)/shard_map/ppermute | solution.py:30
  99.6 36.2 %all-to-all-start.1 = ((bf16[16,3,128,128]{3,2,1,0:T(8,128)(2,1)}), bf16[16,3,128,128]{3,2,1,0:T(8,128)(2,1)S(1)}, u32[]{:S(2)}, u32[]{:S(2)}) async-start(bf16[16,3,128,128]{3,2,1,0:T(8,128)(2,1)} %project_qkv.1), calls=%async_computation.1 | async-start | bytes 3145728 | tf_op jit(solution)/shard_map/all_to_all | solution.py:804
  105.3 15.5 %collective-permute-start.15 = (bf16[128,2048]{1,0:T(8,128)(2,1)S(1)}, bf16[128,2048]{1,0:T(8,128)(2,1)S(1)}, u32[]{:S(2)}, u32[]{:S(2)}) collective-permute-start(bf16[128,2048]{1,0:T(8,128)(2,1)S(1)} %copy-done.2), channel_id=1, source_target_pairs={{0,96},{32,64},{64,32},{96,0},{1,97},{33,65},{65,33},{97,1},{2,98}... | collective-permute-start | bytes 1572872 | tf_op jit(solution)/shard_map/ppermute | solution.py:30
  108.2 14.0 %collective-permute-start.17 = (bf16[128,2048]{1,0:T(8,128)(2,1)S(1)}, bf16[128,2048]{1,0:T(8,128)(2,1)S(1)}, u32[]{:S(2)}, u32[]{:S(2)}) collective-permute-start(bf16[128,2048]{1,0:T(8,128)(2,1)S(1)} %copy-done.2), channel_id=1, source_target_pairs={{0,32},{32,0},{64,96},{96,64},{1,33},{33,1},{65,97},{97,65},{2,34}... | collective-permute-start | bytes 1572872 | tf_op jit(solution)/shard_map/ppermute | solution.py:30
  122.2 13.6 %collective-permute-start.18 = (bf16[64,2048]{1,0:T(8,128)(2,1)S(1)}, bf16[64,2048]{1,0:T(8,128)(2,1)}, u32[]{:S(2)}, u32[]{:S(2)}) collective-permute-start(bf16[64,2048]{1,0:T(8,128)(2,1)S(1)} %slice.609), channel_id=1, source_target_pairs={{0,96},{32,64},{64,32},{96,0},{1,97},{33,65},{65,33},{97,1},{2,98}... | collective-permute-start | bytes 786440 | tf_op jit(solution)/shard_map/ppermute | solution.py:30
  126.1 26.2 %collective-permute-start.19 = (bf16[4,1024,128]{2,1,0:T(8,128)(2,1)}, bf16[4,1024,128]{2,1,0:T(8,128)(2,1)}, u32[]{:S(2)}, u32[]{:S(2)}) collective-permute-start(bf16[4,1024,128]{2,1,0:T(8,128)(2,1)} %stack.2.refs_10_.refs_0_), channel_id=1, source_target_pairs={{0,16},{8,24},{16,0},{24,8},{1,17},{9,25},{17,1},{25,9},{2,18},{10... | collective-permute-start | bytes 3145736 | tf_op jit(solution)/shard_map/ppermute | solution.py:30
  128.8 24.5 %collective-permute-start.20 = (bf16[4,1024,128]{2,1,0:T(8,128)(2,1)}, bf16[4,1024,128]{2,1,0:T(8,128)(2,1)}, u32[]{:S(2)}, u32[]{:S(2)}) collective-permute-start(bf16[4,1024,128]{2,1,0:T(8,128)(2,1)} %stack.2.refs_10_.refs_0_), channel_id=1, source_target_pairs={{0,24},{8,16},{16,8},{24,0},{1,25},{9,17},{17,9},{25,1},{2,26},{10... | collective-permute-start | bytes 3145736 | tf_op jit(solution)/shard_map/ppermute | solution.py:30
  132.2 28.8 %collective-permute-start.21 = (bf16[4,1040,128]{2,1,0:T(8,128)(2,1)}, bf16[4,1040,128]{2,1,0:T(8,128)(2,1)}, u32[]{:S(2)}, u32[]{:S(2)}) collective-permute-start(bf16[4,1040,128]{2,1,0:T(8,128)(2,1)} %stack.3.refs_20_.refs_10_), channel_id=1, source_target_pairs={{0,2},{2,0},{4,6},{6,4},{1,3},{3,1},{5,7},{7,5},{8,10},{10,8},{12,... | collective-permute-start | bytes 3194888 | tf_op jit(solution)/shard_map/ppermute | solution.py:30
  133.7 30.0 %collective-permute-start.22 = (bf16[4,1040,128]{2,1,0:T(8,128)(2,1)}, bf16[4,1040,128]{2,1,0:T(8,128)(2,1)}, u32[]{:S(2)}, u32[]{:S(2)}) collective-permute-start(bf16[4,1040,128]{2,1,0:T(8,128)(2,1)} %stack.3.refs_20_.refs_10_), channel_id=1, source_target_pairs={{0,6},{2,4},{4,2},{6,0},{1,7},{3,5},{5,3},{7,1},{8,14},{10,12},{12... | collective-permute-start | bytes 3194888 | tf_op jit(solution)/shard_map/ppermute | solution.py:30
  144.8 19.5 %all-to-all-start.2 = ((bf16[16,128,128]{2,1,0:T(8,128)(2,1)}), bf16[16,128,128]{2,1,0:T(8,128)(2,1)S(1)}, u32[]{:S(2)}, u32[]{:S(2)}) async-start(bf16[16,128,128]{2,1,0:T(8,128)(2,1)} %get-tuple-element.75), calls=%async_computation.2 | async-start | bytes 1048576 | tf_op jit(solution)/shard_map/all_to_all | solution.py:804
  181.6 14.5 %collective-permute-start.26 = (bf16[128,2048]{1,0:T(8,128)(2,1)S(1)}, bf16[128,2048]{1,0:T(8,128)(2,1)S(1)}, u32[]{:S(2)}, u32[]{:S(2)}) collective-permute-start(bf16[128,2048]{1,0:T(8,128)(2,1)S(1)} %pad_maximum_fusion.7), channel_id=1, source_target_pairs={{0,96},{32,64},{64,32},{96,0},{1,97},{33,65},{65,33},{97,1},{2,98}... | collective-permute-start | bytes 1572872 | tf_op jit(solution)/shard_map/ppermute | solution.py:30
  183.5 14.7 %collective-permute-start.24 = (bf16[128,2048]{1,0:T(8,128)(2,1)S(1)}, bf16[128,2048]{1,0:T(8,128)(2,1)S(1)}, u32[]{:S(2)}, u32[]{:S(2)}) collective-permute-start(bf16[128,2048]{1,0:T(8,128)(2,1)S(1)} %pad_maximum_fusion.6), channel_id=1, source_target_pairs={{0,32},{32,0},{64,96},{96,64},{1,33},{33,1},{65,97},{97,65},{2,34}... | collective-permute-start | bytes 1572872 | tf_op jit(solution)/shard_map/ppermute | solution.py:30
  184.7 14.2 %collective-permute-start.31 = (bf16[2,1024,128]{2,1,0:T(8,128)(2,1)S(1)}, bf16[2,1024,128]{2,1,0:T(8,128)(2,1)S(1)}, u32[]{:S(2)}, u32[]{:S(2)}) collective-permute-start(bf16[2,1024,128]{2,1,0:T(8,128)(2,1)S(1)} %slice.619), channel_id=1, source_target_pairs={{0,16},{8,24},{16,0},{24,8},{1,17},{9,25},{17,1},{25,9},{2,18},{10... | collective-permute-start | bytes 1572872 | tf_op jit(solution)/shard_map/ppermute | solution.py:30
  196.1 13.6 %collective-permute-start.39 = (bf16[2,1040,128]{2,1,0:T(8,128)(2,1)S(1)}, bf16[2,1040,128]{2,1,0:T(8,128)(2,1)S(1)}, u32[]{:S(2)}, u32[]{:S(2)}) collective-permute-start(bf16[2,1040,128]{2,1,0:T(8,128)(2,1)S(1)} %slice.622), channel_id=1, source_target_pairs={{0,6},{2,4},{4,2},{6,0},{1,7},{3,5},{5,3},{7,1},{8,14},{10,12},{12... | collective-permute-start | bytes 1597448 | tf_op jit(solution)/shard_map/ppermute | solution.py:30
  198.9 13.3 %collective-permute-start.28 = (bf16[128,2048]{1,0:T(8,128)(2,1)S(1)}, bf16[128,2048]{1,0:T(8,128)(2,1)S(1)}, u32[]{:S(2)}, u32[]{:S(2)}) collective-permute-start(bf16[128,2048]{1,0:T(8,128)(2,1)S(1)} %multiply_convert_fusion.refs_0_), channel_id=1, source_target_pairs={{0,96},{32,64},{64,32},{96,0},{1,97},{33,65},{65,33},{97,1},{2,98}... | collective-permute-start | bytes 1572872 | tf_op jit(solution)/shard_map/ppermute | solution.py:30
  200.5 22.1 %collective-permute-start.33 = (bf16[4,1024,128]{2,1,0:T(8,128)(2,1)S(1)}, bf16[4,1024,128]{2,1,0:T(8,128)(2,1)S(1)}, u32[]{:S(2)}, u32[]{:S(2)}) collective-permute-start(bf16[4,1024,128]{2,1,0:T(8,128)(2,1)S(1)} %copy-done.44), channel_id=1, source_target_pairs={{0,1},{1,0},{2,3},{3,2},{4,5},{5,4},{6,7},{7,6},{8,9},{9,8},{10,11... | collective-permute-start | bytes 3145736 | tf_op jit(solution)/shard_map/ppermute | solution.py:30
  269.6 18.7 %collective-permute-start.48 = (bf16[128,2048]{1,0:T(8,128)(2,1)S(1)}, bf16[128,2048]{1,0:T(8,128)(2,1)S(1)}, u32[]{:S(2)}, u32[]{:S(2)}) collective-permute-start(bf16[128,2048]{1,0:T(8,128)(2,1)S(1)} %pad_maximum_fusion.9), channel_id=1, source_target_pairs={{0,96},{32,64},{64,32},{96,0},{1,97},{33,65},{65,33},{97,1},{2,98}... | collective-permute-start | bytes 1572872 | tf_op jit(solution)/shard_map/ppermute | solution.py:30
  271.5 16.8 %collective-permute-start.46 = (bf16[128,2048]{1,0:T(8,128)(2,1)S(1)}, bf16[128,2048]{1,0:T(8,128)(2,1)S(1)}, u32[]{:S(2)}, u32[]{:S(2)}) collective-permute-start(bf16[128,2048]{1,0:T(8,128)(2,1)S(1)} %pad_maximum_fusion.8), channel_id=1, source_target_pairs={{0,32},{32,0},{64,96},{96,64},{1,33},{33,1},{65,97},{97,65},{2,34}... | collective-permute-start | bytes 1572872 | tf_op jit(solution)/shard_map/ppermute | solution.py:30
  289.8 18.1 %collective-permute-start.49 = (bf16[4,4,2064,128]{3,2,1,0:T(8,128)(2,1)}, bf16[4,4,2064,128]{3,2,1,0:T(8,128)(2,1)}, u32[]{:S(2)}, u32[]{:S(2)}) collective-permute-start(bf16[4,4,2064,128]{3,2,1,0:T(8,128)(2,1)} %get-tuple-element.95), channel_id=1, source_target_pairs={{0,1},{1,0},{2,3},{3,2},{4,5},{5,4},{6,7},{7,6},{8,9},{9,8},{10,11... | collective-permute-start | bytes 25362440 | tf_op jit(solution)/shard_map/ppermute | solution.py:30
  289.9 15.5 %collective-permute-start.51 = (bf16[128,2048]{1,0:T(8,128)(2,1)S(1)}, bf16[128,2048]{1,0:T(8,128)(2,1)S(1)}, u32[]{:S(2)}, u32[]{:S(2)}) collective-permute-start(bf16[128,2048]{1,0:T(8,128)(2,1)S(1)} %get-tuple-element.96.refs_0_.refs_5_), channel_id=1, source_target_pairs={{0,96},{32,64},{64,32},{96,0},{1,97},{33,65},{65,33},{97,1},{2,98}... | collective-permute-start | bytes 1572872 | tf_op jit(solution)/shard_map/ppermute | solution.py:30
  291.4 14.9 %collective-permute-start.50 = (bf16[128,2048]{1,0:T(8,128)(2,1)S(1)}, bf16[128,2048]{1,0:T(8,128)(2,1)S(1)}, u32[]{:S(2)}, u32[]{:S(2)}) collective-permute-start(bf16[128,2048]{1,0:T(8,128)(2,1)S(1)} %get-tuple-element.96.refs_0_.refs_5_), channel_id=1, source_target_pairs={{0,32},{32,0},{64,96},{96,64},{1,33},{33,1},{65,97},{97,65},{2,34}... | collective-permute-start | bytes 1572872 | tf_op jit(solution)/shard_map/ppermute | solution.py:30
  322.3 16.9 %all-to-all-start.3 = ((bf16[16,128,128]{2,1,0:T(8,128)(2,1)}), bf16[16,128,128]{2,1,0:T(8,128)(2,1)}, u32[]{:S(2)}, u32[]{:S(2)}) async-start(bf16[16,128,128]{2,1,0:T(8,128)(2,1)} %out_back.1), calls=%async_computation.3 | async-start | bytes 1048576 | tf_op jit(solution)/shard_map/all_to_all | solution.py:804
  330.8 39.3 %collective-permute-start.55 = (bf16[2,2064,128]{2,1,0:T(8,128)(2,1)}, bf16[2,2064,128]{2,1,0:T(8,128)(2,1)S(1)}, u32[]{:S(2)}, u32[]{:S(2)}) collective-permute-start(bf16[2,2064,128]{2,1,0:T(8,128)(2,1)} %get-tuple-element.156), channel_id=1, source_target_pairs={{0,16},{8,24},{16,0},{24,8},{1,17},{9,25},{17,1},{25,9},{2,18},{10... | collective-permute-start | bytes 3170312 | tf_op jit(solution)/shard_map/ppermute | solution.py:30
  333.1 37.0 %collective-permute-start.54 = (bf16[2,2064,128]{2,1,0:T(8,128)(2,1)}, bf16[2,2064,128]{2,1,0:T(8,128)(2,1)}, u32[]{:S(2)}, u32[]{:S(2)}) collective-permute-start(bf16[2,2064,128]{2,1,0:T(8,128)(2,1)} %get-tuple-element.155), channel_id=1, source_target_pairs={{0,24},{8,16},{16,8},{24,0},{1,25},{9,17},{17,9},{25,1},{2,26},{10... | collective-permute-start | bytes 3170312 | tf_op jit(solution)/shard_map/ppermute | solution.py:30
  354.6 28.3 %all-to-all-start.4 = ((bf16[16,3,128,128]{3,2,1,0:T(8,128)(2,1)}), bf16[16,3,128,128]{3,2,1,0:T(8,128)(2,1)}, u32[]{:S(2)}, u32[]{:S(2)}) async-start(bf16[16,3,128,128]{3,2,1,0:T(8,128)(2,1)} %attend_back.1), calls=%async_computation.4 | async-start | bytes 3145728 | tf_op jit(solution)/shard_map/all_to_all | solution.py:804
  405.8 48.4 %collective-permute-start.84 = (bf16[4,2064,128]{2,1,0:T(8,128)(2,1)}, bf16[4,2064,128]{2,1,0:T(8,128)(2,1)}, u32[]{:S(2)}, u32[]{:S(2)}) collective-permute-start(bf16[4,2064,128]{2,1,0:T(8,128)(2,1)} %pad_maximum_fusion.1), channel_id=1, source_target_pairs={{0,24},{8,16},{16,8},{24,0},{1,25},{9,17},{17,9},{25,1},{2,26},{10... | collective-permute-start | bytes 6340616 | tf_op jit(solution)/shard_map/ppermute | solution.py:30
  407.0 48.2 %collective-permute-start.83 = (bf16[4,2064,128]{2,1,0:T(8,128)(2,1)}, bf16[4,2064,128]{2,1,0:T(8,128)(2,1)}, u32[]{:S(2)}, u32[]{:S(2)}) collective-permute-start(bf16[4,2064,128]{2,1,0:T(8,128)(2,1)} %pad_maximum_fusion), channel_id=1, source_target_pairs={{0,16},{8,24},{16,0},{24,8},{1,17},{9,25},{17,1},{25,9},{2,18},{10... | collective-permute-start | bytes 6340616 | tf_op jit(solution)/shard_map/ppermute | solution.py:30
  408.4 13.7 %collective-permute-start.60 = (bf16[2,1024,128]{2,1,0:T(8,128)(2,1)S(1)}, bf16[2,1024,128]{2,1,0:T(8,128)(2,1)S(1)}, u32[]{:S(2)}, u32[]{:S(2)}) collective-permute-start(bf16[2,1024,128]{2,1,0:T(8,128)(2,1)S(1)} %get-tuple-element.161), channel_id=1, source_target_pairs={{0,2},{2,0},{4,6},{6,4},{1,3},{3,1},{5,7},{7,5},{8,10},{10,8},{12,... | collective-permute-start | bytes 1572872 | tf_op jit(solution)/shard_map/ppermute | solution.py:30
  412.9 14.8 %collective-permute-start.59 = (bf16[2,1024,128]{2,1,0:T(8,128)(2,1)S(1)}, bf16[2,1024,128]{2,1,0:T(8,128)(2,1)S(1)}, u32[]{:S(2)}, u32[]{:S(2)}) collective-permute-start(bf16[2,1024,128]{2,1,0:T(8,128)(2,1)S(1)} %get-tuple-element.162), channel_id=1, source_target_pairs={{0,6},{2,4},{4,2},{6,0},{1,7},{3,5},{5,3},{7,1},{8,14},{10,12},{12... | collective-permute-start | bytes 1572872 | tf_op jit(solution)/shard_map/ppermute | solution.py:30
  415.7 83.6 %collective-permute-start.66 = (bf16[128,2048]{1,0:T(8,128)(2,1)S(1)}, bf16[128,2048]{1,0:T(8,128)(2,1)S(1)}, u32[]{:S(2)}, u32[]{:S(2)}) collective-permute-start(bf16[128,2048]{1,0:T(8,128)(2,1)S(1)} %pad_maximum_fusion.13), channel_id=1, source_target_pairs={{0,96},{32,64},{64,32},{96,0},{1,97},{33,65},{65,33},{97,1},{2,98}... | collective-permute-start | bytes 1572872 | tf_op jit(solution)/shard_map/ppermute | solution.py:30
  431.7 31.0 %collective-permute-start.68 = (f32[32,128]{1,0:T(8,128)S(1)}, f32[32,128]{1,0:T(8,128)S(1)}, u32[]{:S(2)}, u32[]{:S(2)}) collective-permute-start(f32[32,128]{1,0:T(8,128)S(1)} %pad_maximum_fusion.19), channel_id=1, source_target_pairs={{0,64},{32,96},{64,0},{96,32},{1,65},{33,97},{65,1},{97,33},{2,66}... | collective-permute-start | bytes 49160 | tf_op jit(solution)/shard_map/ppermute | solution.py:30
  433.2 29.5 %collective-permute-start.69 = (f32[32,128]{1,0:T(8,128)S(1)}, f32[32,128]{1,0:T(8,128)S(1)}, u32[]{:S(2)}, u32[]{:S(2)}) collective-permute-start(f32[32,128]{1,0:T(8,128)S(1)} %pad_maximum_fusion.19), channel_id=1, source_target_pairs={{0,96},{32,64},{64,32},{96,0},{1,97},{33,65},{65,33},{97,1},{2,98}... | collective-permute-start | bytes 49160 | tf_op jit(solution)/shard_map/ppermute | solution.py:30
  459.9 13.2 %collective-permute-start.85 = (bf16[1024,128]{1,0:T(8,128)(2,1)S(1)}, bf16[1024,128]{1,0:T(8,128)(2,1)S(1)}, u32[]{:S(2)}, u32[]{:S(2)}) collective-permute-start(bf16[1024,128]{1,0:T(8,128)(2,1)S(1)} %get-tuple-element.165), channel_id=1, source_target_pairs={{0,6},{2,4},{4,2},{6,0},{1,7},{3,5},{5,3},{7,1},{8,14},{10,12},{12... | collective-permute-start | bytes 786440 | tf_op jit(solution)/shard_map/ppermute | solution.py:30
  468.1 52.2 %collective-permute-start.73 = (bf16[4,1024,128]{2,1,0:T(8,128)(2,1)}, bf16[4,1024,128]{2,1,0:T(8,128)(2,1)}, u32[]{:S(2)}, u32[]{:S(2)}) collective-permute-start(bf16[4,1024,128]{2,1,0:T(8,128)(2,1)} %pad_maximum_fusion.2), channel_id=1, source_target_pairs={{0,2},{2,0},{4,6},{6,4},{1,3},{3,1},{5,7},{7,5},{8,10},{10,8},{12,... | collective-permute-start | bytes 3145736 | tf_op jit(solution)/shard_map/ppermute | solution.py:30
  469.4 50.8 %collective-permute-start.74 = (bf16[4,1024,128]{2,1,0:T(8,128)(2,1)}, bf16[4,1024,128]{2,1,0:T(8,128)(2,1)}, u32[]{:S(2)}, u32[]{:S(2)}) collective-permute-start(bf16[4,1024,128]{2,1,0:T(8,128)(2,1)} %pad_maximum_fusion.3), channel_id=1, source_target_pairs={{0,6},{2,4},{4,2},{6,0},{1,7},{3,5},{5,3},{7,1},{8,14},{10,12},{12... | collective-permute-start | bytes 3145736 | tf_op jit(solution)/shard_map/ppermute | solution.py:30
  478.9 20.8 %collective-permute-start.65 = (bf16[128,2048]{1,0:T(8,128)(2,1)S(1)}, bf16[128,2048]{1,0:T(8,128)(2,1)S(1)}, u32[]{:S(2)}, u32[]{:S(2)}) collective-permute-start(bf16[128,2048]{1,0:T(8,128)(2,1)S(1)} %copy-done.15), channel_id=1, source_target_pairs={{0,32},{32,0},{64,96},{96,64},{1,33},{33,1},{65,97},{97,65},{2,34}... | collective-permute-start | bytes 1572872 | tf_op jit(solution)/shard_map/ppermute | solution.py:30
  481.6 15.1 %collective-permute-start.87 = (bf16[1040,128]{1,0:T(8,128)(2,1)S(1)}, bf16[1040,128]{1,0:T(8,128)(2,1)S(1)}, u32[]{:S(2)}, u32[]{:S(2)}) collective-permute-start(bf16[1040,128]{1,0:T(8,128)(2,1)S(1)} %get-tuple-element.164), channel_id=1, source_target_pairs={{0,2},{2,0},{4,6},{6,4},{1,3},{3,1},{5,7},{7,5},{8,10},{10,8},{12,... | collective-permute-start | bytes 798728 | tf_op jit(solution)/shard_map/ppermute | solution.py:30
  499.8 14.9 %collective-permute-start.86 = (bf16[2064,128]{1,0:T(8,128)(2,1)}, bf16[2064,128]{1,0:T(8,128)(2,1)S(1)}, u32[]{:S(2)}, u32[]{:S(2)}) collective-permute-start(bf16[2064,128]{1,0:T(8,128)(2,1)} %pad_maximum_fusion.4), channel_id=1, source_target_pairs={{0,2},{2,0},{4,6},{6,4},{1,3},{3,1},{5,7},{7,5},{8,10},{10,8},{12,... | collective-permute-start | bytes 1585160 | tf_op jit(solution)/shard_map/ppermute | solution.py:30
  (113 other events, 1260.1 us)

commit v3 on v2

--- a/solution.py
+++ b/solution.py
@@ -44,6 +44,16 @@
     near1, near3 = near
     far1 = swap(after(near3[:half], *hold), axis, 1)
     return value, near1, far1, swap(near1[half:], axis, 3), near3
+
+
+def spread4(value, axis):
+    return (value, *(swap(value, axis, step) for step in (1, 2, 3)))
+
+
+def collect4(parts, axis, earlier=()):
+    own = parts[0]
+    sums = [add(*terms).astype(bf16) for terms in parts[1:]]
+    return add(*own, *(swap(after(v, *earlier), axis, k + 1) for k, v in enumerate(sums)))
 
 
 def add(*values):
@@ -247,10 +257,11 @@
         return waits
 
     def rows(self, refs, target):
-        return [
-            self.copy(ref, target.at[first : first + ref.shape[0]])
-            for ref, first in zip(refs, (0, 128, 256, 320, 384))
-        ]
+        copies, first = [], 0
+        for ref in refs:
+            copies.append(self.copy(ref, target.at[first : first + ref.shape[0]]))
+            first += ref.shape[0]
+        return copies
 
 
 def wait_all(copies):
@@ -372,9 +383,9 @@
 
 
 def mlp_kernel(*refs):
-    rows, dy_rows, weights = refs[:5], refs[5:10], refs[10:30]
-    hidden_ref, d_gate_ref, d_up_ref, part_ref = refs[30:34]
-    acts, acts_dy, w_gate, w_up, w_down, acc, sems = refs[34:]
+    rows, dy_rows, weights = refs[:5], refs[5:9], refs[9:29]
+    hidden_ref, d_gate_ref, d_up_ref, part_ref = refs[29:33]
+    acts, acts_dy, w_gate, w_up, w_down, acc, sems = refs[33:]
     load = Loader(sems)
     acts_in = load.rows(rows, acts)
     gates = load.mlp_weight(weights, "gate", w_gate)
@@ -451,12 +462,8 @@
 
 
 def mlp_grad_kernel(d_gate_ref, d_up_ref, hidden_ref, *refs):
-    rows, dy_rows, outs, (acts, acts_dy, hidden, sems) = (
-        refs[:5],
-        refs[5:10],
-        refs[10:12],
-        refs[12:],
-    )
+    rows, dy_rows, outs = refs[:5], refs[5:9], (refs[9:11], refs[11:13])
+    acts, acts_dy, hidden, sems = refs[13:]
     load = Loader(sems)
     acts_in = load.rows(rows, acts)
     hidden_in = [
@@ -464,14 +471,16 @@
     ]
     dy_in = load.rows(dy_rows, acts_dy)
     wait_all(acts_in)
-    for n in range(3):
+    for n, name in enumerate(("gate", "up", "down")):
         hidden_in[n].wait()
         if n == 2:
             wait_all(dy_in)
 
-        def store(core, k, block, first=n * 688):
-            y = ((k >> 2) & 1) * 2 + (k >> 3)
-            outs[core][y, k & 3, first : first + 688] = block
+        def store(core, k, block, name=name):
+            y, z = ((k >> 2) & 1) * 2 + (k >> 3), k & 3
+            for group, first_row, rows, at in MLP_ROWS[name]:
+                place = outs[group][core].at[(y, z) if group == 0 else (z, y)]
+                place[first_row : first_row + rows] = block[at : at + rows]
 
         feature_grads(hidden.at[n], acts if n < 2 else acts_dy, store)
 
@@ -479,7 +488,7 @@
 def mlp_grad(d_gate, d_up, hidden, rows, dy_rows):
     return kernel_call(
         mlp_grad_kernel,
-        (shape_of(4, 4, 2064, 128),) * 2,
+        (shape_of(4, 4, GROUP_A, 128),) * 2 + (shape_of(4, 4, GROUP_B, 128),) * 2,
         (d_gate, d_up, hidden, *rows, *dy_rows),
         [ROWS, ROWS, pltpu.VMEM((3, 2, 512, 688), bf16)],
         13,
@@ -527,11 +536,10 @@
 
 
 def qkv_back_kernel(source_ref, dqkv_ref, mine_ref, theirs_ref, *refs):
-    rows, (part_ref, gain_ref, dqkv, acts, weight, tokens, acc, sems) = refs[:5], refs[5:]
+    part_ref, dqkv, acts, weight, acc, sems = refs
     load = Loader(sems, source_ref)
     dqkv_in = load.copy(dqkv_ref, dqkv)
     arrived = load.weight((mine_ref, theirs_ref), 0, weight)
-    tokens_in = load.rows(rows, tokens)
     dqkv_in.wait()
     unpack_heads(dqkv, acts)
     for slab in range(2):
@@ -540,31 +548,22 @@
         if slab == 0:
             acc[...] = part
         else:
-            acc[...] += part
-            part_ref[...] = acc[...].astype(bf16).reshape(4, 128, 2048)
-    wait_all(tokens_in)
-    gain_ref[...] = jnp.zeros_like(gain_ref)
-    for first in range(0, 512, 64):
-        values = tokens[first : first + 64].astype(f32)
-        inverse = lax.rsqrt(jnp.sum(values * values, axis=1, keepdims=True) / 2048.0 + norm_eps)
-        product = acc[first : first + 64] * values * inverse
-        gain_ref[...] += jnp.sum(product.reshape(8, 8, 2048), axis=0)
-
-
-def qkv_back(source, dqkv, weights, token_rows):
+            part_ref[...] = (acc[...] + part).astype(bf16).reshape(4, 128, 2048)
+
+
+def qkv_back(source, dqkv, weights):
     return kernel_call(
         qkv_back_kernel,
-        (shape_of(4, 128, 2048), shape_of(8, 2048, dtype=f32)),
-        (source, dqkv, *weights, *token_rows),
+        shape_of(4, 128, 2048),
+        (source, dqkv, *weights),
         [
             pltpu.VMEM((16, 3, 128, 128), bf16),
             pltpu.VMEM((2, 512, 768), bf16),
             weight_scratch(768),
-            ROWS,
             pltpu.VMEM((512, 2048), f32),
         ],
-        1 + 32 + 5,
-        12,
+        1 + 32,
+        9,
         "qkv_back",
         smem=1,
     )
@@ -796,8 +795,8 @@
     sequence = (x ^ (blk >> 2)) * 2 + yl
     ends = jnp.cumsum(lax.dynamic_slice_in_dim(block_lengths, sequence, 1, 0)[0])
 
-    normed1, tok_low, dy = prepare(place, tokens[0], output_grad[0], first_gain)
-    tok = tok_low.astype(f32)
+    normed1, tok, dy = prepare(place, tokens[0], output_grad[0], first_gain)
+    tok = tok.astype(f32)
     blkaxes = ("yh", "z", "c")
 
     def exchange(value):
@@ -811,20 +810,18 @@
     source = ((yl ^ (rel >> 3)) * 2 + (yh ^ ((rel >> 2) & 1))) * 4 + (z ^ (rel & 3))
 
     rows1 = gather4(normed1, "x")
-    dy_rows = gather4(after(dy, rows1[4]), "x")
+    dy_rows = spread4(after(dy, rows1[4]), "x")
     mine = plane_exchange(jnp.broadcast_to(shard1[None], (16,) + shard1.shape))
-    mine = after(mine, *rows1[2:4], *dy_rows[2:4], cosine, sine)
+    mine = after(mine, *rows1[2:4], *dy_rows[1:], cosine, sine)
     w_attn = (mine, swap(mine, "c", 1))
 
     orders = "zy", "yz"
     shards = after(shard_a, mine), after(shard_b, mine)
-    near = [[swap(v, o[0], 1), swap(v, o[0], 3)] for v, o in zip(shards, orders)]
-    rows1 = (after(rows1[0], *near[0], *near[1]),) + rows1[1:]
-    far = [swap(n[1], o[0], 1) for n, o in zip(near, orders)]
-    qkv = exchange(after(project_qkv(source, rows1, w_attn, own_cosine, own_sine), *far))
-    plane = [stacked((v, n[0], f, n[1])) for v, n, f in zip(shards, near, far)]
-    tok_rows = gather4(after(tok_low, mine), "x")
-    low, attended, lse = attend(ends, after(qkv, *plane, *tok_rows[2:4]))
+    pieces = [spread4(v, o[0]) for v, o in zip(shards, orders)]
+    qkv = project_qkv(source, rows1, w_attn, own_cosine, own_sine)
+    qkv = exchange(after(qkv, *pieces[0], *pieces[1]))
+    plane = [stacked(v) for v in pieces]
+    low, attended, lse = attend(ends, after(qkv, *plane))
     low = exchange(low)
     near = [[swap(v, o[1], 1), swap(v, o[1], 3)] for v, o in zip(plane, orders)]
     part = project_out(source, after(low, *near[0], *near[1]), w_attn)
@@ -841,32 +838,38 @@
 
     far = scatter_far([part[2]], "x")
     near1, near3 = scatter_near([part[1]], [part[3]], far, "x")
-    mlp_mine, mlp_theirs = mlp_grad(after(d_gate, *far), d_up, hidden, rows2, dy_rows)
-    d_normed2 = add(part[0], after(near1, mlp_mine), near3)
+    grads = mlp_grad(after(d_gate, *far), d_up, hidden, rows2, dy_rows)
+    d_normed2 = add(part[0], after(near1, grads[0]), near3)
     back2, second_part = norm_back(d_normed2, residual, inverse2, second_gain)
     d_residual = dy.astype(f32) + back2
     d_attn = d_residual.astype(bf16)
     rows3 = gather4(d_attn, "x")
 
-    mlp_got = swap(after(mlp_theirs, d_attn), "c", 1)
-    rows3 = (after(rows3[0], mlp_got),) + rows3[1:]
+    orders = "yz", "zy"
+    mine = grads[0], grads[2]
+    got = [swap(after(v, d_attn), "c", 1) for v in (grads[1], grads[3])]
+    terms = [pairs(m, g) for m, g in zip(mine, got)]
+    sums = [far_sums(t[2]) for t in terms]
+    rows3 = (after(rows3[0], *sums[0], *sums[1]),) + rows3[1:]
+    far = [(swap(v[0], o[0], 1), swap(v[1], o[0], 3)) for v, o in zip(sums, orders)]
     d_out = out_back(source, rows3, w_attn)
-    mlp_mine = after(mlp_mine, d_out)
-    sums = far_sums(pairs(mlp_mine, mlp_got)[2])
+    terms = [pairs(after(m, d_out), g) for m, g in zip(mine, got)]
+    sums = [near_sums(t[1], t[3], f) for t, f in zip(terms, far)]
     d_out = exchange(d_out)
-    d_out = after(d_out, *sums)
-    far = swap(sums[0], "y", 1), swap(sums[1], "y", 3)
+    d_out = after(d_out, *sums[0], *sums[1])
+    near = [(swap(v[0], o[0], 1), swap(v[1], o[0], 3)) for v, o in zip(sums, orders)]
     dqkv = attend_back(ends, qkv, d_out, attended, lse, cosine, sine)
-    terms = pairs(after(mlp_mine, dqkv), mlp_got)
-    sums = near_sums(terms[1], terms[3], far)
+    dqkv = after(dqkv, *near[0], *near[1])
     down_part = project_down(after(hidden, dqkv), w_mlp)
-    dqkv = exchange(dqkv)
-    dqkv = after(dqkv, *sums, down_part)
-    near = swap(sums[0], "y", 1), swap(sums[1], "y", 3)
+    out_far = scatter_far([down_part[2]], "x")
+    mine = after(mine[0], down_part), after(mine[1], down_part)
+    terms = [pairs(m, g) for m, g in zip(mine, got)]
+    along = [add(*t[0], *n).astype(bf16) for t, n in zip(terms, near)]
+    dqkv = after(exchange(dqkv), *out_far, *along)
 
     qkv_mine, qkv_theirs = qkv_grad(dqkv, low, rows1, rows3)
     qkv_got = swap(qkv_theirs, "c", 1)
-    part, first_part = qkv_back(source, after(dqkv, qkv_mine), w_attn, tok_rows)
+    part = qkv_back(source, after(dqkv, qkv_mine), w_attn)
     sums = far_sums(pairs(qkv_mine, qkv_got)[2])
     qkv_far = swap(sums[0], "z", 1), swap(sums[1], "z", 3)
     part = after(part, *sums)
@@ -874,22 +877,23 @@
     qkv_terms = pairs(after(qkv_mine, *far), qkv_got)
     sums = near_sums(qkv_terms[1], qkv_terms[3], qkv_far)
     qkv_near = swap(sums[0], "z", 1), swap(sums[1], "z", 3)
-    d_near = scatter_near([part[1]], [part[3]], far, "x", sums[:1])
+    d_near = scatter_near([part[1]], [part[3]], far, "x")
     d_normed1 = add(part[0], *d_near)
-    down_part = after(down_part, *sums)
-    output = residual + scatter4([[down_part[k]] for k in range(4)], "x")
+    out_near = scatter_near([after(down_part[1], *d_near)], [down_part[3]], out_far, "x")
+    output = residual + add(down_part[0], *out_near)
     layer_output = restore(place, output.astype(bf16))[None]
-    back1, _ = norm_back(d_normed1, tok, inverse_rms(tok), first_gain)
+    back1, first_part = norm_back(d_normed1, tok, inverse_rms(tok), first_gain)
     input_grad = d_residual + back1
-    along = add(*terms[0], *(after(v, *sums) for v in near)).astype(bf16)
-    grad_mlp = scatter4([[along[k]] for k in range(4)], "z")
+    along = [after(v, *sums) for v in along]
+    grad_a, grad_b = (
+        collect4([[v[k]] for k in range(4)], o[1]) for v, o in zip(along, orders)
+    )
     along = add(*qkv_terms[0], *qkv_near).astype(bf16)
-    grad_qkv = scatter4([[along[k]] for k in range(4)], "y")
-
-    first_part = jnp.sum(after(first_part, *sums), axis=0)
+    grad_qkv = collect4([[along[k]] for k in range(4)], "y")
+
     gains = jnp.concatenate([absolute(first_part), absolute(second_part)], axis=0)
     gains = total4(total4(gains, "x"), "y")
-    gains = total4(after(gains, input_grad, *qkv_near), "z")
+    gains = total4(after(gains, *qkv_near), "z")
     gains = gains + swap(gains, "c", 1)
     input_grad = restore(place, input_grad)[None]
     return (
@@ -901,9 +905,9 @@
         grad_qkv[512:768].T,
         grad_qkv[768:],
         gains[16:].reshape(2048),
-        grad_mlp[:688].T,
-        grad_mlp[688:1376].T,
-        grad_mlp[1376:],
+        grad_a[:688].T,
+        jnp.concatenate([grad_a[688:], grad_b[:352]], axis=0).T,
+        grad_b[352:],
     )
 
 

time: 555 us -> 532 us (0.959)
  waiting for transfers between devices: 217 us -> 172 us
  starting transfers between devices: 122 us -> 139 us
  local copies, waits for them, and re-layouts: 28.1 us -> 34.5 us
    ppermute x89 -> x90, waiting for transfers between devices: 197 us -> 149 us  [swap(): return lax.ppermute(value, names, [(i, i ^ step) for i in range(count)])]
    ppermute x89 -> x90, starting transfers between devices: 95.2 us -> 107 us  [swap(): return lax.ppermute(value, names, [(i, i ^ step) for i in range(count)])]
    all_to_all x4, waiting for transfers between devices: 11.2 us -> 22.6 us  [exchange(): lax.all_to_all(value, blkaxes, split_axis=0, concat_axis=0, tiled=True)]
    all_to_all x1, waiting for transfers between devices: 8.09 us -> 0.56 us  [plane_exchange(): return lax.all_to_all(value, PLANE, split_axis=0, concat_axis=0, tiled=True)]
    unnamed x140 -> x144, local copies, waits for them, and re-layouts: 14.7 us -> 18.5 us
  transfers between devices with their start and end apart: 94 -> 95, of which waited for: 47 -> 44; matrix products, arithmetic and copies ran while one was open for 9% -> 10% of each run, Pallas kernels for 14% -> 16%
where the time goes in v3:
time: 532 us; the launch traced here: 523 us
  waiting for transfers between devices  172 us (32%)
  starting transfers between devices  139 us (26%)
  Pallas kernels  126 us (24%)
  other arithmetic  49.6 us (9%)
  local copies, waits for them, and re-layouts  34.5 us (6%)
    ppermute x90, waiting for transfers between devices, swap(): return lax.ppermute(value, names, [(i, i ^ step) for i in range(count)])  149 us
    ppermute x90, starting transfers between devices, swap(): return lax.ppermute(value, names, [(i, i ^ step) for i in range(count)])  107 us
    pallas_call x8, Pallas kernels, kernel_call(): pl.pallas_call(kernel, out_shape=out_shape, in_specs=[smem_spec()] * smem...  91.7 us
    all_to_all x4, starting transfers between devices, exchange(): lax.all_to_all(value, blkaxes, split_axis=0, concat_axis=0, tiled=True)  23.8 us
    all_to_all x4, waiting for transfers between devices, exchange(): lax.all_to_all(value, blkaxes, split_axis=0, concat_axis=0, tiled=True)  22.6 us
    unnamed x144, local copies, waits for them, and re-layouts  18.5 us
    pallas_call x1, Pallas kernels, attend_back(): pl.pallas_call(attend_back_kernel, out_shape=jax.ShapeDtypeStruct((16, 3,...  15.5 us
  transfers between devices with their start and end apart: 95, of which 44 were waited for; matrix products, arithmetic and copies ran while one was open for 10% of the time, Pallas kernels for 16%

profile of v3, /device:TPU:8, one launch (start us, length us, event | category | flops | bytes accessed | tf_op | source)
XLA Modules:
  0.0 523.4 jit_solution(4859529040815392942)
XLA Ops:
  4.4 2.9 broadcast_in_dim.99
  7.3 8.5 %all-to-all-start = ((bf16[16,1024,128]{2,1,0:T(8,128)(2,1)}), bf16[16,1024,128]{2,1,0:T(8,128)(2,1)}, u32[]{:S(2)}, u32[]{:S(2)}) async-start(bf16[16,1024,128]{2,1,0:T(8,128)(2,1)} %broadcast_in_dim.99), calls=%async_computation | async-start | bytes 8388608 | tf_op jit(solution)/shard_map/all_to_all | solution.py:741
  22.4 11.5 %collective-permute-done.1.refs_4_ = bf16[128,2048]{1,0:T(8,128)(2,1)S(1)} collective-permute-done((bf16[128,2048]{1,0:T(8,128)(2,1)}, bf16[128,2048]{1,0:T(8,128)(2,1)S(1)}, u32[]{:S(2)}, u32[]{:S(2)}) %collective-permute-start.1) | collective-permute-done | bytes 524320 | tf_op jit(solution)/shard_map/ppermute | solution.py:30
  34.2 3.9 collective-permute-start.5
  42.3 3.7 fusion.8
  46.1 17.3 %collective-permute-done.2.refs_2_ = bf16[64,2048]{1,0:T(8,128)(2,1)S(1)} collective-permute-done((bf16[64,2048]{1,0:T(8,128)(2,1)S(1)}, bf16[64,2048]{1,0:T(8,128)(2,1)S(1)}, u32[]{:S(2)}, u32[]{:S(2)}) %collective-permute-start.2) | collective-permute-done | bytes 262176 | tf_op jit(solution)/shard_map/ppermute | solution.py:30
  63.3 4.8 collective-permute-done.3.refs_3_
  72.9 6.9 %collective-permute-start.9 = (bf16[1024,128]{1,0:T(8,128)(2,1)S(1)}, bf16[1024,128]{1,0:T(8,128)(2,1)S(1)}, u32[]{:S(2)}, u32[]{:S(2)}) collective-permute-start(bf16[1024,128]{1,0:T(8,128)(2,1)S(1)} %pad_maximum_fusion.16.own), channel_id=1, source_target_pairs={{0,4},{2,6},{4,0},{6,2},{1,5},{3,7},{5,1},{7,3},{8,12},{10,14},{12... | collective-permute-start | bytes 786440 | tf_op jit(solution)/shard_map/ppermute | solution.py:30
  79.8 3.8 collective-permute-start.12
  84.1 9.9 %project_qkv.1 = bf16[16,3,128,128]{3,2,1,0:T(8,128)(2,1)} custom-call(s32[16]{0:T(128)} %multiply_add_fusion.source_ref, bf16[128,2048]{1,0:T(8,128)(2,1)} %get-tuple-element.65.refs_0_, bf16[128,2048]{1,0:T(8,128)(2,1)} %copy-done.32, bf16[64,2048]{1,0:T(8,128)(2,1)} %copy-done.60, bf16[64,2048]{1,0:T(8,128)(2,1)} %copy-done.61, ...), custom_call_target="tpu_custom_call" | custom-call | flops 11500000256 | tf_op jit(solution)/shard_map/project_qkv/pallas_call | solution.py:278
  97.0 8.1 %all-to-all-start.1 = ((bf16[16,3,128,128]{3,2,1,0:T(8,128)(2,1)}), bf16[16,3,128,128]{3,2,1,0:T(8,128)(2,1)S(1)}, u32[]{:S(2)}, u32[]{:S(2)}) async-start(bf16[16,3,128,128]{3,2,1,0:T(8,128)(2,1)} %project_qkv.1), calls=%async_computation.1 | async-start | bytes 3145728 | tf_op jit(solution)/shard_map/all_to_all | solution.py:803
  108.1 4.0 collective-permute-start.15
  117.9 11.4 %all-to-all-done.1.qkv_ref = bf16[16,3,128,128]{3,2,1,0:T(8,128)(2,1)S(1)} async-done(((bf16[16,3,128,128]{3,2,1,0:T(8,128)(2,1)}), bf16[16,3,128,128]{3,2,1,0:T(8,128)(2,1)S(1)}, u32[]{:S(2)}, u32[]{:S(2)}) %all-to-all-start.1) | async-done | bytes 1572896 | tf_op jit(solution)/shard_map/all_to_all | solution.py:803
  130.4 7.8 %attend.1 = (bf16[16,128,128]{2,1,0:T(8,128)(2,1)}, f32[2048,128]{1,0:T(8,128)}, f32[1,2048]{1,0:T(1,128)}) custom-call(s32[12]{0:T(128)} %bitcast.261, bf16[16,3,128,128]{3,2,1,0:T(8,128)(2,1)} %copy-done.12), custom_call_target="tpu_custom_call" | custom-call | flops 9200000000 | tf_op jit(solution)/shard_map/attend/pallas_call | solution.py:668
  138.2 4.1 all-to-all-start.2
  142.3 3.6 collective-permute-done.14.refs_10_.refs_1_
  146.0 3.2 collective-permute-done.15.refs_13_.refs_4_
  149.8 7.0 %all-to-all-done.2.low_ref = bf16[16,128,128]{2,1,0:T(8,128)(2,1)S(1)} async-done(((bf16[16,128,128]{2,1,0:T(8,128)(2,1)}), bf16[16,128,128]{2,1,0:T(8,128)(2,1)S(1)}, u32[]{:S(2)}, u32[]{:S(2)}) %all-to-all-start.2) | async-done | bytes 524320 | tf_op jit(solution)/shard_map/all_to_all | solution.py:803
  157.7 5.2 project_out.1
  167.5 5.6 %collective-permute-done.18 = bf16[64,2048]{1,0:T(8,128)(2,1)S(1)} collective-permute-done((bf16[64,2048]{1,0:T(8,128)(2,1)S(1)}, bf16[64,2048]{1,0:T(8,128)(2,1)S(1)}, u32[]{:S(2)}, u32[]{:S(2)}) %collective-permute-start.18) | collective-permute-done | bytes 262176 | tf_op jit(solution)/shard_map/ppermute | solution.py:30
  182.5 5.6 %collective-permute-done.21 = bf16[128,2048]{1,0:T(8,128)(2,1)S(1)} collective-permute-done((bf16[128,2048]{1,0:T(8,128)(2,1)S(1)}, bf16[128,2048]{1,0:T(8,128)(2,1)S(1)}, u32[]{:S(2)}, u32[]{:S(2)}) %collective-permute-start.21) | collective-permute-done | bytes 524320 | tf_op jit(solution)/shard_map/ppermute | solution.py:30
  188.0 4.8 collective-permute-start.34
  196.0 7.4 %collective-permute-done.34.refs_22_.refs_13_ = bf16[2,1040,128]{2,1,0:T(8,128)(2,1)S(1)} collective-permute-done((bf16[2,1040,128]{2,1,0:T(8,128)(2,1)S(1)}, bf16[2,1040,128]{2,1,0:T(8,128)(2,1)S(1)}, u32[]{:S(2)}, u32[]{:S(2)}) %collective-permute-start.34) | collective-permute-done | bytes 532512 | tf_op jit(solution)/shard_map/ppermute | solution.py:30
  210.0 5.6 %collective-permute-done.24.refs_2_ = bf16[64,2048]{1,0:T(8,128)(2,1)S(1)} collective-permute-done((bf16[64,2048]{1,0:T(8,128)(2,1)S(1)}, bf16[64,2048]{1,0:T(8,128)(2,1)S(1)}, u32[]{:S(2)}, u32[]{:S(2)}) %collective-permute-start.24) | collective-permute-done | bytes 262176 | tf_op jit(solution)/shard_map/ppermute | solution.py:30
  223.6 29.5 %mlp.1 = (bf16[2,512,688]{2,1,0:T(8,128)(2,1)}, bf16[2,512,688]{2,1,0:T(8,128)(2,1)}, bf16[2,512,688]{2,1,0:T(8,128)(2,1)}, bf16[4,128,2048]{2,1,0:T(8,128)(2,1)}) custom-call(bf16[128,2048]{1,0:T(8,128)(2,1)} %copy-done.16, bf16[128,2048]{1,0:T(8,128)(2,1)} %copy-done.35, bf16[64,2048]{1,0:T(8,128)(2,1)} %copy-done.64, bf16[64,2048]{1,0:T(8,128)(2,1)} %copy-done.65, ...), custom_call_target="tpu_custom_call" | custom-call | flops 32199999488 | tf_op jit(solution)/shard_map/mlp/pallas_call | solution.py:278
  256.6 7.6 %collective-permute-done.40 = bf16[64,2048]{1,0:T(8,128)(2,1)S(1)} collective-permute-done((bf16[64,2048]{1,0:T(8,128)(2,1)S(1)}, bf16[64,2048]{1,0:T(8,128)(2,1)S(1)}, u32[]{:S(2)}, u32[]{:S(2)}) %collective-permute-start.40) | collective-permute-done | bytes 262176 | tf_op jit(solution)/shard_map/ppermute | solution.py:30
  266.6 14.2 %mlp_grad.1 = (bf16[4,4,1024,128]{3,2,1,0:T(8,128)(2,1)}, bf16[4,4,1024,128]{3,2,1,0:T(8,128)(2,1)}, bf16[4,4,1040,128]{3,2,1,0:T(8,128)(2,1)}, bf16[4,4,1040,128]{3,2,1,0:T(8,128)(2,1)}) custom-call(bf16[2,512,688]{2,1,0:T(8,128)(2,1)} %get-tuple-element.88.d_gate_ref, bf16[2,512,688]{2,1,0:T(8,128)(2,1)} %get-tuple-element.89.d_up_ref, ...), custom_call_target="tpu_custom_call" | custom-call | flops 20700000256 | tf_op jit(solution)/shard_map/mlp_grad/pallas_call | solution.py:278
  287.8 12.4 %collective-permute-done.47.refs_4_.refs_9_ = bf16[128,2048]{1,0:T(8,128)(2,1)S(1)} collective-permute-done((bf16[128,2048]{1,0:T(8,128)(2,1)S(1)}, bf16[128,2048]{1,0:T(8,128)(2,1)S(1)}, u32[]{:S(2)}, u32[]{:S(2)}) %collective-permute-start.47) | collective-permute-done | bytes 524320 | tf_op jit(solution)/shard_map/ppermute | solution.py:30
  303.0 3.2 fusion.32
  311.7 6.3 %out_back.1 = bf16[16,128,128]{2,1,0:T(8,128)(2,1)} custom-call(s32[16]{0:T(128)} %multiply_add_fusion.source_ref, bf16[128,2048]{1,0:T(8,128)(2,1)} %copy-done.19, bf16[128,2048]{1,0:T(8,128)(2,1)} %copy-done.34, bf16[64,2048]{1,0:T(8,128)(2,1)} %copy-done.62, bf16[64,2048]{1,0:T(8,128)(2,1)} %copy-done.63, bf16[128,2048]{1,0:T(8,128)(2,1)} %copy-done.33, ...), custom_call_target="tpu_custom_call" | custom-call | flops 6899999744 | tf_op jit(solution)/shard_map/out_back/pallas_call | solution.py:278
  318.0 5.3 %all-to-all-start.3 = ((bf16[16,128,128]{2,1,0:T(8,128)(2,1)}), bf16[16,128,128]{2,1,0:T(8,128)(2,1)S(1)}, u32[]{:S(2)}, u32[]{:S(2)}) async-start(bf16[16,128,128]{2,1,0:T(8,128)(2,1)} %out_back.1), calls=%async_computation.3 | async-start | bytes 1048576 | tf_op jit(solution)/shard_map/all_to_all | solution.py:803
  335.7 3.2 collective-permute-start.55
  338.8 4.6 collective-permute-done.53
  350.7 15.5 %attend_back.1 = bf16[16,3,128,128]{3,2,1,0:T(8,128)(2,1)} custom-call(s32[12]{0:T(128)} %bitcast.262, bf16[16,3,128,128]{3,2,1,0:T(8,128)(2,1)} %copy-done.12, bf16[16,128,128]{2,1,0:T(8,128)(2,1)} %copy-done.17, f32[2048,128]{1,0:T(8,128)} %get-tuple-element.101.out_ref, f32[1,2048]{1,0:T(1,128)} %get-tuple-element.102.lse_ref, f32[2048,128]{1,0:T(8,128)} %copy-done.14, ...), custom_call_target="tpu_custom_call" | custom-call | flops 17250000896 | tf_op jit(solution)/shard_map/attend_back/pallas_call | solution.py:725
  366.2 5.9 %collective-permute-done.56 = bf16[4,1040,128]{2,1,0:T(8,128)(2,1)} collective-permute-done((bf16[4,1040,128]{2,1,0:T(8,128)(2,1)S(1)}, bf16[4,1040,128]{2,1,0:T(8,128)(2,1)}, u32[]{:S(2)}, u32[]{:S(2)}) %collective-permute-start.56) | collective-permute-done | bytes 1064992 | tf_op jit(solution)/shard_map/ppermute | solution.py:30
  374.6 6.4 %all-to-all-start.4 = ((bf16[16,3,128,128]{3,2,1,0:T(8,128)(2,1)}), bf16[16,3,128,128]{3,2,1,0:T(8,128)(2,1)}, u32[]{:S(2)}, u32[]{:S(2)}) async-start(bf16[16,3,128,128]{3,2,1,0:T(8,128)(2,1)} %attend_back.1), calls=%async_computation.4 | async-start | bytes 3145728 | tf_op jit(solution)/shard_map/all_to_all | solution.py:803
  380.9 8.0 %project_down.1 = bf16[4,128,2048]{2,1,0:T(8,128)(2,1)} custom-call(bf16[2,512,688]{2,1,0:T(8,128)(2,1)} %get-tuple-element.104.hidden_ref, bf16[4,1024,128]{2,1,0:T(8,128)(2,1)} %stack.2.refs_9_.refs_0_, bf16[4,1024,128]{2,1,0:T(8,128)(2,1)} %collective-permute-done.14.refs_10_.refs_1_, bf16[2,1024,128]{2,1,0:T(8,128)(2,1)} %copy-done.54, ...), custom_call_target="tpu_custom_call" | custom-call | flops 9200000000 | tf_op jit(solution)/shard_map/project_down/pallas_call | solution.py:278
  395.2 3.7 fusion.5
  400.5 4.2 all-to-all-done.4.dqkv_ref
  404.7 9.3 %qkv_grad.1 = (bf16[4,4,1024,128]{3,2,1,0:T(8,128)(2,1)}, bf16[4,4,1024,128]{3,2,1,0:T(8,128)(2,1)}) custom-call(bf16[16,3,128,128]{3,2,1,0:T(8,128)(2,1)} %all-to-all-done.4.dqkv_ref, bf16[16,128,128]{2,1,0:T(8,128)(2,1)} %copy-done.15, bf16[128,2048]{1,0:T(8,128)(2,1)} %get-tuple-element.65.refs_0_, bf16[128,2048]{1,0:T(8,128)(2,1)} %copy-done.32, ...), custom_call_target="tpu_custom_call" | custom-call | flops 11500000256 | tf_op jit(solution)/shard_map/qkv_grad/pallas_call | solution.py:278
  415.2 9.3 %qkv_back.1 = bf16[4,128,2048]{2,1,0:T(8,128)(2,1)} custom-call(s32[16]{0:T(128)} %multiply_add_fusion.source_ref, bf16[16,3,128,128]{3,2,1,0:T(8,128)(2,1)} %all-to-all-done.4.dqkv_ref, bf16[16,1024,128]{2,1,0:T(8,128)(2,1)} %all-to-all-done.refs_5_.mine_ref, bf16[16,1024,128]{2,1,0:T(8,128)(2,1)} %collective-permute-done.7.refs_6_.theirs_ref), custom_call_target="tpu_custom_call" | custom-call | flops 10350000128 | tf_op jit(solution)/shard_map/qkv_back/pallas_call | solution.py:278
  432.4 3.0 collective-permute-start.73
  441.3 4.6 collective-permute-done.75
  456.0 3.4 collective-permute-done.64
  460.3 4.7 collective-permute-done.86
  477.1 4.0 collective-permute-done.88
  481.1 3.5 collective-permute-start.76
  498.7 4.3 collective-permute-done.76
  (396 shorter events, 188.7 us)
Async XLA Ops:
  7.3 62.1 %all-to-all-start = ((bf16[16,1024,128]{2,1,0:T(8,128)(2,1)}), bf16[16,1024,128]{2,1,0:T(8,128)(2,1)}, u32[]{:S(2)}, u32[]{:S(2)}) async-start(bf16[16,1024,128]{2,1,0:T(8,128)(2,1)} %broadcast_in_dim.99), calls=%async_computation | async-start | bytes 8388608 | tf_op jit(solution)/shard_map/all_to_all | solution.py:741
  19.3 14.6 %collective-permute-start.1 = (bf16[128,2048]{1,0:T(8,128)(2,1)}, bf16[128,2048]{1,0:T(8,128)(2,1)S(1)}, u32[]{:S(2)}, u32[]{:S(2)}) collective-permute-start(bf16[128,2048]{1,0:T(8,128)(2,1)} %get-tuple-element.65.refs_0_), channel_id=1, source_target_pairs={{0,96},{32,64},{64,32},{96,0},{1,97},{33,65},{65,33},{97,1},{2,98}... | collective-permute-start | bytes 1572872 | tf_op jit(solution)/shard_map/ppermute | solution.py:30
  22.2 16.6 %collective-permute-start = (bf16[128,2048]{1,0:T(8,128)(2,1)}, bf16[128,2048]{1,0:T(8,128)(2,1)S(1)}, u32[]{:S(2)}, u32[]{:S(2)}) collective-permute-start(bf16[128,2048]{1,0:T(8,128)(2,1)} %get-tuple-element.65.refs_0_), channel_id=1, source_target_pairs={{0,32},{32,0},{64,96},{96,64},{1,33},{33,1},{65,97},{97,65},{2,34}... | collective-permute-start | bytes 1572872 | tf_op jit(solution)/shard_map/ppermute | solution.py:30
  33.9 34.9 %collective-permute-start.4 = (bf16[128,2048]{1,0:T(8,128)(2,1)}, bf16[128,2048]{1,0:T(8,128)(2,1)}, u32[]{:S(2)}, u32[]{:S(2)}) collective-permute-start(bf16[128,2048]{1,0:T(8,128)(2,1)} %get-tuple-element.67.refs_5_), channel_id=1, source_target_pairs={{0,32},{32,0},{64,96},{96,64},{1,33},{33,1},{65,97},{97,65},{2,34}... | collective-permute-start | bytes 1572872 | tf_op jit(solution)/shard_map/ppermute | solution.py:30
  34.2 34.7 %collective-permute-start.5 = (bf16[128,2048]{1,0:T(8,128)(2,1)}, bf16[128,2048]{1,0:T(8,128)(2,1)}, u32[]{:S(2)}, u32[]{:S(2)}) collective-permute-start(bf16[128,2048]{1,0:T(8,128)(2,1)} %get-tuple-element.67.refs_5_), channel_id=1, source_target_pairs={{0,64},{32,96},{64,0},{96,32},{1,65},{33,97},{65,1},{97,33},{2,66}... | collective-permute-start | bytes 1572872 | tf_op jit(solution)/shard_map/ppermute | solution.py:30
  38.2 30.7 %collective-permute-start.6 = (bf16[128,2048]{1,0:T(8,128)(2,1)}, bf16[128,2048]{1,0:T(8,128)(2,1)}, u32[]{:S(2)}, u32[]{:S(2)}) collective-permute-start(bf16[128,2048]{1,0:T(8,128)(2,1)} %get-tuple-element.67.refs_5_), channel_id=1, source_target_pairs={{0,96},{32,64},{64,32},{96,0},{1,97},{33,65},{65,33},{97,1},{2,98}... | collective-permute-start | bytes 1572872 | tf_op jit(solution)/shard_map/ppermute | solution.py:30
  38.7 24.7 %collective-permute-start.2 = (bf16[64,2048]{1,0:T(8,128)(2,1)S(1)}, bf16[64,2048]{1,0:T(8,128)(2,1)S(1)}, u32[]{:S(2)}, u32[]{:S(2)}) collective-permute-start(bf16[64,2048]{1,0:T(8,128)(2,1)S(1)} %slice.610), channel_id=1, source_target_pairs={{0,32},{32,0},{64,96},{96,64},{1,33},{33,1},{65,97},{97,65},{2,34}... | collective-permute-start | bytes 786440 | tf_op jit(solution)/shard_map/ppermute | solution.py:30
  39.6 28.6 %collective-permute-start.3 = (bf16[64,2048]{1,0:T(8,128)(2,1)S(1)}, bf16[64,2048]{1,0:T(8,128)(2,1)S(1)}, u32[]{:S(2)}, u32[]{:S(2)}) collective-permute-start(bf16[64,2048]{1,0:T(8,128)(2,1)S(1)} %slice.611), channel_id=1, source_target_pairs={{0,96},{32,64},{64,32},{96,0},{1,97},{33,65},{65,33},{97,1},{2,98}... | collective-permute-start | bytes 786440 | tf_op jit(solution)/shard_map/ppermute | solution.py:30
  69.4 14.2 %collective-permute-start.7 = (bf16[16,1024,128]{2,1,0:T(8,128)(2,1)}, bf16[16,1024,128]{2,1,0:T(8,128)(2,1)}, u32[]{:S(2)}, u32[]{:S(2)}) collective-permute-start(bf16[16,1024,128]{2,1,0:T(8,128)(2,1)} %all-to-all-done.refs_5_.mine_ref), channel_id=1, source_target_pairs={{0,1},{1,0},{2,3},{3,2},{4,5},{5,4},{6,7},{7,6},{8,9},{9,8},{10,11... | collective-permute-start | bytes 12582920 | tf_op jit(solution)/shard_map/ppermute | solution.py:30
  72.9 21.1 %collective-permute-start.9 = (bf16[1024,128]{1,0:T(8,128)(2,1)S(1)}, bf16[1024,128]{1,0:T(8,128)(2,1)S(1)}, u32[]{:S(2)}, u32[]{:S(2)}) collective-permute-start(bf16[1024,128]{1,0:T(8,128)(2,1)S(1)} %pad_maximum_fusion.16.own), channel_id=1, source_target_pairs={{0,4},{2,6},{4,0},{6,2},{1,5},{3,7},{5,1},{7,3},{8,12},{10,14},{12... | collective-permute-start | bytes 786440 | tf_op jit(solution)/shard_map/ppermute | solution.py:30
  79.8 15.0 %collective-permute-start.10 = (bf16[1024,128]{1,0:T(8,128)(2,1)S(1)}, bf16[1024,128]{1,0:T(8,128)(2,1)S(1)}, u32[]{:S(2)}, u32[]{:S(2)}) collective-permute-start(bf16[1024,128]{1,0:T(8,128)(2,1)S(1)} %pad_maximum_fusion.16.own), channel_id=1, source_target_pairs={{0,6},{2,4},{4,2},{6,0},{1,7},{3,5},{5,3},{7,1},{8,14},{10,12},{12... | collective-permute-start | bytes 786440 | tf_op jit(solution)/shard_map/ppermute | solution.py:30
  79.8 15.0 %collective-permute-start.11 = (bf16[1040,128]{1,0:T(8,128)(2,1)S(1)}, bf16[1040,128]{1,0:T(8,128)(2,1)S(1)}, u32[]{:S(2)}, u32[]{:S(2)}) collective-permute-start(bf16[1040,128]{1,0:T(8,128)(2,1)S(1)} %pad_maximum_fusion.14.own), channel_id=1, source_target_pairs={{0,16},{8,24},{16,0},{24,8},{1,17},{9,25},{17,1},{25,9},{2,18},{10... | collective-permute-start | bytes 798728 | tf_op jit(solution)/shard_map/ppermute | solution.py:30
  79.8 15.0 %collective-permute-start.12 = (bf16[1040,128]{1,0:T(8,128)(2,1)S(1)}, bf16[1040,128]{1,0:T(8,128)(2,1)S(1)}, u32[]{:S(2)}, u32[]{:S(2)}) collective-permute-start(bf16[1040,128]{1,0:T(8,128)(2,1)S(1)} %pad_maximum_fusion.14.own), channel_id=1, source_target_pairs={{0,8},{8,0},{16,24},{24,16},{1,9},{9,1},{17,25},{25,17},{2,10},{10... | collective-permute-start | bytes 798728 | tf_op jit(solution)/shard_map/ppermute | solution.py:30
  97.0 32.3 %all-to-all-start.1 = ((bf16[16,3,128,128]{3,2,1,0:T(8,128)(2,1)}), bf16[16,3,128,128]{3,2,1,0:T(8,128)(2,1)S(1)}, u32[]{:S(2)}, u32[]{:S(2)}) async-start(bf16[16,3,128,128]{3,2,1,0:T(8,128)(2,1)} %project_qkv.1), calls=%async_computation.1 | async-start | bytes 3145728 | tf_op jit(solution)/shard_map/all_to_all | solution.py:803
  108.0 38.0 %collective-permute-start.14 = (bf16[4,1024,128]{2,1,0:T(8,128)(2,1)}, bf16[4,1024,128]{2,1,0:T(8,128)(2,1)}, u32[]{:S(2)}, u32[]{:S(2)}) collective-permute-start(bf16[4,1024,128]{2,1,0:T(8,128)(2,1)} %stack.2.refs_9_.refs_0_), channel_id=1, source_target_pairs={{0,16},{8,24},{16,0},{24,8},{1,17},{9,25},{17,1},{25,9},{2,18},{10... | collective-permute-start | bytes 3145736 | tf_op jit(solution)/shard_map/ppermute | solution.py:30
  108.1 41.1 %collective-permute-start.15 = (bf16[4,1024,128]{2,1,0:T(8,128)(2,1)}, bf16[4,1024,128]{2,1,0:T(8,128)(2,1)}, u32[]{:S(2)}, u32[]{:S(2)}) collective-permute-start(bf16[4,1024,128]{2,1,0:T(8,128)(2,1)} %stack.2.refs_9_.refs_0_), channel_id=1, source_target_pairs={{0,24},{8,16},{16,8},{24,0},{1,25},{9,17},{17,9},{25,1},{2,26},{10... | collective-permute-start | bytes 3145736 | tf_op jit(solution)/shard_map/ppermute | solution.py:30
  114.3 34.9 %collective-permute-start.16 = (bf16[4,1040,128]{2,1,0:T(8,128)(2,1)}, bf16[4,1040,128]{2,1,0:T(8,128)(2,1)S(1)}, u32[]{:S(2)}, u32[]{:S(2)}) collective-permute-start(bf16[4,1040,128]{2,1,0:T(8,128)(2,1)} %stack.3.refs_19_.refs_10_), channel_id=1, source_target_pairs={{0,2},{2,0},{4,6},{6,4},{1,3},{3,1},{5,7},{7,5},{8,10},{10,8},{12,... | collective-permute-start | bytes 3194888 | tf_op jit(solution)/shard_map/ppermute | solution.py:30
  115.8 34.0 %collective-permute-start.17 = (bf16[4,1040,128]{2,1,0:T(8,128)(2,1)}, bf16[4,1040,128]{2,1,0:T(8,128)(2,1)}, u32[]{:S(2)}, u32[]{:S(2)}) collective-permute-start(bf16[4,1040,128]{2,1,0:T(8,128)(2,1)} %stack.3.refs_19_.refs_10_), channel_id=1, source_target_pairs={{0,6},{2,4},{4,2},{6,0},{1,7},{3,5},{5,3},{7,1},{8,14},{10,12},{12... | collective-permute-start | bytes 3194888 | tf_op jit(solution)/shard_map/ppermute | solution.py:30
  138.2 18.7 %all-to-all-start.2 = ((bf16[16,128,128]{2,1,0:T(8,128)(2,1)}), bf16[16,128,128]{2,1,0:T(8,128)(2,1)S(1)}, u32[]{:S(2)}, u32[]{:S(2)}) async-start(bf16[16,128,128]{2,1,0:T(8,128)(2,1)} %get-tuple-element.73), calls=%async_computation.2 | async-start | bytes 1048576 | tf_op jit(solution)/shard_map/all_to_all | solution.py:803
  176.3 16.6 %collective-permute-start.19 = (bf16[128,2048]{1,0:T(8,128)(2,1)S(1)}, bf16[128,2048]{1,0:T(8,128)(2,1)S(1)}, u32[]{:S(2)}, u32[]{:S(2)}) collective-permute-start(bf16[128,2048]{1,0:T(8,128)(2,1)S(1)} %pad_maximum_fusion.6), channel_id=1, source_target_pairs={{0,32},{32,0},{64,96},{96,64},{1,33},{33,1},{65,97},{97,65},{2,34}... | collective-permute-start | bytes 1572872 | tf_op jit(solution)/shard_map/ppermute | solution.py:30
  177.5 16.1 %collective-permute-start.26 = (bf16[2,1024,128]{2,1,0:T(8,128)(2,1)S(1)}, bf16[2,1024,128]{2,1,0:T(8,128)(2,1)S(1)}, u32[]{:S(2)}, u32[]{:S(2)}) collective-permute-start(bf16[2,1024,128]{2,1,0:T(8,128)(2,1)S(1)} %slice.623), channel_id=1, source_target_pairs={{0,16},{8,24},{16,0},{24,8},{1,17},{9,25},{17,1},{25,9},{2,18},{10... | collective-permute-start | bytes 1572872 | tf_op jit(solution)/shard_map/ppermute | solution.py:30
  178.7 16.7 %collective-permute-start.27 = (bf16[2,1024,128]{2,1,0:T(8,128)(2,1)S(1)}, bf16[2,1024,128]{2,1,0:T(8,128)(2,1)S(1)}, u32[]{:S(2)}, u32[]{:S(2)}) collective-permute-start(bf16[2,1024,128]{2,1,0:T(8,128)(2,1)S(1)} %slice.624), channel_id=1, source_target_pairs={{0,24},{8,16},{16,8},{24,0},{1,25},{9,17},{17,9},{25,1},{2,26},{10... | collective-permute-start | bytes 1572872 | tf_op jit(solution)/shard_map/ppermute | solution.py:30
  188.0 15.3 %collective-permute-start.34 = (bf16[2,1040,128]{2,1,0:T(8,128)(2,1)S(1)}, bf16[2,1040,128]{2,1,0:T(8,128)(2,1)S(1)}, u32[]{:S(2)}, u32[]{:S(2)}) collective-permute-start(bf16[2,1040,128]{2,1,0:T(8,128)(2,1)S(1)} %slice.626), channel_id=1, source_target_pairs={{0,6},{2,4},{4,2},{6,0},{1,7},{3,5},{5,3},{7,1},{8,14},{10,12},{12... | collective-permute-start | bytes 1597448 | tf_op jit(solution)/shard_map/ppermute | solution.py:30
  195.4 21.7 %collective-permute-start.28 = (bf16[4,1024,128]{2,1,0:T(8,128)(2,1)S(1)}, bf16[4,1024,128]{2,1,0:T(8,128)(2,1)S(1)}, u32[]{:S(2)}, u32[]{:S(2)}) collective-permute-start(bf16[4,1024,128]{2,1,0:T(8,128)(2,1)S(1)} %copy-done.47), channel_id=1, source_target_pairs={{0,1},{1,0},{2,3},{3,2},{4,5},{5,4},{6,7},{7,6},{8,9},{9,8},{10,11... | collective-permute-start | bytes 3145736 | tf_op jit(solution)/shard_map/ppermute | solution.py:30
  264.9 16.0 %collective-permute-start.43 = (bf16[128,2048]{1,0:T(8,128)(2,1)S(1)}, bf16[128,2048]{1,0:T(8,128)(2,1)S(1)}, u32[]{:S(2)}, u32[]{:S(2)}) collective-permute-start(bf16[128,2048]{1,0:T(8,128)(2,1)S(1)} %pad_maximum_fusion.9), channel_id=1, source_target_pairs={{0,96},{32,64},{64,32},{96,0},{1,97},{33,65},{65,33},{97,1},{2,98}... | collective-permute-start | bytes 1572872 | tf_op jit(solution)/shard_map/ppermute | solution.py:30
  266.5 14.4 %collective-permute-start.41 = (bf16[128,2048]{1,0:T(8,128)(2,1)S(1)}, bf16[128,2048]{1,0:T(8,128)(2,1)S(1)}, u32[]{:S(2)}, u32[]{:S(2)}) collective-permute-start(bf16[128,2048]{1,0:T(8,128)(2,1)S(1)} %pad_maximum_fusion.8), channel_id=1, source_target_pairs={{0,32},{32,0},{64,96},{96,64},{1,33},{33,1},{65,97},{97,65},{2,34}... | collective-permute-start | bytes 1572872 | tf_op jit(solution)/shard_map/ppermute | solution.py:30
  283.4 19.6 %collective-permute-start.44 = (bf16[4,4,1024,128]{3,2,1,0:T(8,128)(2,1)}, bf16[4,4,1024,128]{3,2,1,0:T(8,128)(2,1)S(1)}, u32[]{:S(2)}, u32[]{:S(2)}) collective-permute-start(bf16[4,4,1024,128]{3,2,1,0:T(8,128)(2,1)} %get-tuple-element.93), channel_id=1, source_target_pairs={{0,1},{1,0},{2,3},{3,2},{4,5},{5,4},{6,7},{7,6},{8,9},{9,8},{10,11... | collective-permute-start | bytes 12582920 | tf_op jit(solution)/shard_map/ppermute | solution.py:30
  284.6 22.1 %collective-permute-start.45 = (bf16[4,4,1040,128]{3,2,1,0:T(8,128)(2,1)S(1)}, bf16[4,4,1040,128]{3,2,1,0:T(8,128)(2,1)S(1)}, u32[]{:S(2)}, u32[]{:S(2)}) collective-permute-start(bf16[4,4,1040,128]{3,2,1,0:T(8,128)(2,1)S(1)} %copy-done.43), channel_id=1, source_target_pairs={{0,1},{1,0},{2,3},{3,2},{4,5},{5,4},{6,7},{7,6},{8,9},{9,8},{10,11... | collective-permute-start | bytes 12779528 | tf_op jit(solution)/shard_map/ppermute | solution.py:30
  284.6 15.5 %collective-permute-start.47 = (bf16[128,2048]{1,0:T(8,128)(2,1)S(1)}, bf16[128,2048]{1,0:T(8,128)(2,1)S(1)}, u32[]{:S(2)}, u32[]{:S(2)}) collective-permute-start(bf16[128,2048]{1,0:T(8,128)(2,1)S(1)} %get-tuple-element.97.refs_0_.refs_5_), channel_id=1, source_target_pairs={{0,96},{32,64},{64,32},{96,0},{1,97},{33,65},{65,33},{97,1},{2,98}... | collective-permute-start | bytes 1572872 | tf_op jit(solution)/shard_map/ppermute | solution.py:30
  286.4 14.7 %collective-permute-start.46 = (bf16[128,2048]{1,0:T(8,128)(2,1)S(1)}, bf16[128,2048]{1,0:T(8,128)(2,1)S(1)}, u32[]{:S(2)}, u32[]{:S(2)}) collective-permute-start(bf16[128,2048]{1,0:T(8,128)(2,1)S(1)} %get-tuple-element.97.refs_0_.refs_5_), channel_id=1, source_target_pairs={{0,32},{32,0},{64,96},{96,64},{1,33},{33,1},{65,97},{97,65},{2,34}... | collective-permute-start | bytes 1572872 | tf_op jit(solution)/shard_map/ppermute | solution.py:30
  306.2 24.7 %collective-permute-start.51 = (bf16[2,1024,128]{2,1,0:T(8,128)(2,1)}, bf16[2,1024,128]{2,1,0:T(8,128)(2,1)}, u32[]{:S(2)}, u32[]{:S(2)}) collective-permute-start(bf16[2,1024,128]{2,1,0:T(8,128)(2,1)} %get-tuple-element.168), channel_id=1, source_target_pairs={{0,16},{8,24},{16,0},{24,8},{1,17},{9,25},{17,1},{25,9},{2,18},{10... | collective-permute-start | bytes 1572872 | tf_op jit(solution)/shard_map/ppermute | solution.py:30
  306.2 24.7 %collective-permute-start.50 = (bf16[2,1024,128]{2,1,0:T(8,128)(2,1)}, bf16[2,1024,128]{2,1,0:T(8,128)(2,1)}, u32[]{:S(2)}, u32[]{:S(2)}) collective-permute-start(bf16[2,1024,128]{2,1,0:T(8,128)(2,1)} %get-tuple-element.167), channel_id=1, source_target_pairs={{0,24},{8,16},{16,8},{24,0},{1,25},{9,17},{17,9},{25,1},{2,26},{10... | collective-permute-start | bytes 1572872 | tf_op jit(solution)/shard_map/ppermute | solution.py:30
  318.0 31.9 %all-to-all-start.3 = ((bf16[16,128,128]{2,1,0:T(8,128)(2,1)}), bf16[16,128,128]{2,1,0:T(8,128)(2,1)S(1)}, u32[]{:S(2)}, u32[]{:S(2)}) async-start(bf16[16,128,128]{2,1,0:T(8,128)(2,1)} %out_back.1), calls=%async_computation.3 | async-start | bytes 1048576 | tf_op jit(solution)/shard_map/all_to_all | solution.py:803
  323.3 20.2 %collective-permute-start.53 = (bf16[2,1040,128]{2,1,0:T(8,128)(2,1)S(1)}, bf16[2,1040,128]{2,1,0:T(8,128)(2,1)S(1)}, u32[]{:S(2)}, u32[]{:S(2)}) collective-permute-start(bf16[2,1040,128]{2,1,0:T(8,128)(2,1)S(1)} %get-tuple-element.156), channel_id=1, source_target_pairs={{0,2},{2,0},{4,6},{6,4},{1,3},{3,1},{5,7},{7,5},{8,10},{10,8},{12,... | collective-permute-start | bytes 1597448 | tf_op jit(solution)/shard_map/ppermute | solution.py:30
  325.2 19.4 %collective-permute-start.52 = (bf16[2,1040,128]{2,1,0:T(8,128)(2,1)S(1)}, bf16[2,1040,128]{2,1,0:T(8,128)(2,1)S(1)}, u32[]{:S(2)}, u32[]{:S(2)}) collective-permute-start(bf16[2,1040,128]{2,1,0:T(8,128)(2,1)S(1)} %get-tuple-element.155), channel_id=1, source_target_pairs={{0,6},{2,4},{4,2},{6,0},{1,7},{3,5},{5,3},{7,1},{8,14},{10,12},{12... | collective-permute-start | bytes 1597448 | tf_op jit(solution)/shard_map/ppermute | solution.py:30
  334.2 32.0 %collective-permute-start.54 = (bf16[4,1024,128]{2,1,0:T(8,128)(2,1)}, bf16[4,1024,128]{2,1,0:T(8,128)(2,1)}, u32[]{:S(2)}, u32[]{:S(2)}) collective-permute-start(bf16[4,1024,128]{2,1,0:T(8,128)(2,1)} %pad_maximum_fusion.2), channel_id=1, source_target_pairs={{0,16},{8,24},{16,0},{24,8},{1,17},{9,25},{17,1},{25,9},{2,18},{10... | collective-permute-start | bytes 3145736 | tf_op jit(solution)/shard_map/ppermute | solution.py:30
  335.7 30.5 %collective-permute-start.55 = (bf16[4,1024,128]{2,1,0:T(8,128)(2,1)}, bf16[4,1024,128]{2,1,0:T(8,128)(2,1)}, u32[]{:S(2)}, u32[]{:S(2)}) collective-permute-start(bf16[4,1024,128]{2,1,0:T(8,128)(2,1)} %pad_maximum_fusion.3), channel_id=1, source_target_pairs={{0,24},{8,16},{16,8},{24,0},{1,25},{9,17},{17,9},{25,1},{2,26},{10... | collective-permute-start | bytes 3145736 | tf_op jit(solution)/shard_map/ppermute | solution.py:30
  346.7 25.4 %collective-permute-start.56 = (bf16[4,1040,128]{2,1,0:T(8,128)(2,1)S(1)}, bf16[4,1040,128]{2,1,0:T(8,128)(2,1)}, u32[]{:S(2)}, u32[]{:S(2)}) collective-permute-start(bf16[4,1040,128]{2,1,0:T(8,128)(2,1)S(1)} %pad_maximum_fusion), channel_id=1, source_target_pairs={{0,2},{2,0},{4,6},{6,4},{1,3},{3,1},{5,7},{7,5},{8,10},{10,8},{12,... | collective-permute-start | bytes 3194888 | tf_op jit(solution)/shard_map/ppermute | solution.py:30
  348.1 26.5 %collective-permute-start.57 = (bf16[4,1040,128]{2,1,0:T(8,128)(2,1)}, bf16[4,1040,128]{2,1,0:T(8,128)(2,1)}, u32[]{:S(2)}, u32[]{:S(2)}) collective-permute-start(bf16[4,1040,128]{2,1,0:T(8,128)(2,1)} %pad_maximum_fusion.1), channel_id=1, source_target_pairs={{0,6},{2,4},{4,2},{6,0},{1,7},{3,5},{5,3},{7,1},{8,14},{10,12},{12... | collective-permute-start | bytes 3194888 | tf_op jit(solution)/shard_map/ppermute | solution.py:30
  374.6 30.1 %all-to-all-start.4 = ((bf16[16,3,128,128]{3,2,1,0:T(8,128)(2,1)}), bf16[16,3,128,128]{3,2,1,0:T(8,128)(2,1)}, u32[]{:S(2)}, u32[]{:S(2)}) async-start(bf16[16,3,128,128]{3,2,1,0:T(8,128)(2,1)} %attend_back.1), calls=%async_computation.4 | async-start | bytes 3145728 | tf_op jit(solution)/shard_map/all_to_all | solution.py:803
  430.8 62.6 %collective-permute-start.66 = (bf16[128,2048]{1,0:T(8,128)(2,1)}, bf16[128,2048]{1,0:T(8,128)(2,1)}, u32[]{:S(2)}, u32[]{:S(2)}) collective-permute-start(bf16[128,2048]{1,0:T(8,128)(2,1)} %pad_maximum_fusion.13), channel_id=1, source_target_pairs={{0,96},{32,64},{64,32},{96,0},{1,97},{33,65},{65,33},{97,1},{2,98}... | collective-permute-start | bytes 1572872 | tf_op jit(solution)/shard_map/ppermute | solution.py:30
  432.4 14.7 %collective-permute-start.73 = (bf16[2,1024,128]{2,1,0:T(8,128)(2,1)S(1)}, bf16[2,1024,128]{2,1,0:T(8,128)(2,1)S(1)}, u32[]{:S(2)}, u32[]{:S(2)}) collective-permute-start(bf16[2,1024,128]{2,1,0:T(8,128)(2,1)S(1)} %get-tuple-element.161), channel_id=1, source_target_pairs={{0,6},{2,4},{4,2},{6,0},{1,7},{3,5},{5,3},{7,1},{8,14},{10,12},{12... | collective-permute-start | bytes 1572872 | tf_op jit(solution)/shard_map/ppermute | solution.py:30
  437.9 17.0 %collective-permute-start.62 = (bf16[128,2048]{1,0:T(8,128)(2,1)S(1)}, bf16[128,2048]{1,0:T(8,128)(2,1)S(1)}, u32[]{:S(2)}, u32[]{:S(2)}) collective-permute-start(bf16[128,2048]{1,0:T(8,128)(2,1)S(1)} %pad_maximum_fusion.10), channel_id=1, source_target_pairs={{0,32},{32,0},{64,96},{96,64},{1,33},{33,1},{65,97},{97,65},{2,34}... | collective-permute-start | bytes 1572872 | tf_op jit(solution)/shard_map/ppermute | solution.py:30
  438.2 21.3 %collective-permute-start.64 = (bf16[128,2048]{1,0:T(8,128)(2,1)S(1)}, bf16[128,2048]{1,0:T(8,128)(2,1)S(1)}, u32[]{:S(2)}, u32[]{:S(2)}) collective-permute-start(bf16[128,2048]{1,0:T(8,128)(2,1)S(1)} %pad_maximum_fusion.11), channel_id=1, source_target_pairs={{0,96},{32,64},{64,32},{96,0},{1,97},{33,65},{65,33},{97,1},{2,98}... | collective-permute-start | bytes 1572872 | tf_op jit(solution)/shard_map/ppermute | solution.py:30
  451.0 14.0 %collective-permute-start.86 = (bf16[1024,128]{1,0:T(8,128)(2,1)S(1)}, bf16[1024,128]{1,0:T(8,128)(2,1)S(1)}, u32[]{:S(2)}, u32[]{:S(2)}) collective-permute-start(bf16[1024,128]{1,0:T(8,128)(2,1)S(1)} %get-tuple-element.194), channel_id=1, source_target_pairs={{0,6},{2,4},{4,2},{6,0},{1,7},{3,5},{5,3},{7,1},{8,14},{10,12},{12... | collective-permute-start | bytes 786440 | tf_op jit(solution)/shard_map/ppermute | solution.py:30
  459.4 17.6 %collective-permute-start.89 = (bf16[1040,128]{1,0:T(8,128)(2,1)}, bf16[1040,128]{1,0:T(8,128)(2,1)}, u32[]{:S(2)}, u32[]{:S(2)}) collective-permute-start(bf16[1040,128]{1,0:T(8,128)(2,1)} %get-tuple-element.191), channel_id=1, source_target_pairs={{0,24},{8,16},{16,8},{24,0},{1,25},{9,17},{17,9},{25,1},{2,26},{10... | collective-permute-start | bytes 798728 | tf_op jit(solution)/shard_map/ppermute | solution.py:30
  477.0 21.7 %collective-permute-start.74 = (bf16[4,1024,128]{2,1,0:T(8,128)(2,1)}, bf16[4,1024,128]{2,1,0:T(8,128)(2,1)S(1)}, u32[]{:S(2)}, u32[]{:S(2)}) collective-permute-start(bf16[4,1024,128]{2,1,0:T(8,128)(2,1)} %pad_maximum_fusion.4), channel_id=1, source_target_pairs={{0,2},{2,0},{4,6},{6,4},{1,3},{3,1},{5,7},{7,5},{8,10},{10,8},{12,... | collective-permute-start | bytes 3145736 | tf_op jit(solution)/shard_map/ppermute | solution.py:30
  481.1 21.9 %collective-permute-start.76 = (bf16[4,1024,128]{2,1,0:T(8,128)(2,1)}, bf16[4,1024,128]{2,1,0:T(8,128)(2,1)S(1)}, u32[]{:S(2)}, u32[]{:S(2)}) collective-permute-start(bf16[4,1024,128]{2,1,0:T(8,128)(2,1)} %pad_maximum_fusion.5), channel_id=1, source_target_pairs={{0,6},{2,4},{4,2},{6,0},{1,7},{3,5},{5,3},{7,1},{8,14},{10,12},{12... | collective-permute-start | bytes 3145736 | tf_op jit(solution)/shard_map/ppermute | solution.py:30
  (117 other events, 1318.1 us)

commit v4 on v3

--- a/solution.py
+++ b/solution.py
@@ -160,6 +160,30 @@
     )(place, tok, dy, gain)
 
 
+def share_kernel(query_ref, key_ref, value_ref, out_w_ref, copies_ref, rows, sems):
+    for n, ref in enumerate((query_ref, key_ref, value_ref)):
+        rows[n * 256 : (n + 1) * 256] = ref[...].astype(f32).T.astype(bf16)
+    rows[768:] = out_w_ref[...]
+    made = [pltpu.make_async_copy(rows, copies_ref.at[k], sems.at[k]) for k in range(16)]
+    for copy in made:
+        copy.start()
+    for copy in made:
+        copy.wait()
+
+
+def share(query, key, value, out_weight):
+    return pl.pallas_call(
+        share_kernel,
+        out_shape=jax.ShapeDtypeStruct((16, 1024, 128), bf16),
+        in_specs=[vmem_spec()] * 4,
+        out_specs=pl.BlockSpec(memory_space=pl.ANY),
+        scratch_shapes=[pltpu.VMEM((1024, 128), bf16), pltpu.SemaphoreType.DMA((16,))],
+        compiler_params=params(),
+        cost_estimate=cost(3),
+        name="share",
+    )(query, key, value, out_weight)
+
+
 def restore_kernel(place_ref, in_ref, out_ref):
     for r in range(16):
         out_ref[:, block_at(place_ref, r)] = in_ref[:, r * 128 : (r + 1) * 128]
@@ -232,22 +256,25 @@
         source_ref = self.source_ref if source_ref is None else source_ref
         waits = ([], [])
         rows = target.shape[1]
-        for core in range(2):
-            for k in range(16):
-                slab, block = k >> 3, core * 8 + (k & 7)
-                waits[slab].append(
-                    self.copy(
-                        refs[core].at[source_ref[k], first_row : first_row + rows],
-                        target.at[slab, :, block * 128 : (block + 1) * 128],
+        for slab in range(2):
+            for core in range(2):
+                for k in range(8):
+                    block = core * 8 + k
+                    waits[slab].append(
+                        self.copy(
+                            refs[core].at[source_ref[slab * 8 + k], first_row : first_row + rows],
+                            target.at[slab, :, block * 128 : (block + 1) * 128],
+                        )
                     )
-                )
         return waits
 
-    def mlp_weight(self, pieces, name, target):
+    def mlp_weight(self, pieces, name, target, slabs=(0, 1)):
         waits = ([], [])
         for group, first_row, rows, at in MLP_ROWS[name]:
             refs = pieces[group * 10 : group * 10 + 10]
             for array, entry, slab, block in pieces_of(("zy", "yz")[group]):
+                if slab not in slabs:
+                    continue
                 waits[slab].append(
                     self.copy(
                         refs[array].at[entry, first_row : first_row + rows],
@@ -385,13 +412,15 @@
 def mlp_kernel(*refs):
     rows, dy_rows, weights = refs[:5], refs[5:9], refs[9:29]
     hidden_ref, d_gate_ref, d_up_ref, part_ref = refs[29:33]
-    acts, acts_dy, w_gate, w_up, w_down, acc, sems = refs[33:]
+    acts, acts_dy, w_gate, w_up, w_down, sems = refs[33:]
     load = Loader(sems)
     acts_in = load.rows(rows, acts)
-    gates = load.mlp_weight(weights, "gate", w_gate)
-    ups = load.mlp_weight(weights, "up", w_up)
+    names = ("gate", w_gate), ("up", w_up), ("down", w_down)
+    first = [load.mlp_weight(weights, *name, slabs=(0,))[0] for name in names[:2]]
     dy_in = load.rows(dy_rows, acts_dy)
-    downs = load.mlp_weight(weights, "down", w_down)
+    first.append(load.mlp_weight(weights, *names[2], slabs=(0,))[0])
+    second = [load.mlp_weight(weights, *name, slabs=(1,))[1] for name in names]
+    gates, ups, downs = zip(first, second)
     wait_all(acts_in)
     for slab in range(2):
         wait_all(gates[slab])
@@ -407,11 +436,11 @@
         hidden_ref[slab] = (silu * up).astype(bf16)
         d_gate_ref[slab] = (d_hidden * up * sigmoid * (1.0 + gate * (1.0 - sigmoid))).astype(bf16)
         d_up_ref[slab] = (d_hidden * silu).astype(bf16)
-        part = dot_nn(d_gate_ref[slab], w_gate[slab]) + dot_nn(d_up_ref[slab], w_up[slab])
-        if slab == 0:
-            acc[...] = part
-        else:
-            part_ref[...] = (acc[...] + part).astype(bf16).reshape(4, 128, 2048)
+    for column in range(0, 2048, 512):
+        here = slice(column, column + 512)
+        part = dot_nn(d_gate_ref[0], w_gate[0, :, here]) + dot_nn(d_up_ref[0], w_up[0, :, here])
+        part += dot_nn(d_gate_ref[1], w_gate[1, :, here]) + dot_nn(d_up_ref[1], w_up[1, :, here])
+        part_ref[:, :, here] = part.astype(bf16).reshape(4, 128, 512)
 
 
 def mlp(rows, dy_rows, weights):
@@ -420,8 +449,7 @@
         (shape_of(2, 512, 688),) * 3 + (shape_of(4, 128, 2048),),
         (*rows, *dy_rows, *weights),
         [ROWS, ROWS]
-        + [weight_scratch(688)] * 3
-        + [pltpu.VMEM((512, 2048), f32)],
+        + [weight_scratch(688)] * 3,
         10 + 128,
         28,
         "mlp",
@@ -802,16 +830,13 @@
     def exchange(value):
         return lax.all_to_all(value, blkaxes, split_axis=0, concat_axis=0, tiled=True)
 
-    shard1 = jnp.concatenate(
-        [query_weight.T, key_weight.T, value_weight.T, out_weight], axis=0
-    )
     shard_a = jnp.concatenate([gate_weight.T, up_weight.T[:336]], axis=0)
     shard_b = jnp.concatenate([up_weight.T[336:], down_weight], axis=0)
     source = ((yl ^ (rel >> 3)) * 2 + (yh ^ ((rel >> 2) & 1))) * 4 + (z ^ (rel & 3))
 
     rows1 = gather4(normed1, "x")
     dy_rows = spread4(after(dy, rows1[4]), "x")
-    mine = plane_exchange(jnp.broadcast_to(shard1[None], (16,) + shard1.shape))
+    mine = plane_exchange(share(query_weight, key_weight, value_weight, out_weight))
     mine = after(mine, *rows1[2:4], *dy_rows[1:], cosine, sine)
     w_attn = (mine, swap(mine, "c", 1))
 

time: 532 us -> 524 us (0.985)
  local copies, waits for them, and re-layouts: 34.5 us -> 28.8 us
    unnamed x144 -> x141, local copies, waits for them, and re-layouts: 18.5 us -> 15.6 us
where the time goes in v4:
time: 524 us; the launch traced here: 516 us
  waiting for transfers between devices  172 us (33%)
  starting transfers between devices  139 us (27%)
  Pallas kernels  126 us (24%)
  other arithmetic  48.7 us (9%)
  local copies, waits for them, and re-layouts  28.8 us (5%)
    ppermute x90, waiting for transfers between devices, swap(): return lax.ppermute(value, names, [(i, i ^ step) for i in range(count)])  149 us
    ppermute x90, starting transfers between devices, swap(): return lax.ppermute(value, names, [(i, i ^ step) for i in range(count)])  107 us
    pallas_call x8, Pallas kernels, kernel_call(): pl.pallas_call(kernel, out_shape=out_shape, in_specs=[smem_spec()] * smem...  87.7 us
    all_to_all x4, starting transfers between devices, exchange(): lax.all_to_all(value, blkaxes, split_axis=0, concat_axis=0, tiled=True)  23.8 us
    all_to_all x4, waiting for transfers between devices, exchange(): lax.all_to_all(value, blkaxes, split_axis=0, concat_axis=0, tiled=True)  22.5 us
    unnamed x141, local copies, waits for them, and re-layouts  15.6 us
    pallas_call x1, Pallas kernels, attend_back(): pl.pallas_call(attend_back_kernel, out_shape=jax.ShapeDtypeStruct((16, 3,...  15.5 us
  transfers between devices with their start and end apart: 95, of which 44 were waited for; matrix products, arithmetic and copies ran while one was open for 10% of the time, Pallas kernels for 16%

profile of v4, /device:TPU:8, one launch (start us, length us, event | category | flops | bytes accessed | tf_op | source)
XLA Modules:
  0.0 516.4 jit_solution(9551850924962443770)
XLA Ops:
  0.7 3.3 share.1
  4.0 8.4 %all-to-all-start = ((bf16[16,1024,128]{2,1,0:T(8,128)(2,1)}), bf16[16,1024,128]{2,1,0:T(8,128)(2,1)}, u32[]{:S(2)}, u32[]{:S(2)}) async-start(bf16[16,1024,128]{2,1,0:T(8,128)(2,1)} %share.1), calls=%async_computation | async-start | bytes 8388608 | tf_op jit(solution)/shard_map/all_to_all | solution.py:769
  19.0 11.5 %collective-permute-done.1.refs_4_ = bf16[128,2048]{1,0:T(8,128)(2,1)S(1)} collective-permute-done((bf16[128,2048]{1,0:T(8,128)(2,1)}, bf16[128,2048]{1,0:T(8,128)(2,1)S(1)}, u32[]{:S(2)}, u32[]{:S(2)}) %collective-permute-start.1) | collective-permute-done | bytes 524320 | tf_op jit(solution)/shard_map/ppermute | solution.py:30
  30.8 3.9 collective-permute-start.5
  38.9 3.7 fusion.8
  42.6 17.3 %collective-permute-done.2.refs_2_ = bf16[64,2048]{1,0:T(8,128)(2,1)S(1)} collective-permute-done((bf16[64,2048]{1,0:T(8,128)(2,1)S(1)}, bf16[64,2048]{1,0:T(8,128)(2,1)S(1)}, u32[]{:S(2)}, u32[]{:S(2)}) %collective-permute-start.2) | collective-permute-done | bytes 262176 | tf_op jit(solution)/shard_map/ppermute | solution.py:30
  59.9 4.8 collective-permute-done.3.refs_3_
  69.5 6.9 %collective-permute-start.9 = (bf16[1024,128]{1,0:T(8,128)(2,1)S(1)}, bf16[1024,128]{1,0:T(8,128)(2,1)S(1)}, u32[]{:S(2)}, u32[]{:S(2)}) collective-permute-start(bf16[1024,128]{1,0:T(8,128)(2,1)S(1)} %pad_maximum_fusion.15.own), channel_id=1, source_target_pairs={{0,4},{2,6},{4,0},{6,2},{1,5},{3,7},{5,1},{7,3},{8,12},{10,14},{12... | collective-permute-start | bytes 786440 | tf_op jit(solution)/shard_map/ppermute | solution.py:30
  76.4 3.8 collective-permute-start.12
  80.6 9.4 %project_qkv.1 = bf16[16,3,128,128]{3,2,1,0:T(8,128)(2,1)} custom-call(s32[16]{0:T(128)} %multiply_add_fusion.source_ref, bf16[128,2048]{1,0:T(8,128)(2,1)} %get-tuple-element.65.refs_0_, bf16[128,2048]{1,0:T(8,128)(2,1)} %copy-done.32, bf16[64,2048]{1,0:T(8,128)(2,1)} %copy-done.60, bf16[64,2048]{1,0:T(8,128)(2,1)} %copy-done.61, ...), custom_call_target="tpu_custom_call" | custom-call | flops 11500000256 | tf_op jit(solution)/shard_map/project_qkv/pallas_call | solution.py:305
  93.5 8.1 %all-to-all-start.1 = ((bf16[16,3,128,128]{3,2,1,0:T(8,128)(2,1)}), bf16[16,3,128,128]{3,2,1,0:T(8,128)(2,1)S(1)}, u32[]{:S(2)}, u32[]{:S(2)}) async-start(bf16[16,3,128,128]{3,2,1,0:T(8,128)(2,1)} %project_qkv.1), calls=%async_computation.1 | async-start | bytes 3145728 | tf_op jit(solution)/shard_map/all_to_all | solution.py:831
  104.6 4.0 collective-permute-start.15
  114.4 11.4 %all-to-all-done.1.qkv_ref = bf16[16,3,128,128]{3,2,1,0:T(8,128)(2,1)S(1)} async-done(((bf16[16,3,128,128]{3,2,1,0:T(8,128)(2,1)}), bf16[16,3,128,128]{3,2,1,0:T(8,128)(2,1)S(1)}, u32[]{:S(2)}, u32[]{:S(2)}) %all-to-all-start.1) | async-done | bytes 1572896 | tf_op jit(solution)/shard_map/all_to_all | solution.py:831
  126.9 7.8 %attend.1 = (bf16[16,128,128]{2,1,0:T(8,128)(2,1)}, f32[2048,128]{1,0:T(8,128)}, f32[1,2048]{1,0:T(1,128)}) custom-call(s32[12]{0:T(128)} %bitcast.255, bf16[16,3,128,128]{3,2,1,0:T(8,128)(2,1)} %copy-done.12), custom_call_target="tpu_custom_call" | custom-call | flops 9200000000 | tf_op jit(solution)/shard_map/attend/pallas_call | solution.py:696
  134.8 4.1 all-to-all-start.2
  138.9 3.5 collective-permute-done.14.refs_10_.refs_1_
  142.3 3.4 collective-permute-done.15.refs_13_.refs_4_
  146.4 7.0 %all-to-all-done.2.low_ref = bf16[16,128,128]{2,1,0:T(8,128)(2,1)S(1)} async-done(((bf16[16,128,128]{2,1,0:T(8,128)(2,1)}), bf16[16,128,128]{2,1,0:T(8,128)(2,1)S(1)}, u32[]{:S(2)}, u32[]{:S(2)}) %all-to-all-start.2) | async-done | bytes 524320 | tf_op jit(solution)/shard_map/all_to_all | solution.py:831
  154.2 5.2 %project_out.1 = bf16[4,128,2048]{2,1,0:T(8,128)(2,1)} custom-call(s32[16]{0:T(128)} %multiply_add_fusion.source_ref, bf16[16,128,128]{2,1,0:T(8,128)(2,1)} %copy-done.15, bf16[16,1024,128]{2,1,0:T(8,128)(2,1)} %all-to-all-done.refs_5_.mine_ref, bf16[16,1024,128]{2,1,0:T(8,128)(2,1)} %collective-permute-done.7.refs_6_.theirs_ref), custom_call_target="tpu_custom_call" | custom-call | flops 5750000128 | tf_op jit(solution)/shard_map/project_out/pallas_call | solution.py:305
  164.1 5.6 %collective-permute-done.18 = bf16[64,2048]{1,0:T(8,128)(2,1)S(1)} collective-permute-done((bf16[64,2048]{1,0:T(8,128)(2,1)S(1)}, bf16[64,2048]{1,0:T(8,128)(2,1)S(1)}, u32[]{:S(2)}, u32[]{:S(2)}) %collective-permute-start.18) | collective-permute-done | bytes 262176 | tf_op jit(solution)/shard_map/ppermute | solution.py:30
  179.0 5.6 %collective-permute-done.21 = bf16[128,2048]{1,0:T(8,128)(2,1)S(1)} collective-permute-done((bf16[128,2048]{1,0:T(8,128)(2,1)S(1)}, bf16[128,2048]{1,0:T(8,128)(2,1)S(1)}, u32[]{:S(2)}, u32[]{:S(2)}) %collective-permute-start.21) | collective-permute-done | bytes 524320 | tf_op jit(solution)/shard_map/ppermute | solution.py:30
  184.6 4.8 collective-permute-start.34
  192.6 7.4 %collective-permute-done.34.refs_22_.refs_13_ = bf16[2,1040,128]{2,1,0:T(8,128)(2,1)S(1)} collective-permute-done((bf16[2,1040,128]{2,1,0:T(8,128)(2,1)S(1)}, bf16[2,1040,128]{2,1,0:T(8,128)(2,1)S(1)}, u32[]{:S(2)}, u32[]{:S(2)}) %collective-permute-start.34) | collective-permute-done | bytes 532512 | tf_op jit(solution)/shard_map/ppermute | solution.py:30
  206.6 5.6 %collective-permute-done.24.refs_2_ = bf16[64,2048]{1,0:T(8,128)(2,1)S(1)} collective-permute-done((bf16[64,2048]{1,0:T(8,128)(2,1)S(1)}, bf16[64,2048]{1,0:T(8,128)(2,1)S(1)}, u32[]{:S(2)}, u32[]{:S(2)}) %collective-permute-start.24) | collective-permute-done | bytes 262176 | tf_op jit(solution)/shard_map/ppermute | solution.py:30
  220.1 26.6 %mlp.1 = (bf16[2,512,688]{2,1,0:T(8,128)(2,1)}, bf16[2,512,688]{2,1,0:T(8,128)(2,1)}, bf16[2,512,688]{2,1,0:T(8,128)(2,1)}, bf16[4,128,2048]{2,1,0:T(8,128)(2,1)}) custom-call(bf16[128,2048]{1,0:T(8,128)(2,1)} %copy-done.16, bf16[128,2048]{1,0:T(8,128)(2,1)} %copy-done.35, bf16[64,2048]{1,0:T(8,128)(2,1)} %copy-done.64, bf16[64,2048]{1,0:T(8,128)(2,1)} %copy-done.65, ...), custom_call_target="tpu_custom_call" | custom-call | flops 32199999488 | tf_op jit(solution)/shard_map/mlp/pallas_call | solution.py:305
  250.2 7.6 %collective-permute-done.40 = bf16[64,2048]{1,0:T(8,128)(2,1)S(1)} collective-permute-done((bf16[64,2048]{1,0:T(8,128)(2,1)S(1)}, bf16[64,2048]{1,0:T(8,128)(2,1)S(1)}, u32[]{:S(2)}, u32[]{:S(2)}) %collective-permute-start.40) | collective-permute-done | bytes 262176 | tf_op jit(solution)/shard_map/ppermute | solution.py:30
  260.2 14.3 %mlp_grad.1 = (bf16[4,4,1024,128]{3,2,1,0:T(8,128)(2,1)}, bf16[4,4,1024,128]{3,2,1,0:T(8,128)(2,1)}, bf16[4,4,1040,128]{3,2,1,0:T(8,128)(2,1)}, bf16[4,4,1040,128]{3,2,1,0:T(8,128)(2,1)}) custom-call(bf16[2,512,688]{2,1,0:T(8,128)(2,1)} %get-tuple-element.88.d_gate_ref, bf16[2,512,688]{2,1,0:T(8,128)(2,1)} %get-tuple-element.89.d_up_ref, ...), custom_call_target="tpu_custom_call" | custom-call | flops 20700000256 | tf_op jit(solution)/shard_map/mlp_grad/pallas_call | solution.py:305
  281.4 12.4 %collective-permute-done.47.refs_4_.refs_9_ = bf16[128,2048]{1,0:T(8,128)(2,1)S(1)} collective-permute-done((bf16[128,2048]{1,0:T(8,128)(2,1)S(1)}, bf16[128,2048]{1,0:T(8,128)(2,1)S(1)}, u32[]{:S(2)}, u32[]{:S(2)}) %collective-permute-start.47) | collective-permute-done | bytes 524320 | tf_op jit(solution)/shard_map/ppermute | solution.py:30
  296.5 3.2 fusion.32
  305.3 6.1 %out_back.1 = bf16[16,128,128]{2,1,0:T(8,128)(2,1)} custom-call(s32[16]{0:T(128)} %multiply_add_fusion.source_ref, bf16[128,2048]{1,0:T(8,128)(2,1)} %copy-done.19, bf16[128,2048]{1,0:T(8,128)(2,1)} %copy-done.34, bf16[64,2048]{1,0:T(8,128)(2,1)} %copy-done.62, bf16[64,2048]{1,0:T(8,128)(2,1)} %copy-done.63, bf16[128,2048]{1,0:T(8,128)(2,1)} %copy-done.33, ...), custom_call_target="tpu_custom_call" | custom-call | flops 6899999744 | tf_op jit(solution)/shard_map/out_back/pallas_call | solution.py:305
  311.4 5.2 %all-to-all-start.3 = ((bf16[16,128,128]{2,1,0:T(8,128)(2,1)}), bf16[16,128,128]{2,1,0:T(8,128)(2,1)S(1)}, u32[]{:S(2)}, u32[]{:S(2)}) async-start(bf16[16,128,128]{2,1,0:T(8,128)(2,1)} %out_back.1), calls=%async_computation.3 | async-start | bytes 1048576 | tf_op jit(solution)/shard_map/all_to_all | solution.py:831
  329.1 3.2 collective-permute-start.55
  332.2 4.6 collective-permute-done.53
  344.1 15.5 %attend_back.1 = bf16[16,3,128,128]{3,2,1,0:T(8,128)(2,1)} custom-call(s32[12]{0:T(128)} %bitcast.256, bf16[16,3,128,128]{3,2,1,0:T(8,128)(2,1)} %copy-done.12, bf16[16,128,128]{2,1,0:T(8,128)(2,1)} %copy-done.17, f32[2048,128]{1,0:T(8,128)} %get-tuple-element.101.out_ref, f32[1,2048]{1,0:T(1,128)} %get-tuple-element.102.lse_ref, f32[2048,128]{1,0:T(8,128)} %copy-done.14, ...), custom_call_target="tpu_custom_call" | custom-call | flops 17250000896 | tf_op jit(solution)/shard_map/attend_back/pallas_call | solution.py:753
  359.6 5.9 %collective-permute-done.56 = bf16[4,1040,128]{2,1,0:T(8,128)(2,1)} collective-permute-done((bf16[4,1040,128]{2,1,0:T(8,128)(2,1)S(1)}, bf16[4,1040,128]{2,1,0:T(8,128)(2,1)}, u32[]{:S(2)}, u32[]{:S(2)}) %collective-permute-start.56) | collective-permute-done | bytes 1064992 | tf_op jit(solution)/shard_map/ppermute | solution.py:30
  368.0 6.4 %all-to-all-start.4 = ((bf16[16,3,128,128]{3,2,1,0:T(8,128)(2,1)}), bf16[16,3,128,128]{3,2,1,0:T(8,128)(2,1)}, u32[]{:S(2)}, u32[]{:S(2)}) async-start(bf16[16,3,128,128]{3,2,1,0:T(8,128)(2,1)} %attend_back.1), calls=%async_computation.4 | async-start | bytes 3145728 | tf_op jit(solution)/shard_map/all_to_all | solution.py:831
  374.4 8.0 %project_down.1 = bf16[4,128,2048]{2,1,0:T(8,128)(2,1)} custom-call(bf16[2,512,688]{2,1,0:T(8,128)(2,1)} %get-tuple-element.104.hidden_ref, bf16[4,1024,128]{2,1,0:T(8,128)(2,1)} %stack.2.refs_9_.refs_0_, bf16[4,1024,128]{2,1,0:T(8,128)(2,1)} %collective-permute-done.14.refs_10_.refs_1_, bf16[2,1024,128]{2,1,0:T(8,128)(2,1)} %copy-done.54, ...), custom_call_target="tpu_custom_call" | custom-call | flops 9200000000 | tf_op jit(solution)/shard_map/project_down/pallas_call | solution.py:305
  388.6 3.7 fusion.5
  393.9 4.2 all-to-all-done.4.dqkv_ref
  398.1 9.3 %qkv_grad.1 = (bf16[4,4,1024,128]{3,2,1,0:T(8,128)(2,1)}, bf16[4,4,1024,128]{3,2,1,0:T(8,128)(2,1)}) custom-call(bf16[16,3,128,128]{3,2,1,0:T(8,128)(2,1)} %all-to-all-done.4.dqkv_ref, bf16[16,128,128]{2,1,0:T(8,128)(2,1)} %copy-done.15, bf16[128,2048]{1,0:T(8,128)(2,1)} %get-tuple-element.65.refs_0_, bf16[128,2048]{1,0:T(8,128)(2,1)} %copy-done.32, ...), custom_call_target="tpu_custom_call" | custom-call | flops 11500000256 | tf_op jit(solution)/shard_map/qkv_grad/pallas_call | solution.py:305
  408.6 8.8 %qkv_back.1 = bf16[4,128,2048]{2,1,0:T(8,128)(2,1)} custom-call(s32[16]{0:T(128)} %multiply_add_fusion.source_ref, bf16[16,3,128,128]{3,2,1,0:T(8,128)(2,1)} %all-to-all-done.4.dqkv_ref, bf16[16,1024,128]{2,1,0:T(8,128)(2,1)} %all-to-all-done.refs_5_.mine_ref, bf16[16,1024,128]{2,1,0:T(8,128)(2,1)} %collective-permute-done.7.refs_6_.theirs_ref), custom_call_target="tpu_custom_call" | custom-call | flops 10350000128 | tf_op jit(solution)/shard_map/qkv_back/pallas_call | solution.py:305
  425.4 3.0 collective-permute-start.73
  434.3 4.6 collective-permute-done.75
  448.9 3.4 collective-permute-done.64
  453.2 4.7 collective-permute-done.86
  470.1 4.0 collective-permute-done.88
  474.0 3.5 collective-permute-start.76
  491.7 4.2 collective-permute-done.76
  (392 shorter events, 185.4 us)
Async XLA Ops:
  4.0 62.0 %all-to-all-start = ((bf16[16,1024,128]{2,1,0:T(8,128)(2,1)}), bf16[16,1024,128]{2,1,0:T(8,128)(2,1)}, u32[]{:S(2)}, u32[]{:S(2)}) async-start(bf16[16,1024,128]{2,1,0:T(8,128)(2,1)} %share.1), calls=%async_computation | async-start | bytes 8388608 | tf_op jit(solution)/shard_map/all_to_all | solution.py:769
  15.9 14.6 %collective-permute-start.1 = (bf16[128,2048]{1,0:T(8,128)(2,1)}, bf16[128,2048]{1,0:T(8,128)(2,1)S(1)}, u32[]{:S(2)}, u32[]{:S(2)}) collective-permute-start(bf16[128,2048]{1,0:T(8,128)(2,1)} %get-tuple-element.65.refs_0_), channel_id=1, source_target_pairs={{0,96},{32,64},{64,32},{96,0},{1,97},{33,65},{65,33},{97,1},{2,98}... | collective-permute-start | bytes 1572872 | tf_op jit(solution)/shard_map/ppermute | solution.py:30
  18.7 16.6 %collective-permute-start = (bf16[128,2048]{1,0:T(8,128)(2,1)}, bf16[128,2048]{1,0:T(8,128)(2,1)S(1)}, u32[]{:S(2)}, u32[]{:S(2)}) collective-permute-start(bf16[128,2048]{1,0:T(8,128)(2,1)} %get-tuple-element.65.refs_0_), channel_id=1, source_target_pairs={{0,32},{32,0},{64,96},{96,64},{1,33},{33,1},{65,97},{97,65},{2,34}... | collective-permute-start | bytes 1572872 | tf_op jit(solution)/shard_map/ppermute | solution.py:30
  30.5 34.9 %collective-permute-start.4 = (bf16[128,2048]{1,0:T(8,128)(2,1)}, bf16[128,2048]{1,0:T(8,128)(2,1)}, u32[]{:S(2)}, u32[]{:S(2)}) collective-permute-start(bf16[128,2048]{1,0:T(8,128)(2,1)} %get-tuple-element.67.refs_5_), channel_id=1, source_target_pairs={{0,32},{32,0},{64,96},{96,64},{1,33},{33,1},{65,97},{97,65},{2,34}... | collective-permute-start | bytes 1572872 | tf_op jit(solution)/shard_map/ppermute | solution.py:30
  30.8 34.7 %collective-permute-start.5 = (bf16[128,2048]{1,0:T(8,128)(2,1)}, bf16[128,2048]{1,0:T(8,128)(2,1)}, u32[]{:S(2)}, u32[]{:S(2)}) collective-permute-start(bf16[128,2048]{1,0:T(8,128)(2,1)} %get-tuple-element.67.refs_5_), channel_id=1, source_target_pairs={{0,64},{32,96},{64,0},{96,32},{1,65},{33,97},{65,1},{97,33},{2,66}... | collective-permute-start | bytes 1572872 | tf_op jit(solution)/shard_map/ppermute | solution.py:30
  34.7 30.7 %collective-permute-start.6 = (bf16[128,2048]{1,0:T(8,128)(2,1)}, bf16[128,2048]{1,0:T(8,128)(2,1)}, u32[]{:S(2)}, u32[]{:S(2)}) collective-permute-start(bf16[128,2048]{1,0:T(8,128)(2,1)} %get-tuple-element.67.refs_5_), channel_id=1, source_target_pairs={{0,96},{32,64},{64,32},{96,0},{1,97},{33,65},{65,33},{97,1},{2,98}... | collective-permute-start | bytes 1572872 | tf_op jit(solution)/shard_map/ppermute | solution.py:30
  35.2 24.7 %collective-permute-start.2 = (bf16[64,2048]{1,0:T(8,128)(2,1)S(1)}, bf16[64,2048]{1,0:T(8,128)(2,1)S(1)}, u32[]{:S(2)}, u32[]{:S(2)}) collective-permute-start(bf16[64,2048]{1,0:T(8,128)(2,1)S(1)} %slice.610), channel_id=1, source_target_pairs={{0,32},{32,0},{64,96},{96,64},{1,33},{33,1},{65,97},{97,65},{2,34}... | collective-permute-start | bytes 786440 | tf_op jit(solution)/shard_map/ppermute | solution.py:30
  36.1 28.6 %collective-permute-start.3 = (bf16[64,2048]{1,0:T(8,128)(2,1)S(1)}, bf16[64,2048]{1,0:T(8,128)(2,1)S(1)}, u32[]{:S(2)}, u32[]{:S(2)}) collective-permute-start(bf16[64,2048]{1,0:T(8,128)(2,1)S(1)} %slice.611), channel_id=1, source_target_pairs={{0,96},{32,64},{64,32},{96,0},{1,97},{33,65},{65,33},{97,1},{2,98}... | collective-permute-start | bytes 786440 | tf_op jit(solution)/shard_map/ppermute | solution.py:30
  66.0 14.2 %collective-permute-start.7 = (bf16[16,1024,128]{2,1,0:T(8,128)(2,1)}, bf16[16,1024,128]{2,1,0:T(8,128)(2,1)}, u32[]{:S(2)}, u32[]{:S(2)}) collective-permute-start(bf16[16,1024,128]{2,1,0:T(8,128)(2,1)} %all-to-all-done.refs_5_.mine_ref), channel_id=1, source_target_pairs={{0,1},{1,0},{2,3},{3,2},{4,5},{5,4},{6,7},{7,6},{8,9},{9,8},{10,11... | collective-permute-start | bytes 12582920 | tf_op jit(solution)/shard_map/ppermute | solution.py:30
  69.5 20.6 %collective-permute-start.9 = (bf16[1024,128]{1,0:T(8,128)(2,1)S(1)}, bf16[1024,128]{1,0:T(8,128)(2,1)S(1)}, u32[]{:S(2)}, u32[]{:S(2)}) collective-permute-start(bf16[1024,128]{1,0:T(8,128)(2,1)S(1)} %pad_maximum_fusion.15.own), channel_id=1, source_target_pairs={{0,4},{2,6},{4,0},{6,2},{1,5},{3,7},{5,1},{7,3},{8,12},{10,14},{12... | collective-permute-start | bytes 786440 | tf_op jit(solution)/shard_map/ppermute | solution.py:30
  76.4 15.0 %collective-permute-start.10 = (bf16[1024,128]{1,0:T(8,128)(2,1)S(1)}, bf16[1024,128]{1,0:T(8,128)(2,1)S(1)}, u32[]{:S(2)}, u32[]{:S(2)}) collective-permute-start(bf16[1024,128]{1,0:T(8,128)(2,1)S(1)} %pad_maximum_fusion.15.own), channel_id=1, source_target_pairs={{0,6},{2,4},{4,2},{6,0},{1,7},{3,5},{5,3},{7,1},{8,14},{10,12},{12... | collective-permute-start | bytes 786440 | tf_op jit(solution)/shard_map/ppermute | solution.py:30
  76.4 15.0 %collective-permute-start.11 = (bf16[1040,128]{1,0:T(8,128)(2,1)S(1)}, bf16[1040,128]{1,0:T(8,128)(2,1)S(1)}, u32[]{:S(2)}, u32[]{:S(2)}) collective-permute-start(bf16[1040,128]{1,0:T(8,128)(2,1)S(1)} %pad_maximum_fusion.14.own), channel_id=1, source_target_pairs={{0,16},{8,24},{16,0},{24,8},{1,17},{9,25},{17,1},{25,9},{2,18},{10... | collective-permute-start | bytes 798728 | tf_op jit(solution)/shard_map/ppermute | solution.py:30
  76.4 15.0 %collective-permute-start.12 = (bf16[1040,128]{1,0:T(8,128)(2,1)S(1)}, bf16[1040,128]{1,0:T(8,128)(2,1)S(1)}, u32[]{:S(2)}, u32[]{:S(2)}) collective-permute-start(bf16[1040,128]{1,0:T(8,128)(2,1)S(1)} %pad_maximum_fusion.14.own), channel_id=1, source_target_pairs={{0,8},{8,0},{16,24},{24,16},{1,9},{9,1},{17,25},{25,17},{2,10},{10... | collective-permute-start | bytes 798728 | tf_op jit(solution)/shard_map/ppermute | solution.py:30
  93.5 32.3 %all-to-all-start.1 = ((bf16[16,3,128,128]{3,2,1,0:T(8,128)(2,1)}), bf16[16,3,128,128]{3,2,1,0:T(8,128)(2,1)S(1)}, u32[]{:S(2)}, u32[]{:S(2)}) async-start(bf16[16,3,128,128]{3,2,1,0:T(8,128)(2,1)} %project_qkv.1), calls=%async_computation.1 | async-start | bytes 3145728 | tf_op jit(solution)/shard_map/all_to_all | solution.py:831
  104.5 37.8 %collective-permute-start.14 = (bf16[4,1024,128]{2,1,0:T(8,128)(2,1)}, bf16[4,1024,128]{2,1,0:T(8,128)(2,1)}, u32[]{:S(2)}, u32[]{:S(2)}) collective-permute-start(bf16[4,1024,128]{2,1,0:T(8,128)(2,1)} %stack.2.refs_9_.refs_0_), channel_id=1, source_target_pairs={{0,16},{8,24},{16,0},{24,8},{1,17},{9,25},{17,1},{25,9},{2,18},{10... | collective-permute-start | bytes 3145736 | tf_op jit(solution)/shard_map/ppermute | solution.py:30
  104.6 41.1 %collective-permute-start.15 = (bf16[4,1024,128]{2,1,0:T(8,128)(2,1)}, bf16[4,1024,128]{2,1,0:T(8,128)(2,1)}, u32[]{:S(2)}, u32[]{:S(2)}) collective-permute-start(bf16[4,1024,128]{2,1,0:T(8,128)(2,1)} %stack.2.refs_9_.refs_0_), channel_id=1, source_target_pairs={{0,24},{8,16},{16,8},{24,0},{1,25},{9,17},{17,9},{25,1},{2,26},{10... | collective-permute-start | bytes 3145736 | tf_op jit(solution)/shard_map/ppermute | solution.py:30
  110.8 34.9 %collective-permute-start.16 = (bf16[4,1040,128]{2,1,0:T(8,128)(2,1)}, bf16[4,1040,128]{2,1,0:T(8,128)(2,1)S(1)}, u32[]{:S(2)}, u32[]{:S(2)}) collective-permute-start(bf16[4,1040,128]{2,1,0:T(8,128)(2,1)} %stack.3.refs_19_.refs_10_), channel_id=1, source_target_pairs={{0,2},{2,0},{4,6},{6,4},{1,3},{3,1},{5,7},{7,5},{8,10},{10,8},{12,... | collective-permute-start | bytes 3194888 | tf_op jit(solution)/shard_map/ppermute | solution.py:30
  112.4 34.0 %collective-permute-start.17 = (bf16[4,1040,128]{2,1,0:T(8,128)(2,1)}, bf16[4,1040,128]{2,1,0:T(8,128)(2,1)}, u32[]{:S(2)}, u32[]{:S(2)}) collective-permute-start(bf16[4,1040,128]{2,1,0:T(8,128)(2,1)} %stack.3.refs_19_.refs_10_), channel_id=1, source_target_pairs={{0,6},{2,4},{4,2},{6,0},{1,7},{3,5},{5,3},{7,1},{8,14},{10,12},{12... | collective-permute-start | bytes 3194888 | tf_op jit(solution)/shard_map/ppermute | solution.py:30
  134.8 18.7 %all-to-all-start.2 = ((bf16[16,128,128]{2,1,0:T(8,128)(2,1)}), bf16[16,128,128]{2,1,0:T(8,128)(2,1)S(1)}, u32[]{:S(2)}, u32[]{:S(2)}) async-start(bf16[16,128,128]{2,1,0:T(8,128)(2,1)} %get-tuple-element.73), calls=%async_computation.2 | async-start | bytes 1048576 | tf_op jit(solution)/shard_map/all_to_all | solution.py:831
  172.8 16.6 %collective-permute-start.19 = (bf16[128,2048]{1,0:T(8,128)(2,1)S(1)}, bf16[128,2048]{1,0:T(8,128)(2,1)S(1)}, u32[]{:S(2)}, u32[]{:S(2)}) collective-permute-start(bf16[128,2048]{1,0:T(8,128)(2,1)S(1)} %pad_maximum_fusion.6), channel_id=1, source_target_pairs={{0,32},{32,0},{64,96},{96,64},{1,33},{33,1},{65,97},{97,65},{2,34}... | collective-permute-start | bytes 1572872 | tf_op jit(solution)/shard_map/ppermute | solution.py:30
  174.1 16.1 %collective-permute-start.26 = (bf16[2,1024,128]{2,1,0:T(8,128)(2,1)S(1)}, bf16[2,1024,128]{2,1,0:T(8,128)(2,1)S(1)}, u32[]{:S(2)}, u32[]{:S(2)}) collective-permute-start(bf16[2,1024,128]{2,1,0:T(8,128)(2,1)S(1)} %slice.623), channel_id=1, source_target_pairs={{0,16},{8,24},{16,0},{24,8},{1,17},{9,25},{17,1},{25,9},{2,18},{10... | collective-permute-start | bytes 1572872 | tf_op jit(solution)/shard_map/ppermute | solution.py:30
  175.3 16.7 %collective-permute-start.27 = (bf16[2,1024,128]{2,1,0:T(8,128)(2,1)S(1)}, bf16[2,1024,128]{2,1,0:T(8,128)(2,1)S(1)}, u32[]{:S(2)}, u32[]{:S(2)}) collective-permute-start(bf16[2,1024,128]{2,1,0:T(8,128)(2,1)S(1)} %slice.624), channel_id=1, source_target_pairs={{0,24},{8,16},{16,8},{24,0},{1,25},{9,17},{17,9},{25,1},{2,26},{10... | collective-permute-start | bytes 1572872 | tf_op jit(solution)/shard_map/ppermute | solution.py:30
  184.6 15.3 %collective-permute-start.34 = (bf16[2,1040,128]{2,1,0:T(8,128)(2,1)S(1)}, bf16[2,1040,128]{2,1,0:T(8,128)(2,1)S(1)}, u32[]{:S(2)}, u32[]{:S(2)}) collective-permute-start(bf16[2,1040,128]{2,1,0:T(8,128)(2,1)S(1)} %slice.626), channel_id=1, source_target_pairs={{0,6},{2,4},{4,2},{6,0},{1,7},{3,5},{5,3},{7,1},{8,14},{10,12},{12... | collective-permute-start | bytes 1597448 | tf_op jit(solution)/shard_map/ppermute | solution.py:30
  192.0 21.7 %collective-permute-start.28 = (bf16[4,1024,128]{2,1,0:T(8,128)(2,1)S(1)}, bf16[4,1024,128]{2,1,0:T(8,128)(2,1)S(1)}, u32[]{:S(2)}, u32[]{:S(2)}) collective-permute-start(bf16[4,1024,128]{2,1,0:T(8,128)(2,1)S(1)} %copy-done.47), channel_id=1, source_target_pairs={{0,1},{1,0},{2,3},{3,2},{4,5},{5,4},{6,7},{7,6},{8,9},{9,8},{10,11... | collective-permute-start | bytes 3145736 | tf_op jit(solution)/shard_map/ppermute | solution.py:30
  258.4 16.0 %collective-permute-start.43 = (bf16[128,2048]{1,0:T(8,128)(2,1)S(1)}, bf16[128,2048]{1,0:T(8,128)(2,1)S(1)}, u32[]{:S(2)}, u32[]{:S(2)}) collective-permute-start(bf16[128,2048]{1,0:T(8,128)(2,1)S(1)} %pad_maximum_fusion.9), channel_id=1, source_target_pairs={{0,96},{32,64},{64,32},{96,0},{1,97},{33,65},{65,33},{97,1},{2,98}... | collective-permute-start | bytes 1572872 | tf_op jit(solution)/shard_map/ppermute | solution.py:30
  260.1 14.4 %collective-permute-start.41 = (bf16[128,2048]{1,0:T(8,128)(2,1)S(1)}, bf16[128,2048]{1,0:T(8,128)(2,1)S(1)}, u32[]{:S(2)}, u32[]{:S(2)}) collective-permute-start(bf16[128,2048]{1,0:T(8,128)(2,1)S(1)} %pad_maximum_fusion.8), channel_id=1, source_target_pairs={{0,32},{32,0},{64,96},{96,64},{1,33},{33,1},{65,97},{97,65},{2,34}... | collective-permute-start | bytes 1572872 | tf_op jit(solution)/shard_map/ppermute | solution.py:30
  277.0 19.6 %collective-permute-start.44 = (bf16[4,4,1024,128]{3,2,1,0:T(8,128)(2,1)}, bf16[4,4,1024,128]{3,2,1,0:T(8,128)(2,1)S(1)}, u32[]{:S(2)}, u32[]{:S(2)}) collective-permute-start(bf16[4,4,1024,128]{3,2,1,0:T(8,128)(2,1)} %get-tuple-element.93), channel_id=1, source_target_pairs={{0,1},{1,0},{2,3},{3,2},{4,5},{5,4},{6,7},{7,6},{8,9},{9,8},{10,11... | collective-permute-start | bytes 12582920 | tf_op jit(solution)/shard_map/ppermute | solution.py:30
  278.2 22.0 %collective-permute-start.45 = (bf16[4,4,1040,128]{3,2,1,0:T(8,128)(2,1)S(1)}, bf16[4,4,1040,128]{3,2,1,0:T(8,128)(2,1)S(1)}, u32[]{:S(2)}, u32[]{:S(2)}) collective-permute-start(bf16[4,4,1040,128]{3,2,1,0:T(8,128)(2,1)S(1)} %copy-done.43), channel_id=1, source_target_pairs={{0,1},{1,0},{2,3},{3,2},{4,5},{5,4},{6,7},{7,6},{8,9},{9,8},{10,11... | collective-permute-start | bytes 12779528 | tf_op jit(solution)/shard_map/ppermute | solution.py:30
  278.2 15.5 %collective-permute-start.47 = (bf16[128,2048]{1,0:T(8,128)(2,1)S(1)}, bf16[128,2048]{1,0:T(8,128)(2,1)S(1)}, u32[]{:S(2)}, u32[]{:S(2)}) collective-permute-start(bf16[128,2048]{1,0:T(8,128)(2,1)S(1)} %get-tuple-element.97.refs_0_.refs_5_), channel_id=1, source_target_pairs={{0,96},{32,64},{64,32},{96,0},{1,97},{33,65},{65,33},{97,1},{2,98}... | collective-permute-start | bytes 1572872 | tf_op jit(solution)/shard_map/ppermute | solution.py:30
  280.0 14.7 %collective-permute-start.46 = (bf16[128,2048]{1,0:T(8,128)(2,1)S(1)}, bf16[128,2048]{1,0:T(8,128)(2,1)S(1)}, u32[]{:S(2)}, u32[]{:S(2)}) collective-permute-start(bf16[128,2048]{1,0:T(8,128)(2,1)S(1)} %get-tuple-element.97.refs_0_.refs_5_), channel_id=1, source_target_pairs={{0,32},{32,0},{64,96},{96,64},{1,33},{33,1},{65,97},{97,65},{2,34}... | collective-permute-start | bytes 1572872 | tf_op jit(solution)/shard_map/ppermute | solution.py:30
  299.8 24.5 %collective-permute-start.51 = (bf16[2,1024,128]{2,1,0:T(8,128)(2,1)}, bf16[2,1024,128]{2,1,0:T(8,128)(2,1)}, u32[]{:S(2)}, u32[]{:S(2)}) collective-permute-start(bf16[2,1024,128]{2,1,0:T(8,128)(2,1)} %get-tuple-element.168), channel_id=1, source_target_pairs={{0,16},{8,24},{16,0},{24,8},{1,17},{9,25},{17,1},{25,9},{2,18},{10... | collective-permute-start | bytes 1572872 | tf_op jit(solution)/shard_map/ppermute | solution.py:30
  299.8 24.5 %collective-permute-start.50 = (bf16[2,1024,128]{2,1,0:T(8,128)(2,1)}, bf16[2,1024,128]{2,1,0:T(8,128)(2,1)}, u32[]{:S(2)}, u32[]{:S(2)}) collective-permute-start(bf16[2,1024,128]{2,1,0:T(8,128)(2,1)} %get-tuple-element.167), channel_id=1, source_target_pairs={{0,24},{8,16},{16,8},{24,0},{1,25},{9,17},{17,9},{25,1},{2,26},{10... | collective-permute-start | bytes 1572872 | tf_op jit(solution)/shard_map/ppermute | solution.py:30
  311.4 31.8 %all-to-all-start.3 = ((bf16[16,128,128]{2,1,0:T(8,128)(2,1)}), bf16[16,128,128]{2,1,0:T(8,128)(2,1)S(1)}, u32[]{:S(2)}, u32[]{:S(2)}) async-start(bf16[16,128,128]{2,1,0:T(8,128)(2,1)} %out_back.1), calls=%async_computation.3 | async-start | bytes 1048576 | tf_op jit(solution)/shard_map/all_to_all | solution.py:831
  316.7 20.2 %collective-permute-start.53 = (bf16[2,1040,128]{2,1,0:T(8,128)(2,1)S(1)}, bf16[2,1040,128]{2,1,0:T(8,128)(2,1)S(1)}, u32[]{:S(2)}, u32[]{:S(2)}) collective-permute-start(bf16[2,1040,128]{2,1,0:T(8,128)(2,1)S(1)} %get-tuple-element.156), channel_id=1, source_target_pairs={{0,2},{2,0},{4,6},{6,4},{1,3},{3,1},{5,7},{7,5},{8,10},{10,8},{12,... | collective-permute-start | bytes 1597448 | tf_op jit(solution)/shard_map/ppermute | solution.py:30
  318.6 19.4 %collective-permute-start.52 = (bf16[2,1040,128]{2,1,0:T(8,128)(2,1)S(1)}, bf16[2,1040,128]{2,1,0:T(8,128)(2,1)S(1)}, u32[]{:S(2)}, u32[]{:S(2)}) collective-permute-start(bf16[2,1040,128]{2,1,0:T(8,128)(2,1)S(1)} %get-tuple-element.155), channel_id=1, source_target_pairs={{0,6},{2,4},{4,2},{6,0},{1,7},{3,5},{5,3},{7,1},{8,14},{10,12},{12... | collective-permute-start | bytes 1597448 | tf_op jit(solution)/shard_map/ppermute | solution.py:30
  327.6 32.0 %collective-permute-start.54 = (bf16[4,1024,128]{2,1,0:T(8,128)(2,1)}, bf16[4,1024,128]{2,1,0:T(8,128)(2,1)}, u32[]{:S(2)}, u32[]{:S(2)}) collective-permute-start(bf16[4,1024,128]{2,1,0:T(8,128)(2,1)} %pad_maximum_fusion.2), channel_id=1, source_target_pairs={{0,16},{8,24},{16,0},{24,8},{1,17},{9,25},{17,1},{25,9},{2,18},{10... | collective-permute-start | bytes 3145736 | tf_op jit(solution)/shard_map/ppermute | solution.py:30
  329.1 30.5 %collective-permute-start.55 = (bf16[4,1024,128]{2,1,0:T(8,128)(2,1)}, bf16[4,1024,128]{2,1,0:T(8,128)(2,1)}, u32[]{:S(2)}, u32[]{:S(2)}) collective-permute-start(bf16[4,1024,128]{2,1,0:T(8,128)(2,1)} %pad_maximum_fusion.3), channel_id=1, source_target_pairs={{0,24},{8,16},{16,8},{24,0},{1,25},{9,17},{17,9},{25,1},{2,26},{10... | collective-permute-start | bytes 3145736 | tf_op jit(solution)/shard_map/ppermute | solution.py:30
  340.1 25.4 %collective-permute-start.56 = (bf16[4,1040,128]{2,1,0:T(8,128)(2,1)S(1)}, bf16[4,1040,128]{2,1,0:T(8,128)(2,1)}, u32[]{:S(2)}, u32[]{:S(2)}) collective-permute-start(bf16[4,1040,128]{2,1,0:T(8,128)(2,1)S(1)} %pad_maximum_fusion), channel_id=1, source_target_pairs={{0,2},{2,0},{4,6},{6,4},{1,3},{3,1},{5,7},{7,5},{8,10},{10,8},{12,... | collective-permute-start | bytes 3194888 | tf_op jit(solution)/shard_map/ppermute | solution.py:30
  341.5 26.5 %collective-permute-start.57 = (bf16[4,1040,128]{2,1,0:T(8,128)(2,1)}, bf16[4,1040,128]{2,1,0:T(8,128)(2,1)}, u32[]{:S(2)}, u32[]{:S(2)}) collective-permute-start(bf16[4,1040,128]{2,1,0:T(8,128)(2,1)} %pad_maximum_fusion.1), channel_id=1, source_target_pairs={{0,6},{2,4},{4,2},{6,0},{1,7},{3,5},{5,3},{7,1},{8,14},{10,12},{12... | collective-permute-start | bytes 3194888 | tf_op jit(solution)/shard_map/ppermute | solution.py:30
  368.0 30.1 %all-to-all-start.4 = ((bf16[16,3,128,128]{3,2,1,0:T(8,128)(2,1)}), bf16[16,3,128,128]{3,2,1,0:T(8,128)(2,1)}, u32[]{:S(2)}, u32[]{:S(2)}) async-start(bf16[16,3,128,128]{3,2,1,0:T(8,128)(2,1)} %attend_back.1), calls=%async_computation.4 | async-start | bytes 3145728 | tf_op jit(solution)/shard_map/all_to_all | solution.py:831
  423.7 62.6 %collective-permute-start.66 = (bf16[128,2048]{1,0:T(8,128)(2,1)}, bf16[128,2048]{1,0:T(8,128)(2,1)}, u32[]{:S(2)}, u32[]{:S(2)}) collective-permute-start(bf16[128,2048]{1,0:T(8,128)(2,1)} %pad_maximum_fusion.13), channel_id=1, source_target_pairs={{0,96},{32,64},{64,32},{96,0},{1,97},{33,65},{65,33},{97,1},{2,98}... | collective-permute-start | bytes 1572872 | tf_op jit(solution)/shard_map/ppermute | solution.py:30
  425.4 14.7 %collective-permute-start.73 = (bf16[2,1024,128]{2,1,0:T(8,128)(2,1)S(1)}, bf16[2,1024,128]{2,1,0:T(8,128)(2,1)S(1)}, u32[]{:S(2)}, u32[]{:S(2)}) collective-permute-start(bf16[2,1024,128]{2,1,0:T(8,128)(2,1)S(1)} %get-tuple-element.161), channel_id=1, source_target_pairs={{0,6},{2,4},{4,2},{6,0},{1,7},{3,5},{5,3},{7,1},{8,14},{10,12},{12... | collective-permute-start | bytes 1572872 | tf_op jit(solution)/shard_map/ppermute | solution.py:30
  430.8 17.0 %collective-permute-start.62 = (bf16[128,2048]{1,0:T(8,128)(2,1)S(1)}, bf16[128,2048]{1,0:T(8,128)(2,1)S(1)}, u32[]{:S(2)}, u32[]{:S(2)}) collective-permute-start(bf16[128,2048]{1,0:T(8,128)(2,1)S(1)} %pad_maximum_fusion.10), channel_id=1, source_target_pairs={{0,32},{32,0},{64,96},{96,64},{1,33},{33,1},{65,97},{97,65},{2,34}... | collective-permute-start | bytes 1572872 | tf_op jit(solution)/shard_map/ppermute | solution.py:30
  431.1 21.3 %collective-permute-start.64 = (bf16[128,2048]{1,0:T(8,128)(2,1)S(1)}, bf16[128,2048]{1,0:T(8,128)(2,1)S(1)}, u32[]{:S(2)}, u32[]{:S(2)}) collective-permute-start(bf16[128,2048]{1,0:T(8,128)(2,1)S(1)} %pad_maximum_fusion.11), channel_id=1, source_target_pairs={{0,96},{32,64},{64,32},{96,0},{1,97},{33,65},{65,33},{97,1},{2,98}... | collective-permute-start | bytes 1572872 | tf_op jit(solution)/shard_map/ppermute | solution.py:30
  443.9 14.0 %collective-permute-start.86 = (bf16[1024,128]{1,0:T(8,128)(2,1)S(1)}, bf16[1024,128]{1,0:T(8,128)(2,1)S(1)}, u32[]{:S(2)}, u32[]{:S(2)}) collective-permute-start(bf16[1024,128]{1,0:T(8,128)(2,1)S(1)} %get-tuple-element.194), channel_id=1, source_target_pairs={{0,6},{2,4},{4,2},{6,0},{1,7},{3,5},{5,3},{7,1},{8,14},{10,12},{12... | collective-permute-start | bytes 786440 | tf_op jit(solution)/shard_map/ppermute | solution.py:30
  452.4 17.6 %collective-permute-start.89 = (bf16[1040,128]{1,0:T(8,128)(2,1)}, bf16[1040,128]{1,0:T(8,128)(2,1)}, u32[]{:S(2)}, u32[]{:S(2)}) collective-permute-start(bf16[1040,128]{1,0:T(8,128)(2,1)} %get-tuple-element.191), channel_id=1, source_target_pairs={{0,24},{8,16},{16,8},{24,0},{1,25},{9,17},{17,9},{25,1},{2,26},{10... | collective-permute-start | bytes 798728 | tf_op jit(solution)/shard_map/ppermute | solution.py:30
  470.0 21.7 %collective-permute-start.74 = (bf16[4,1024,128]{2,1,0:T(8,128)(2,1)}, bf16[4,1024,128]{2,1,0:T(8,128)(2,1)S(1)}, u32[]{:S(2)}, u32[]{:S(2)}) collective-permute-start(bf16[4,1024,128]{2,1,0:T(8,128)(2,1)} %pad_maximum_fusion.4), channel_id=1, source_target_pairs={{0,2},{2,0},{4,6},{6,4},{1,3},{3,1},{5,7},{7,5},{8,10},{10,8},{12,... | collective-permute-start | bytes 3145736 | tf_op jit(solution)/shard_map/ppermute | solution.py:30
  474.0 21.9 %collective-permute-start.76 = (bf16[4,1024,128]{2,1,0:T(8,128)(2,1)}, bf16[4,1024,128]{2,1,0:T(8,128)(2,1)S(1)}, u32[]{:S(2)}, u32[]{:S(2)}) collective-permute-start(bf16[4,1024,128]{2,1,0:T(8,128)(2,1)} %pad_maximum_fusion.5), channel_id=1, source_target_pairs={{0,6},{2,4},{4,2},{6,0},{1,7},{3,5},{5,3},{7,1},{8,14},{10,12},{12... | collective-permute-start | bytes 3145736 | tf_op jit(solution)/shard_map/ppermute | solution.py:30
  (117 other events, 1311.6 us)

commit v5 on v4

--- a/solution.py
+++ b/solution.py
@@ -710,8 +710,10 @@
 
 
 def attend_back_kernel(
-    ends_ref, qkv_ref, grad_ref, out_ref, lse_ref, cos_ref, sin_ref, dqkv_ref, dk_ref, dv_ref
+    ends_ref, qkv_ref, grad_ref, out_ref, lse_ref, cos_ref, sin_ref, dqkv_ref, dk_ref, dv_ref, key_ref
 ):
+    for i in range(SEQ // TILE):
+        key_ref[:, i * TILE : (i + 1) * TILE] = rows_of(qkv_ref, 1, i).astype(f32).T.astype(bf16)
     dk_ref[...] = jnp.zeros_like(dk_ref)
     dv_ref[...] = jnp.zeros_like(dv_ref)
 
@@ -729,7 +731,7 @@
         delta = jnp.broadcast_to(product, (TILE, 128)).T[0:1, :]
         lse = lse_ref[:, here]
         end = visible_end(ends_ref, i * TILE)
-        dq = jnp.zeros((TILE, HEAD_DIM), f32)
+        dq = jnp.zeros((HEAD_DIM, TILE), f32)
         for kb in range(key_blocks(i)):
             there = slice(kb * TILE, (kb + 1) * TILE)
             key = rows_of(qkv_ref, 1, kb)
@@ -741,8 +743,8 @@
             dprobs = dot_nt(rows_of(qkv_ref, 2, kb), grad)
             dscores = (probs * (dprobs - delta)).astype(bf16)
             dk_ref[there, :] += dot_nn(dscores, query)
-            dq = dq + dot_tn(dscores, key)
-        dqkv_ref[2 * i : 2 * i + 2, 0] = turn_back(dq, i)
+            dq = dq + dot_nn(key_ref[:, there], dscores)
+        dqkv_ref[2 * i : 2 * i + 2, 0] = turn_back(dq.T, i)
     for i in range(SEQ // TILE):
         here = slice(i * TILE, (i + 1) * TILE)
         dqkv_ref[2 * i : 2 * i + 2, 1] = turn_back(dk_ref[here, :], i)
@@ -755,7 +757,11 @@
         out_shape=jax.ShapeDtypeStruct((16, 3, 128, HEAD_DIM), bf16),
         in_specs=[smem_spec()] + [vmem_spec()] * 6,
         out_specs=vmem_spec(),
-        scratch_shapes=[pltpu.VMEM((SEQ, HEAD_DIM), f32), pltpu.VMEM((SEQ, HEAD_DIM), f32)],
+        scratch_shapes=[
+            pltpu.VMEM((SEQ, HEAD_DIM), f32),
+            pltpu.VMEM((SEQ, HEAD_DIM), f32),
+            pltpu.VMEM((HEAD_DIM, SEQ), bf16),
+        ],
         compiler_params=params(),
         cost_estimate=cost(15),
         name="attend_back",

time: 524 us -> 524 us (level)
  transfers between devices with their start and end apart: 95 -> 95, of which waited for: 44 -> 44; matrix products, arithmetic and copies ran while one was open for 10% -> 10% of each run, Pallas kernels for 16% -> 15%
where the time goes in v5:
time: 524 us; the launch traced here: 516 us
  waiting for transfers between devices  174 us (33%)
  starting transfers between devices  139 us (27%)
  Pallas kernels  124 us (24%)
  other arithmetic  48.7 us (9%)
  local copies, waits for them, and re-layouts  28.8 us (5%)
    ppermute x90, waiting for transfers between devices, swap(): return lax.ppermute(value, names, [(i, i ^ step) for i in range(count)])  151 us
    ppermute x90, starting transfers between devices, swap(): return lax.ppermute(value, names, [(i, i ^ step) for i in range(count)])  107 us
    pallas_call x8, Pallas kernels, kernel_call(): pl.pallas_call(kernel, out_shape=out_shape, in_specs=[smem_spec()] * smem...  87.6 us
    all_to_all x4, starting transfers between devices, exchange(): lax.all_to_all(value, blkaxes, split_axis=0, concat_axis=0, tiled=True)  23.8 us
    all_to_all x4, waiting for transfers between devices, exchange(): lax.all_to_all(value, blkaxes, split_axis=0, concat_axis=0, tiled=True)  22.5 us
    unnamed x141, local copies, waits for them, and re-layouts  15.6 us
    pallas_call x1, Pallas kernels, attend_back(): pl.pallas_call(attend_back_kernel, out_shape=jax.ShapeDtypeStruct((16, 3,...  13.6 us
  transfers between devices with their start and end apart: 95, of which 44 were waited for; matrix products, arithmetic and copies ran while one was open for 10% of the time, Pallas kernels for 15%

profile of v5, /device:TPU:8, one launch (start us, length us, event | category | flops | bytes accessed | tf_op | source)
XLA Modules:
  0.0 516.4 jit_solution(14112104848775665224)
XLA Ops:
  0.7 3.3 share.1
  4.0 8.4 %all-to-all-start = ((bf16[16,1024,128]{2,1,0:T(8,128)(2,1)}), bf16[16,1024,128]{2,1,0:T(8,128)(2,1)}, u32[]{:S(2)}, u32[]{:S(2)}) async-start(bf16[16,1024,128]{2,1,0:T(8,128)(2,1)} %share.1), calls=%async_computation | async-start | bytes 8388608 | tf_op jit(solution)/shard_map/all_to_all | solution.py:775
  19.0 11.5 %collective-permute-done.1.refs_4_ = bf16[128,2048]{1,0:T(8,128)(2,1)S(1)} collective-permute-done((bf16[128,2048]{1,0:T(8,128)(2,1)}, bf16[128,2048]{1,0:T(8,128)(2,1)S(1)}, u32[]{:S(2)}, u32[]{:S(2)}) %collective-permute-start.1) | collective-permute-done | bytes 524320 | tf_op jit(solution)/shard_map/ppermute | solution.py:30
  30.8 3.9 collective-permute-start.5
  38.9 3.7 fusion.8
  42.6 17.3 %collective-permute-done.2.refs_2_ = bf16[64,2048]{1,0:T(8,128)(2,1)S(1)} collective-permute-done((bf16[64,2048]{1,0:T(8,128)(2,1)S(1)}, bf16[64,2048]{1,0:T(8,128)(2,1)S(1)}, u32[]{:S(2)}, u32[]{:S(2)}) %collective-permute-start.2) | collective-permute-done | bytes 262176 | tf_op jit(solution)/shard_map/ppermute | solution.py:30
  59.9 4.8 collective-permute-done.3.refs_3_
  69.5 6.9 %collective-permute-start.9 = (bf16[1024,128]{1,0:T(8,128)(2,1)S(1)}, bf16[1024,128]{1,0:T(8,128)(2,1)S(1)}, u32[]{:S(2)}, u32[]{:S(2)}) collective-permute-start(bf16[1024,128]{1,0:T(8,128)(2,1)S(1)} %pad_maximum_fusion.15.own), channel_id=1, source_target_pairs={{0,4},{2,6},{4,0},{6,2},{1,5},{3,7},{5,1},{7,3},{8,12},{10,14},{12... | collective-permute-start | bytes 786440 | tf_op jit(solution)/shard_map/ppermute | solution.py:30
  76.4 3.8 collective-permute-start.12
  80.6 9.4 %project_qkv.1 = bf16[16,3,128,128]{3,2,1,0:T(8,128)(2,1)} custom-call(s32[16]{0:T(128)} %multiply_add_fusion.source_ref, bf16[128,2048]{1,0:T(8,128)(2,1)} %get-tuple-element.65.refs_0_, bf16[128,2048]{1,0:T(8,128)(2,1)} %copy-done.32, bf16[64,2048]{1,0:T(8,128)(2,1)} %copy-done.60, bf16[64,2048]{1,0:T(8,128)(2,1)} %copy-done.61, ...), custom_call_target="tpu_custom_call" | custom-call | flops 11500000256 | tf_op jit(solution)/shard_map/project_qkv/pallas_call | solution.py:305
  93.5 8.1 %all-to-all-start.1 = ((bf16[16,3,128,128]{3,2,1,0:T(8,128)(2,1)}), bf16[16,3,128,128]{3,2,1,0:T(8,128)(2,1)S(1)}, u32[]{:S(2)}, u32[]{:S(2)}) async-start(bf16[16,3,128,128]{3,2,1,0:T(8,128)(2,1)} %project_qkv.1), calls=%async_computation.1 | async-start | bytes 3145728 | tf_op jit(solution)/shard_map/all_to_all | solution.py:837
  104.6 4.0 collective-permute-start.15
  114.4 11.4 %all-to-all-done.1.qkv_ref = bf16[16,3,128,128]{3,2,1,0:T(8,128)(2,1)S(1)} async-done(((bf16[16,3,128,128]{3,2,1,0:T(8,128)(2,1)}), bf16[16,3,128,128]{3,2,1,0:T(8,128)(2,1)S(1)}, u32[]{:S(2)}, u32[]{:S(2)}) %all-to-all-start.1) | async-done | bytes 1572896 | tf_op jit(solution)/shard_map/all_to_all | solution.py:837
  126.9 7.8 %attend.1 = (bf16[16,128,128]{2,1,0:T(8,128)(2,1)}, f32[2048,128]{1,0:T(8,128)}, f32[1,2048]{1,0:T(1,128)}) custom-call(s32[12]{0:T(128)} %bitcast.255, bf16[16,3,128,128]{3,2,1,0:T(8,128)(2,1)} %copy-done.12), custom_call_target="tpu_custom_call" | custom-call | flops 9200000000 | tf_op jit(solution)/shard_map/attend/pallas_call | solution.py:696
  134.8 4.1 all-to-all-start.2
  138.9 3.5 collective-permute-done.14.refs_10_.refs_1_
  142.3 3.4 collective-permute-done.15.refs_13_.refs_4_
  146.4 7.0 %all-to-all-done.2.low_ref = bf16[16,128,128]{2,1,0:T(8,128)(2,1)S(1)} async-done(((bf16[16,128,128]{2,1,0:T(8,128)(2,1)}), bf16[16,128,128]{2,1,0:T(8,128)(2,1)S(1)}, u32[]{:S(2)}, u32[]{:S(2)}) %all-to-all-start.2) | async-done | bytes 524320 | tf_op jit(solution)/shard_map/all_to_all | solution.py:837
  154.2 5.2 %project_out.1 = bf16[4,128,2048]{2,1,0:T(8,128)(2,1)} custom-call(s32[16]{0:T(128)} %multiply_add_fusion.source_ref, bf16[16,128,128]{2,1,0:T(8,128)(2,1)} %copy-done.15, bf16[16,1024,128]{2,1,0:T(8,128)(2,1)} %all-to-all-done.refs_5_.mine_ref, bf16[16,1024,128]{2,1,0:T(8,128)(2,1)} %collective-permute-done.7.refs_6_.theirs_ref), custom_call_target="tpu_custom_call" | custom-call | flops 5750000128 | tf_op jit(solution)/shard_map/project_out/pallas_call | solution.py:305
  164.1 5.6 %collective-permute-done.18 = bf16[64,2048]{1,0:T(8,128)(2,1)S(1)} collective-permute-done((bf16[64,2048]{1,0:T(8,128)(2,1)S(1)}, bf16[64,2048]{1,0:T(8,128)(2,1)S(1)}, u32[]{:S(2)}, u32[]{:S(2)}) %collective-permute-start.18) | collective-permute-done | bytes 262176 | tf_op jit(solution)/shard_map/ppermute | solution.py:30
  179.0 5.6 %collective-permute-done.21 = bf16[128,2048]{1,0:T(8,128)(2,1)S(1)} collective-permute-done((bf16[128,2048]{1,0:T(8,128)(2,1)S(1)}, bf16[128,2048]{1,0:T(8,128)(2,1)S(1)}, u32[]{:S(2)}, u32[]{:S(2)}) %collective-permute-start.21) | collective-permute-done | bytes 524320 | tf_op jit(solution)/shard_map/ppermute | solution.py:30
  184.6 4.8 collective-permute-start.34
  192.6 7.4 %collective-permute-done.34.refs_22_.refs_13_ = bf16[2,1040,128]{2,1,0:T(8,128)(2,1)S(1)} collective-permute-done((bf16[2,1040,128]{2,1,0:T(8,128)(2,1)S(1)}, bf16[2,1040,128]{2,1,0:T(8,128)(2,1)S(1)}, u32[]{:S(2)}, u32[]{:S(2)}) %collective-permute-start.34) | collective-permute-done | bytes 532512 | tf_op jit(solution)/shard_map/ppermute | solution.py:30
  206.6 5.6 %collective-permute-done.24.refs_2_ = bf16[64,2048]{1,0:T(8,128)(2,1)S(1)} collective-permute-done((bf16[64,2048]{1,0:T(8,128)(2,1)S(1)}, bf16[64,2048]{1,0:T(8,128)(2,1)S(1)}, u32[]{:S(2)}, u32[]{:S(2)}) %collective-permute-start.24) | collective-permute-done | bytes 262176 | tf_op jit(solution)/shard_map/ppermute | solution.py:30
  220.1 26.6 %mlp.1 = (bf16[2,512,688]{2,1,0:T(8,128)(2,1)}, bf16[2,512,688]{2,1,0:T(8,128)(2,1)}, bf16[2,512,688]{2,1,0:T(8,128)(2,1)}, bf16[4,128,2048]{2,1,0:T(8,128)(2,1)}) custom-call(bf16[128,2048]{1,0:T(8,128)(2,1)} %copy-done.16, bf16[128,2048]{1,0:T(8,128)(2,1)} %copy-done.35, bf16[64,2048]{1,0:T(8,128)(2,1)} %copy-done.64, bf16[64,2048]{1,0:T(8,128)(2,1)} %copy-done.65, ...), custom_call_target="tpu_custom_call" | custom-call | flops 32199999488 | tf_op jit(solution)/shard_map/mlp/pallas_call | solution.py:305
  250.2 7.6 %collective-permute-done.40 = bf16[64,2048]{1,0:T(8,128)(2,1)S(1)} collective-permute-done((bf16[64,2048]{1,0:T(8,128)(2,1)S(1)}, bf16[64,2048]{1,0:T(8,128)(2,1)S(1)}, u32[]{:S(2)}, u32[]{:S(2)}) %collective-permute-start.40) | collective-permute-done | bytes 262176 | tf_op jit(solution)/shard_map/ppermute | solution.py:30
  260.2 14.3 %mlp_grad.1 = (bf16[4,4,1024,128]{3,2,1,0:T(8,128)(2,1)}, bf16[4,4,1024,128]{3,2,1,0:T(8,128)(2,1)}, bf16[4,4,1040,128]{3,2,1,0:T(8,128)(2,1)}, bf16[4,4,1040,128]{3,2,1,0:T(8,128)(2,1)}) custom-call(bf16[2,512,688]{2,1,0:T(8,128)(2,1)} %get-tuple-element.88.d_gate_ref, bf16[2,512,688]{2,1,0:T(8,128)(2,1)} %get-tuple-element.89.d_up_ref, ...), custom_call_target="tpu_custom_call" | custom-call | flops 20700000256 | tf_op jit(solution)/shard_map/mlp_grad/pallas_call | solution.py:305
  281.4 12.4 %collective-permute-done.47.refs_4_.refs_9_ = bf16[128,2048]{1,0:T(8,128)(2,1)S(1)} collective-permute-done((bf16[128,2048]{1,0:T(8,128)(2,1)S(1)}, bf16[128,2048]{1,0:T(8,128)(2,1)S(1)}, u32[]{:S(2)}, u32[]{:S(2)}) %collective-permute-start.47) | collective-permute-done | bytes 524320 | tf_op jit(solution)/shard_map/ppermute | solution.py:30
  296.5 3.2 fusion.32
  305.3 6.1 %out_back.1 = bf16[16,128,128]{2,1,0:T(8,128)(2,1)} custom-call(s32[16]{0:T(128)} %multiply_add_fusion.source_ref, bf16[128,2048]{1,0:T(8,128)(2,1)} %copy-done.19, bf16[128,2048]{1,0:T(8,128)(2,1)} %copy-done.34, bf16[64,2048]{1,0:T(8,128)(2,1)} %copy-done.62, bf16[64,2048]{1,0:T(8,128)(2,1)} %copy-done.63, bf16[128,2048]{1,0:T(8,128)(2,1)} %copy-done.33, ...), custom_call_target="tpu_custom_call" | custom-call | flops 6899999744 | tf_op jit(solution)/shard_map/out_back/pallas_call | solution.py:305
  311.4 5.2 %all-to-all-start.3 = ((bf16[16,128,128]{2,1,0:T(8,128)(2,1)}), bf16[16,128,128]{2,1,0:T(8,128)(2,1)S(1)}, u32[]{:S(2)}, u32[]{:S(2)}) async-start(bf16[16,128,128]{2,1,0:T(8,128)(2,1)} %out_back.1), calls=%async_computation.3 | async-start | bytes 1048576 | tf_op jit(solution)/shard_map/all_to_all | solution.py:837
  329.1 3.1 collective-permute-start.55
  332.2 4.6 collective-permute-done.53
  344.1 13.6 %attend_back.1 = bf16[16,3,128,128]{3,2,1,0:T(8,128)(2,1)} custom-call(s32[12]{0:T(128)} %bitcast.256, bf16[16,3,128,128]{3,2,1,0:T(8,128)(2,1)} %copy-done.12, bf16[16,128,128]{2,1,0:T(8,128)(2,1)} %copy-done.17, f32[2048,128]{1,0:T(8,128)} %get-tuple-element.101.out_ref, f32[1,2048]{1,0:T(1,128)} %get-tuple-element.102.lse_ref, f32[2048,128]{1,0:T(8,128)} %copy-done.14, ...), custom_call_target="tpu_custom_call" | custom-call | flops 17250000896 | tf_op jit(solution)/shard_map/attend_back/pallas_call | solution.py:755
  357.7 7.8 %collective-permute-done.56 = bf16[4,1040,128]{2,1,0:T(8,128)(2,1)} collective-permute-done((bf16[4,1040,128]{2,1,0:T(8,128)(2,1)S(1)}, bf16[4,1040,128]{2,1,0:T(8,128)(2,1)}, u32[]{:S(2)}, u32[]{:S(2)}) %collective-permute-start.56) | collective-permute-done | bytes 1064992 | tf_op jit(solution)/shard_map/ppermute | solution.py:30
  368.0 6.4 %all-to-all-start.4 = ((bf16[16,3,128,128]{3,2,1,0:T(8,128)(2,1)}), bf16[16,3,128,128]{3,2,1,0:T(8,128)(2,1)}, u32[]{:S(2)}, u32[]{:S(2)}) async-start(bf16[16,3,128,128]{3,2,1,0:T(8,128)(2,1)} %attend_back.1), calls=%async_computation.4 | async-start | bytes 3145728 | tf_op jit(solution)/shard_map/all_to_all | solution.py:837
  374.3 8.0 %project_down.1 = bf16[4,128,2048]{2,1,0:T(8,128)(2,1)} custom-call(bf16[2,512,688]{2,1,0:T(8,128)(2,1)} %get-tuple-element.104.hidden_ref, bf16[4,1024,128]{2,1,0:T(8,128)(2,1)} %stack.2.refs_9_.refs_0_, bf16[4,1024,128]{2,1,0:T(8,128)(2,1)} %collective-permute-done.14.refs_10_.refs_1_, bf16[2,1024,128]{2,1,0:T(8,128)(2,1)} %copy-done.54, ...), custom_call_target="tpu_custom_call" | custom-call | flops 9200000000 | tf_op jit(solution)/shard_map/project_down/pallas_call | solution.py:305
  388.6 3.7 fusion.5
  393.9 4.2 all-to-all-done.4.dqkv_ref
  398.1 9.3 %qkv_grad.1 = (bf16[4,4,1024,128]{3,2,1,0:T(8,128)(2,1)}, bf16[4,4,1024,128]{3,2,1,0:T(8,128)(2,1)}) custom-call(bf16[16,3,128,128]{3,2,1,0:T(8,128)(2,1)} %all-to-all-done.4.dqkv_ref, bf16[16,128,128]{2,1,0:T(8,128)(2,1)} %copy-done.15, bf16[128,2048]{1,0:T(8,128)(2,1)} %get-tuple-element.65.refs_0_, bf16[128,2048]{1,0:T(8,128)(2,1)} %copy-done.32, ...), custom_call_target="tpu_custom_call" | custom-call | flops 11500000256 | tf_op jit(solution)/shard_map/qkv_grad/pallas_call | solution.py:305
  408.6 8.8 %qkv_back.1 = bf16[4,128,2048]{2,1,0:T(8,128)(2,1)} custom-call(s32[16]{0:T(128)} %multiply_add_fusion.source_ref, bf16[16,3,128,128]{3,2,1,0:T(8,128)(2,1)} %all-to-all-done.4.dqkv_ref, bf16[16,1024,128]{2,1,0:T(8,128)(2,1)} %all-to-all-done.refs_5_.mine_ref, bf16[16,1024,128]{2,1,0:T(8,128)(2,1)} %collective-permute-done.7.refs_6_.theirs_ref), custom_call_target="tpu_custom_call" | custom-call | flops 10350000128 | tf_op jit(solution)/shard_map/qkv_back/pallas_call | solution.py:305
  425.4 3.0 collective-permute-start.73
  434.2 4.6 collective-permute-done.75
  448.9 3.4 collective-permute-done.64
  453.2 4.7 collective-permute-done.86
  470.1 4.0 collective-permute-done.88
  474.0 3.5 collective-permute-start.76
  491.7 4.3 collective-permute-done.76
  (392 shorter events, 185.5 us)
Async XLA Ops:
  4.0 62.0 %all-to-all-start = ((bf16[16,1024,128]{2,1,0:T(8,128)(2,1)}), bf16[16,1024,128]{2,1,0:T(8,128)(2,1)}, u32[]{:S(2)}, u32[]{:S(2)}) async-start(bf16[16,1024,128]{2,1,0:T(8,128)(2,1)} %share.1), calls=%async_computation | async-start | bytes 8388608 | tf_op jit(solution)/shard_map/all_to_all | solution.py:775
  15.9 14.6 %collective-permute-start.1 = (bf16[128,2048]{1,0:T(8,128)(2,1)}, bf16[128,2048]{1,0:T(8,128)(2,1)S(1)}, u32[]{:S(2)}, u32[]{:S(2)}) collective-permute-start(bf16[128,2048]{1,0:T(8,128)(2,1)} %get-tuple-element.65.refs_0_), channel_id=1, source_target_pairs={{0,96},{32,64},{64,32},{96,0},{1,97},{33,65},{65,33},{97,1},{2,98}... | collective-permute-start | bytes 1572872 | tf_op jit(solution)/shard_map/ppermute | solution.py:30
  18.7 16.6 %collective-permute-start = (bf16[128,2048]{1,0:T(8,128)(2,1)}, bf16[128,2048]{1,0:T(8,128)(2,1)S(1)}, u32[]{:S(2)}, u32[]{:S(2)}) collective-permute-start(bf16[128,2048]{1,0:T(8,128)(2,1)} %get-tuple-element.65.refs_0_), channel_id=1, source_target_pairs={{0,32},{32,0},{64,96},{96,64},{1,33},{33,1},{65,97},{97,65},{2,34}... | collective-permute-start | bytes 1572872 | tf_op jit(solution)/shard_map/ppermute | solution.py:30
  30.5 34.9 %collective-permute-start.4 = (bf16[128,2048]{1,0:T(8,128)(2,1)}, bf16[128,2048]{1,0:T(8,128)(2,1)}, u32[]{:S(2)}, u32[]{:S(2)}) collective-permute-start(bf16[128,2048]{1,0:T(8,128)(2,1)} %get-tuple-element.67.refs_5_), channel_id=1, source_target_pairs={{0,32},{32,0},{64,96},{96,64},{1,33},{33,1},{65,97},{97,65},{2,34}... | collective-permute-start | bytes 1572872 | tf_op jit(solution)/shard_map/ppermute | solution.py:30
  30.8 34.7 %collective-permute-start.5 = (bf16[128,2048]{1,0:T(8,128)(2,1)}, bf16[128,2048]{1,0:T(8,128)(2,1)}, u32[]{:S(2)}, u32[]{:S(2)}) collective-permute-start(bf16[128,2048]{1,0:T(8,128)(2,1)} %get-tuple-element.67.refs_5_), channel_id=1, source_target_pairs={{0,64},{32,96},{64,0},{96,32},{1,65},{33,97},{65,1},{97,33},{2,66}... | collective-permute-start | bytes 1572872 | tf_op jit(solution)/shard_map/ppermute | solution.py:30
  34.7 30.7 %collective-permute-start.6 = (bf16[128,2048]{1,0:T(8,128)(2,1)}, bf16[128,2048]{1,0:T(8,128)(2,1)}, u32[]{:S(2)}, u32[]{:S(2)}) collective-permute-start(bf16[128,2048]{1,0:T(8,128)(2,1)} %get-tuple-element.67.refs_5_), channel_id=1, source_target_pairs={{0,96},{32,64},{64,32},{96,0},{1,97},{33,65},{65,33},{97,1},{2,98}... | collective-permute-start | bytes 1572872 | tf_op jit(solution)/shard_map/ppermute | solution.py:30
  35.2 24.7 %collective-permute-start.2 = (bf16[64,2048]{1,0:T(8,128)(2,1)S(1)}, bf16[64,2048]{1,0:T(8,128)(2,1)S(1)}, u32[]{:S(2)}, u32[]{:S(2)}) collective-permute-start(bf16[64,2048]{1,0:T(8,128)(2,1)S(1)} %slice.610), channel_id=1, source_target_pairs={{0,32},{32,0},{64,96},{96,64},{1,33},{33,1},{65,97},{97,65},{2,34}... | collective-permute-start | bytes 786440 | tf_op jit(solution)/shard_map/ppermute | solution.py:30
  36.1 28.6 %collective-permute-start.3 = (bf16[64,2048]{1,0:T(8,128)(2,1)S(1)}, bf16[64,2048]{1,0:T(8,128)(2,1)S(1)}, u32[]{:S(2)}, u32[]{:S(2)}) collective-permute-start(bf16[64,2048]{1,0:T(8,128)(2,1)S(1)} %slice.611), channel_id=1, source_target_pairs={{0,96},{32,64},{64,32},{96,0},{1,97},{33,65},{65,33},{97,1},{2,98}... | collective-permute-start | bytes 786440 | tf_op jit(solution)/shard_map/ppermute | solution.py:30
  66.0 14.2 %collective-permute-start.7 = (bf16[16,1024,128]{2,1,0:T(8,128)(2,1)}, bf16[16,1024,128]{2,1,0:T(8,128)(2,1)}, u32[]{:S(2)}, u32[]{:S(2)}) collective-permute-start(bf16[16,1024,128]{2,1,0:T(8,128)(2,1)} %all-to-all-done.refs_5_.mine_ref), channel_id=1, source_target_pairs={{0,1},{1,0},{2,3},{3,2},{4,5},{5,4},{6,7},{7,6},{8,9},{9,8},{10,11... | collective-permute-start | bytes 12582920 | tf_op jit(solution)/shard_map/ppermute | solution.py:30
  69.5 20.6 %collective-permute-start.9 = (bf16[1024,128]{1,0:T(8,128)(2,1)S(1)}, bf16[1024,128]{1,0:T(8,128)(2,1)S(1)}, u32[]{:S(2)}, u32[]{:S(2)}) collective-permute-start(bf16[1024,128]{1,0:T(8,128)(2,1)S(1)} %pad_maximum_fusion.15.own), channel_id=1, source_target_pairs={{0,4},{2,6},{4,0},{6,2},{1,5},{3,7},{5,1},{7,3},{8,12},{10,14},{12... | collective-permute-start | bytes 786440 | tf_op jit(solution)/shard_map/ppermute | solution.py:30
  76.4 15.0 %collective-permute-start.10 = (bf16[1024,128]{1,0:T(8,128)(2,1)S(1)}, bf16[1024,128]{1,0:T(8,128)(2,1)S(1)}, u32[]{:S(2)}, u32[]{:S(2)}) collective-permute-start(bf16[1024,128]{1,0:T(8,128)(2,1)S(1)} %pad_maximum_fusion.15.own), channel_id=1, source_target_pairs={{0,6},{2,4},{4,2},{6,0},{1,7},{3,5},{5,3},{7,1},{8,14},{10,12},{12... | collective-permute-start | bytes 786440 | tf_op jit(solution)/shard_map/ppermute | solution.py:30
  76.4 15.0 %collective-permute-start.11 = (bf16[1040,128]{1,0:T(8,128)(2,1)S(1)}, bf16[1040,128]{1,0:T(8,128)(2,1)S(1)}, u32[]{:S(2)}, u32[]{:S(2)}) collective-permute-start(bf16[1040,128]{1,0:T(8,128)(2,1)S(1)} %pad_maximum_fusion.14.own), channel_id=1, source_target_pairs={{0,16},{8,24},{16,0},{24,8},{1,17},{9,25},{17,1},{25,9},{2,18},{10... | collective-permute-start | bytes 798728 | tf_op jit(solution)/shard_map/ppermute | solution.py:30
  76.4 15.0 %collective-permute-start.12 = (bf16[1040,128]{1,0:T(8,128)(2,1)S(1)}, bf16[1040,128]{1,0:T(8,128)(2,1)S(1)}, u32[]{:S(2)}, u32[]{:S(2)}) collective-permute-start(bf16[1040,128]{1,0:T(8,128)(2,1)S(1)} %pad_maximum_fusion.14.own), channel_id=1, source_target_pairs={{0,8},{8,0},{16,24},{24,16},{1,9},{9,1},{17,25},{25,17},{2,10},{10... | collective-permute-start | bytes 798728 | tf_op jit(solution)/shard_map/ppermute | solution.py:30
  93.5 32.3 %all-to-all-start.1 = ((bf16[16,3,128,128]{3,2,1,0:T(8,128)(2,1)}), bf16[16,3,128,128]{3,2,1,0:T(8,128)(2,1)S(1)}, u32[]{:S(2)}, u32[]{:S(2)}) async-start(bf16[16,3,128,128]{3,2,1,0:T(8,128)(2,1)} %project_qkv.1), calls=%async_computation.1 | async-start | bytes 3145728 | tf_op jit(solution)/shard_map/all_to_all | solution.py:837
  104.5 37.8 %collective-permute-start.14 = (bf16[4,1024,128]{2,1,0:T(8,128)(2,1)}, bf16[4,1024,128]{2,1,0:T(8,128)(2,1)}, u32[]{:S(2)}, u32[]{:S(2)}) collective-permute-start(bf16[4,1024,128]{2,1,0:T(8,128)(2,1)} %stack.2.refs_9_.refs_0_), channel_id=1, source_target_pairs={{0,16},{8,24},{16,0},{24,8},{1,17},{9,25},{17,1},{25,9},{2,18},{10... | collective-permute-start | bytes 3145736 | tf_op jit(solution)/shard_map/ppermute | solution.py:30
  104.6 41.1 %collective-permute-start.15 = (bf16[4,1024,128]{2,1,0:T(8,128)(2,1)}, bf16[4,1024,128]{2,1,0:T(8,128)(2,1)}, u32[]{:S(2)}, u32[]{:S(2)}) collective-permute-start(bf16[4,1024,128]{2,1,0:T(8,128)(2,1)} %stack.2.refs_9_.refs_0_), channel_id=1, source_target_pairs={{0,24},{8,16},{16,8},{24,0},{1,25},{9,17},{17,9},{25,1},{2,26},{10... | collective-permute-start | bytes 3145736 | tf_op jit(solution)/shard_map/ppermute | solution.py:30
  110.8 34.9 %collective-permute-start.16 = (bf16[4,1040,128]{2,1,0:T(8,128)(2,1)}, bf16[4,1040,128]{2,1,0:T(8,128)(2,1)S(1)}, u32[]{:S(2)}, u32[]{:S(2)}) collective-permute-start(bf16[4,1040,128]{2,1,0:T(8,128)(2,1)} %stack.3.refs_19_.refs_10_), channel_id=1, source_target_pairs={{0,2},{2,0},{4,6},{6,4},{1,3},{3,1},{5,7},{7,5},{8,10},{10,8},{12,... | collective-permute-start | bytes 3194888 | tf_op jit(solution)/shard_map/ppermute | solution.py:30
  112.4 34.0 %collective-permute-start.17 = (bf16[4,1040,128]{2,1,0:T(8,128)(2,1)}, bf16[4,1040,128]{2,1,0:T(8,128)(2,1)}, u32[]{:S(2)}, u32[]{:S(2)}) collective-permute-start(bf16[4,1040,128]{2,1,0:T(8,128)(2,1)} %stack.3.refs_19_.refs_10_), channel_id=1, source_target_pairs={{0,6},{2,4},{4,2},{6,0},{1,7},{3,5},{5,3},{7,1},{8,14},{10,12},{12... | collective-permute-start | bytes 3194888 | tf_op jit(solution)/shard_map/ppermute | solution.py:30
  134.8 18.7 %all-to-all-start.2 = ((bf16[16,128,128]{2,1,0:T(8,128)(2,1)}), bf16[16,128,128]{2,1,0:T(8,128)(2,1)S(1)}, u32[]{:S(2)}, u32[]{:S(2)}) async-start(bf16[16,128,128]{2,1,0:T(8,128)(2,1)} %get-tuple-element.73), calls=%async_computation.2 | async-start | bytes 1048576 | tf_op jit(solution)/shard_map/all_to_all | solution.py:837
  172.8 16.6 %collective-permute-start.19 = (bf16[128,2048]{1,0:T(8,128)(2,1)S(1)}, bf16[128,2048]{1,0:T(8,128)(2,1)S(1)}, u32[]{:S(2)}, u32[]{:S(2)}) collective-permute-start(bf16[128,2048]{1,0:T(8,128)(2,1)S(1)} %pad_maximum_fusion.6), channel_id=1, source_target_pairs={{0,32},{32,0},{64,96},{96,64},{1,33},{33,1},{65,97},{97,65},{2,34}... | collective-permute-start | bytes 1572872 | tf_op jit(solution)/shard_map/ppermute | solution.py:30
  174.1 16.1 %collective-permute-start.26 = (bf16[2,1024,128]{2,1,0:T(8,128)(2,1)S(1)}, bf16[2,1024,128]{2,1,0:T(8,128)(2,1)S(1)}, u32[]{:S(2)}, u32[]{:S(2)}) collective-permute-start(bf16[2,1024,128]{2,1,0:T(8,128)(2,1)S(1)} %slice.623), channel_id=1, source_target_pairs={{0,16},{8,24},{16,0},{24,8},{1,17},{9,25},{17,1},{25,9},{2,18},{10... | collective-permute-start | bytes 1572872 | tf_op jit(solution)/shard_map/ppermute | solution.py:30
  175.3 16.7 %collective-permute-start.27 = (bf16[2,1024,128]{2,1,0:T(8,128)(2,1)S(1)}, bf16[2,1024,128]{2,1,0:T(8,128)(2,1)S(1)}, u32[]{:S(2)}, u32[]{:S(2)}) collective-permute-start(bf16[2,1024,128]{2,1,0:T(8,128)(2,1)S(1)} %slice.624), channel_id=1, source_target_pairs={{0,24},{8,16},{16,8},{24,0},{1,25},{9,17},{17,9},{25,1},{2,26},{10... | collective-permute-start | bytes 1572872 | tf_op jit(solution)/shard_map/ppermute | solution.py:30
  184.6 15.3 %collective-permute-start.34 = (bf16[2,1040,128]{2,1,0:T(8,128)(2,1)S(1)}, bf16[2,1040,128]{2,1,0:T(8,128)(2,1)S(1)}, u32[]{:S(2)}, u32[]{:S(2)}) collective-permute-start(bf16[2,1040,128]{2,1,0:T(8,128)(2,1)S(1)} %slice.626), channel_id=1, source_target_pairs={{0,6},{2,4},{4,2},{6,0},{1,7},{3,5},{5,3},{7,1},{8,14},{10,12},{12... | collective-permute-start | bytes 1597448 | tf_op jit(solution)/shard_map/ppermute | solution.py:30
  192.0 21.7 %collective-permute-start.28 = (bf16[4,1024,128]{2,1,0:T(8,128)(2,1)S(1)}, bf16[4,1024,128]{2,1,0:T(8,128)(2,1)S(1)}, u32[]{:S(2)}, u32[]{:S(2)}) collective-permute-start(bf16[4,1024,128]{2,1,0:T(8,128)(2,1)S(1)} %copy-done.47), channel_id=1, source_target_pairs={{0,1},{1,0},{2,3},{3,2},{4,5},{5,4},{6,7},{7,6},{8,9},{9,8},{10,11... | collective-permute-start | bytes 3145736 | tf_op jit(solution)/shard_map/ppermute | solution.py:30
  258.4 16.0 %collective-permute-start.43 = (bf16[128,2048]{1,0:T(8,128)(2,1)S(1)}, bf16[128,2048]{1,0:T(8,128)(2,1)S(1)}, u32[]{:S(2)}, u32[]{:S(2)}) collective-permute-start(bf16[128,2048]{1,0:T(8,128)(2,1)S(1)} %pad_maximum_fusion.9), channel_id=1, source_target_pairs={{0,96},{32,64},{64,32},{96,0},{1,97},{33,65},{65,33},{97,1},{2,98}... | collective-permute-start | bytes 1572872 | tf_op jit(solution)/shard_map/ppermute | solution.py:30
  260.1 14.4 %collective-permute-start.41 = (bf16[128,2048]{1,0:T(8,128)(2,1)S(1)}, bf16[128,2048]{1,0:T(8,128)(2,1)S(1)}, u32[]{:S(2)}, u32[]{:S(2)}) collective-permute-start(bf16[128,2048]{1,0:T(8,128)(2,1)S(1)} %pad_maximum_fusion.8), channel_id=1, source_target_pairs={{0,32},{32,0},{64,96},{96,64},{1,33},{33,1},{65,97},{97,65},{2,34}... | collective-permute-start | bytes 1572872 | tf_op jit(solution)/shard_map/ppermute | solution.py:30
  277.0 19.6 %collective-permute-start.44 = (bf16[4,4,1024,128]{3,2,1,0:T(8,128)(2,1)}, bf16[4,4,1024,128]{3,2,1,0:T(8,128)(2,1)S(1)}, u32[]{:S(2)}, u32[]{:S(2)}) collective-permute-start(bf16[4,4,1024,128]{3,2,1,0:T(8,128)(2,1)} %get-tuple-element.93), channel_id=1, source_target_pairs={{0,1},{1,0},{2,3},{3,2},{4,5},{5,4},{6,7},{7,6},{8,9},{9,8},{10,11... | collective-permute-start | bytes 12582920 | tf_op jit(solution)/shard_map/ppermute | solution.py:30
  278.2 22.0 %collective-permute-start.45 = (bf16[4,4,1040,128]{3,2,1,0:T(8,128)(2,1)S(1)}, bf16[4,4,1040,128]{3,2,1,0:T(8,128)(2,1)S(1)}, u32[]{:S(2)}, u32[]{:S(2)}) collective-permute-start(bf16[4,4,1040,128]{3,2,1,0:T(8,128)(2,1)S(1)} %copy-done.43), channel_id=1, source_target_pairs={{0,1},{1,0},{2,3},{3,2},{4,5},{5,4},{6,7},{7,6},{8,9},{9,8},{10,11... | collective-permute-start | bytes 12779528 | tf_op jit(solution)/shard_map/ppermute | solution.py:30
  278.2 15.5 %collective-permute-start.47 = (bf16[128,2048]{1,0:T(8,128)(2,1)S(1)}, bf16[128,2048]{1,0:T(8,128)(2,1)S(1)}, u32[]{:S(2)}, u32[]{:S(2)}) collective-permute-start(bf16[128,2048]{1,0:T(8,128)(2,1)S(1)} %get-tuple-element.97.refs_0_.refs_5_), channel_id=1, source_target_pairs={{0,96},{32,64},{64,32},{96,0},{1,97},{33,65},{65,33},{97,1},{2,98}... | collective-permute-start | bytes 1572872 | tf_op jit(solution)/shard_map/ppermute | solution.py:30
  280.0 14.7 %collective-permute-start.46 = (bf16[128,2048]{1,0:T(8,128)(2,1)S(1)}, bf16[128,2048]{1,0:T(8,128)(2,1)S(1)}, u32[]{:S(2)}, u32[]{:S(2)}) collective-permute-start(bf16[128,2048]{1,0:T(8,128)(2,1)S(1)} %get-tuple-element.97.refs_0_.refs_5_), channel_id=1, source_target_pairs={{0,32},{32,0},{64,96},{96,64},{1,33},{33,1},{65,97},{97,65},{2,34}... | collective-permute-start | bytes 1572872 | tf_op jit(solution)/shard_map/ppermute | solution.py:30
  299.8 24.5 %collective-permute-start.51 = (bf16[2,1024,128]{2,1,0:T(8,128)(2,1)}, bf16[2,1024,128]{2,1,0:T(8,128)(2,1)}, u32[]{:S(2)}, u32[]{:S(2)}) collective-permute-start(bf16[2,1024,128]{2,1,0:T(8,128)(2,1)} %get-tuple-element.168), channel_id=1, source_target_pairs={{0,16},{8,24},{16,0},{24,8},{1,17},{9,25},{17,1},{25,9},{2,18},{10... | collective-permute-start | bytes 1572872 | tf_op jit(solution)/shard_map/ppermute | solution.py:30
  299.8 24.5 %collective-permute-start.50 = (bf16[2,1024,128]{2,1,0:T(8,128)(2,1)}, bf16[2,1024,128]{2,1,0:T(8,128)(2,1)}, u32[]{:S(2)}, u32[]{:S(2)}) collective-permute-start(bf16[2,1024,128]{2,1,0:T(8,128)(2,1)} %get-tuple-element.167), channel_id=1, source_target_pairs={{0,24},{8,16},{16,8},{24,0},{1,25},{9,17},{17,9},{25,1},{2,26},{10... | collective-permute-start | bytes 1572872 | tf_op jit(solution)/shard_map/ppermute | solution.py:30
  311.4 31.8 %all-to-all-start.3 = ((bf16[16,128,128]{2,1,0:T(8,128)(2,1)}), bf16[16,128,128]{2,1,0:T(8,128)(2,1)S(1)}, u32[]{:S(2)}, u32[]{:S(2)}) async-start(bf16[16,128,128]{2,1,0:T(8,128)(2,1)} %out_back.1), calls=%async_computation.3 | async-start | bytes 1048576 | tf_op jit(solution)/shard_map/all_to_all | solution.py:837
  316.7 20.2 %collective-permute-start.53 = (bf16[2,1040,128]{2,1,0:T(8,128)(2,1)S(1)}, bf16[2,1040,128]{2,1,0:T(8,128)(2,1)S(1)}, u32[]{:S(2)}, u32[]{:S(2)}) collective-permute-start(bf16[2,1040,128]{2,1,0:T(8,128)(2,1)S(1)} %get-tuple-element.156), channel_id=1, source_target_pairs={{0,2},{2,0},{4,6},{6,4},{1,3},{3,1},{5,7},{7,5},{8,10},{10,8},{12,... | collective-permute-start | bytes 1597448 | tf_op jit(solution)/shard_map/ppermute | solution.py:30
  318.6 19.4 %collective-permute-start.52 = (bf16[2,1040,128]{2,1,0:T(8,128)(2,1)S(1)}, bf16[2,1040,128]{2,1,0:T(8,128)(2,1)S(1)}, u32[]{:S(2)}, u32[]{:S(2)}) collective-permute-start(bf16[2,1040,128]{2,1,0:T(8,128)(2,1)S(1)} %get-tuple-element.155), channel_id=1, source_target_pairs={{0,6},{2,4},{4,2},{6,0},{1,7},{3,5},{5,3},{7,1},{8,14},{10,12},{12... | collective-permute-start | bytes 1597448 | tf_op jit(solution)/shard_map/ppermute | solution.py:30
  327.6 30.1 %collective-permute-start.54 = (bf16[4,1024,128]{2,1,0:T(8,128)(2,1)}, bf16[4,1024,128]{2,1,0:T(8,128)(2,1)}, u32[]{:S(2)}, u32[]{:S(2)}) collective-permute-start(bf16[4,1024,128]{2,1,0:T(8,128)(2,1)} %pad_maximum_fusion.2), channel_id=1, source_target_pairs={{0,16},{8,24},{16,0},{24,8},{1,17},{9,25},{17,1},{25,9},{2,18},{10... | collective-permute-start | bytes 3145736 | tf_op jit(solution)/shard_map/ppermute | solution.py:30
  329.1 28.6 %collective-permute-start.55 = (bf16[4,1024,128]{2,1,0:T(8,128)(2,1)}, bf16[4,1024,128]{2,1,0:T(8,128)(2,1)}, u32[]{:S(2)}, u32[]{:S(2)}) collective-permute-start(bf16[4,1024,128]{2,1,0:T(8,128)(2,1)} %pad_maximum_fusion.3), channel_id=1, source_target_pairs={{0,24},{8,16},{16,8},{24,0},{1,25},{9,17},{17,9},{25,1},{2,26},{10... | collective-permute-start | bytes 3145736 | tf_op jit(solution)/shard_map/ppermute | solution.py:30
  340.1 25.4 %collective-permute-start.56 = (bf16[4,1040,128]{2,1,0:T(8,128)(2,1)S(1)}, bf16[4,1040,128]{2,1,0:T(8,128)(2,1)}, u32[]{:S(2)}, u32[]{:S(2)}) collective-permute-start(bf16[4,1040,128]{2,1,0:T(8,128)(2,1)S(1)} %pad_maximum_fusion), channel_id=1, source_target_pairs={{0,2},{2,0},{4,6},{6,4},{1,3},{3,1},{5,7},{7,5},{8,10},{10,8},{12,... | collective-permute-start | bytes 3194888 | tf_op jit(solution)/shard_map/ppermute | solution.py:30
  341.5 26.5 %collective-permute-start.57 = (bf16[4,1040,128]{2,1,0:T(8,128)(2,1)}, bf16[4,1040,128]{2,1,0:T(8,128)(2,1)}, u32[]{:S(2)}, u32[]{:S(2)}) collective-permute-start(bf16[4,1040,128]{2,1,0:T(8,128)(2,1)} %pad_maximum_fusion.1), channel_id=1, source_target_pairs={{0,6},{2,4},{4,2},{6,0},{1,7},{3,5},{5,3},{7,1},{8,14},{10,12},{12... | collective-permute-start | bytes 3194888 | tf_op jit(solution)/shard_map/ppermute | solution.py:30
  368.0 30.1 %all-to-all-start.4 = ((bf16[16,3,128,128]{3,2,1,0:T(8,128)(2,1)}), bf16[16,3,128,128]{3,2,1,0:T(8,128)(2,1)}, u32[]{:S(2)}, u32[]{:S(2)}) async-start(bf16[16,3,128,128]{3,2,1,0:T(8,128)(2,1)} %attend_back.1), calls=%async_computation.4 | async-start | bytes 3145728 | tf_op jit(solution)/shard_map/all_to_all | solution.py:837
  423.7 62.6 %collective-permute-start.66 = (bf16[128,2048]{1,0:T(8,128)(2,1)}, bf16[128,2048]{1,0:T(8,128)(2,1)}, u32[]{:S(2)}, u32[]{:S(2)}) collective-permute-start(bf16[128,2048]{1,0:T(8,128)(2,1)} %pad_maximum_fusion.13), channel_id=1, source_target_pairs={{0,96},{32,64},{64,32},{96,0},{1,97},{33,65},{65,33},{97,1},{2,98}... | collective-permute-start | bytes 1572872 | tf_op jit(solution)/shard_map/ppermute | solution.py:30
  425.4 14.7 %collective-permute-start.73 = (bf16[2,1024,128]{2,1,0:T(8,128)(2,1)S(1)}, bf16[2,1024,128]{2,1,0:T(8,128)(2,1)S(1)}, u32[]{:S(2)}, u32[]{:S(2)}) collective-permute-start(bf16[2,1024,128]{2,1,0:T(8,128)(2,1)S(1)} %get-tuple-element.161), channel_id=1, source_target_pairs={{0,6},{2,4},{4,2},{6,0},{1,7},{3,5},{5,3},{7,1},{8,14},{10,12},{12... | collective-permute-start | bytes 1572872 | tf_op jit(solution)/shard_map/ppermute | solution.py:30
  430.8 17.0 %collective-permute-start.62 = (bf16[128,2048]{1,0:T(8,128)(2,1)S(1)}, bf16[128,2048]{1,0:T(8,128)(2,1)S(1)}, u32[]{:S(2)}, u32[]{:S(2)}) collective-permute-start(bf16[128,2048]{1,0:T(8,128)(2,1)S(1)} %pad_maximum_fusion.10), channel_id=1, source_target_pairs={{0,32},{32,0},{64,96},{96,64},{1,33},{33,1},{65,97},{97,65},{2,34}... | collective-permute-start | bytes 1572872 | tf_op jit(solution)/shard_map/ppermute | solution.py:30
  431.1 21.3 %collective-permute-start.64 = (bf16[128,2048]{1,0:T(8,128)(2,1)S(1)}, bf16[128,2048]{1,0:T(8,128)(2,1)S(1)}, u32[]{:S(2)}, u32[]{:S(2)}) collective-permute-start(bf16[128,2048]{1,0:T(8,128)(2,1)S(1)} %pad_maximum_fusion.11), channel_id=1, source_target_pairs={{0,96},{32,64},{64,32},{96,0},{1,97},{33,65},{65,33},{97,1},{2,98}... | collective-permute-start | bytes 1572872 | tf_op jit(solution)/shard_map/ppermute | solution.py:30
  443.9 14.0 %collective-permute-start.86 = (bf16[1024,128]{1,0:T(8,128)(2,1)S(1)}, bf16[1024,128]{1,0:T(8,128)(2,1)S(1)}, u32[]{:S(2)}, u32[]{:S(2)}) collective-permute-start(bf16[1024,128]{1,0:T(8,128)(2,1)S(1)} %get-tuple-element.194), channel_id=1, source_target_pairs={{0,6},{2,4},{4,2},{6,0},{1,7},{3,5},{5,3},{7,1},{8,14},{10,12},{12... | collective-permute-start | bytes 786440 | tf_op jit(solution)/shard_map/ppermute | solution.py:30
  452.4 17.6 %collective-permute-start.89 = (bf16[1040,128]{1,0:T(8,128)(2,1)}, bf16[1040,128]{1,0:T(8,128)(2,1)}, u32[]{:S(2)}, u32[]{:S(2)}) collective-permute-start(bf16[1040,128]{1,0:T(8,128)(2,1)} %get-tuple-element.191), channel_id=1, source_target_pairs={{0,24},{8,16},{16,8},{24,0},{1,25},{9,17},{17,9},{25,1},{2,26},{10... | collective-permute-start | bytes 798728 | tf_op jit(solution)/shard_map/ppermute | solution.py:30
  470.0 21.7 %collective-permute-start.74 = (bf16[4,1024,128]{2,1,0:T(8,128)(2,1)}, bf16[4,1024,128]{2,1,0:T(8,128)(2,1)S(1)}, u32[]{:S(2)}, u32[]{:S(2)}) collective-permute-start(bf16[4,1024,128]{2,1,0:T(8,128)(2,1)} %pad_maximum_fusion.4), channel_id=1, source_target_pairs={{0,2},{2,0},{4,6},{6,4},{1,3},{3,1},{5,7},{7,5},{8,10},{10,8},{12,... | collective-permute-start | bytes 3145736 | tf_op jit(solution)/shard_map/ppermute | solution.py:30
  474.0 21.9 %collective-permute-start.76 = (bf16[4,1024,128]{2,1,0:T(8,128)(2,1)}, bf16[4,1024,128]{2,1,0:T(8,128)(2,1)S(1)}, u32[]{:S(2)}, u32[]{:S(2)}) collective-permute-start(bf16[4,1024,128]{2,1,0:T(8,128)(2,1)} %pad_maximum_fusion.5), channel_id=1, source_target_pairs={{0,6},{2,4},{4,2},{6,0},{1,7},{3,5},{5,3},{7,1},{8,14},{10,12},{12... | collective-permute-start | bytes 3145736 | tf_op jit(solution)/shard_map/ppermute | solution.py:30
  (117 other events, 1311.6 us)
